TPU v7x, 256 devices: a whole 4x4x8 slice. The times are simulated.
256 devices in a mesh: dp: 8 (over x, z_lo), tensor: 32 (over y, z_hi, core).
Axes of the slice: x: 4, y: 4, z: 8 (z_hi: 4, z_lo: 2; z = z_hi * 2 + z_lo), core: 2. Of those that a mesh axis runs over, the one named last changes fastest.
Arguments:
- hidden_in: bfloat16 [1024, 12288], P('dp', 'tensor'), may hold values from -300 to 300, as said below
- ln_gain: float32 [12288], P('tensor'), may hold values from 0.5 to 1.5
- ln_bias: float32 [12288], P('tensor'), may hold values from -3 to 3
- q_weight: bfloat16 [12288, 12288], P('dp', 'tensor'), may hold values from -2 to 2
- grad_query: bfloat16 [1024, 12288], P('dp', 'tensor'), may hold values from -6 to 6
Outputs:
- grad_input: float32 [1024, 12288], P('dp', 'tensor')
- grad_weight: float32 [12288, 12288], P('dp', 'tensor')
- grad_gain: float32 [12288], P('tensor')
- grad_bias: float32 [12288], P('tensor')
Inputs may be any that keep to these rules, and one draw needn't show every extreme that they name: `hidden_in`: finite values.
All inputs are finite; a program needn't handle non-finite values.
Results may differ from a plain program's by a relative error of at most 0.0029.
Values may be sent and summed in bfloat16 or wider, within the bound.
No kernel may reach another device: no remote copies, remote signals or barrier semaphores. Data moves between devices by JAX's collectives and lax.ppermute only.
A program may use at most 128 MiB of HBM per device.

v0:
```python
import jax
import jax.numpy as jnp
from jax import lax
from jax.sharding import PartitionSpec as P


def body(hidden_in, ln_gain, ln_bias, q_weight, grad_query):
    values = hidden_in.astype(jnp.float32)
    width = values.shape[1] * lax.axis_size("tensor")
    row_sum, row_square = lax.psum(
        (jnp.sum(values, axis=1), jnp.sum(values * values, axis=1)), "tensor"
    )
    row_mean = row_sum / width
    row_var = row_square / width - row_mean * row_mean
    inv_std = lax.rsqrt(row_var + 1e-05)
    standard = (values - row_mean[:, None]) * inv_std[:, None]
    normed_local = (standard * ln_gain + ln_bias).astype(jnp.bfloat16)
    normed = lax.all_gather(normed_local, "tensor", axis=1, tiled=True)
    grad_weight = lax.psum_scatter(
        lax.dot_general(
            normed, grad_query, (((0,), (0,)), ((), ())), preferred_element_type=jnp.float32
        ),
        "dp",
        scatter_dimension=0,
        tiled=True,
    )
    partial_input = lax.dot_general(
        grad_query,
        lax.all_gather(q_weight, "dp", axis=0, tiled=True),
        (((1,), (1,)), ((), ())),
        preferred_element_type=jnp.float32,
    )
    grad_normed = lax.psum_scatter(partial_input, "tensor", scatter_dimension=1, tiled=True)
    grad_gain, grad_bias = lax.psum(
        (jnp.sum(grad_normed * standard, axis=0), jnp.sum(grad_normed, axis=0)), "dp"
    )
    scaled = grad_normed * ln_gain
    first, second = lax.psum(
        (jnp.sum(scaled, axis=1), jnp.sum(scaled * standard, axis=1)), "tensor"
    )
    first = first / width
    second = second / width
    grad_input = inv_std[:, None] * (scaled - first[:, None] - standard * second[:, None])
    return (grad_input, grad_weight, grad_gain, grad_bias)


def solution(mesh):
    placed = (P("dp", "tensor"), P("tensor"), P("tensor"), P("dp", "tensor"), P("dp", "tensor"))
    return jax.shard_map(
        body,
        mesh=mesh,
        in_specs=placed,
        out_specs=(P("dp", "tensor"), P("dp", "tensor"), P("tensor"), P("tensor")),
        check_vma=False,
    )
```

profile of v0, /device:TPU:1, one launch (start us, length us, event | category | flops | bytes accessed | tf_op | source)
XLA Modules:
  0.0 771.3 jit_solution(4628467628634352626)
XLA Ops:
  7.2 0.0 copy-start
  7.2 0.0 all-gather.3.cloned.1.call-start
  7.2 0.7 all-gather.3.cloned.1.call-update
  7.9 0.0 reduce-scatter.3.cloned.1.call-start
  8.0 196.3 %all-gather.3.cloned.1.call-done = bf16[12288,384]{1,0:T(8,128)(2,1)} async-done(((bf16[1536,384]{1,0:T(8,128)(2,1)}), bf16[12288,384]{1,0:T(8,128)(2,1)}) %all-gather.3.cloned.1.call-update) | async-done | bytes 9437200 | tf_op jit(solution)/shard_map/all_gather | solution.py:29
  204.3 0.0 copy-done
  204.3 9.4 %fusion.12 = f32[128,12288]{1,0:T(8,128)} fusion(bf16[128,384]{1,0:T(8,128)(2,1)S(1)} %copy-done, bf16[12288,384]{1,0:T(8,128)(2,1)} %all-gather.3.cloned.1.call-done), kind=kOutput, calls=%fused_computation.20 | convolution fusion | flops 1207959552 | bytes 15826944 | tf_op jit(solution)/shard_map/dot_general | solution.py:27
  213.7 0.0 reduce-scatter.3.cloned.1.call-update
  213.7 0.0 all-gather.5.cloned.1.call-start
  213.7 0.8 copy-done.1
  214.6 0.1 fusion
  214.7 72.3 %all-reduce.1 = (f32[128]{0:T(128)S(1)}, f32[128]{0:T(128)S(1)}) all-reduce(f32[128]{0:T(128)S(1)} %get-tuple-element.9, f32[128]{0:T(128)S(1)} %get-tuple-element.8), channel_id=1, replica_groups=mesh['dp'=8,'tensor'=32] {'tensor'}, use_global_device_ids=true, to_apply=%region_3.0 | all-reduce | flops 256 | bytes 2048 | tf_op jit(solution)/shard_map/psum | solution.py:10
  287.0 36.6 %reduce-scatter.3.cloned.1.call-done = f32[128,384]{1,0:T(8,128)} async-done(((f32[128,12288]{1,0:T(8,128)}), f32[128,384]{1,0:T(8,128)}) %reduce-scatter.3.cloned.1.call-update) | async-done | bytes 196624 | tf_op jit(solution)/shard_map/reduce_scatter | solution.py:33
  323.6 0.0 copy-done.3
  323.6 1.7 fusion.11
  325.3 0.0 all-gather.5.cloned.1.call-update
  325.4 0.0 reduce-scatter.5.cloned.1.call-start
  325.4 60.3 %all-gather.5.cloned.1.call-done = bf16[128,12288]{1,0:T(8,128)(2,1)} async-done(((bf16[128,384]{1,0:T(8,128)(2,1)}), bf16[128,12288]{1,0:T(8,128)(2,1)}) %all-gather.5.cloned.1.call-update) | async-done | bytes 3145744 | tf_op jit(solution)/shard_map/all_gather | solution.py:18
  385.7 11.0 %fusion.13 = f32[12288,384]{1,0:T(8,128)} fusion(bf16[128,12288]{1,0:T(8,128)(2,1)} %all-gather.5.cloned.1.call-done, bf16[128,384]{1,0:T(8,128)(2,1)S(1)} %copy-done), kind=kOutput, calls=%fused_computation.21 | convolution fusion | flops 1207959552 | bytes 22118400 | tf_op jit(solution)/shard_map/dot_general | solution.py:20
  396.7 0.0 reduce-scatter.5.cloned.1.call-update
  396.7 71.3 %all-reduce = (f32[128]{0:T(128)S(1)}, f32[128]{0:T(128)S(1)}) all-reduce(f32[128]{0:T(128)S(1)} %get-tuple-element.5, f32[128]{0:T(128)S(1)} %get-tuple-element.6), channel_id=1, replica_groups=mesh['dp'=8,'tensor'=32] {'tensor'}, use_global_device_ids=true, to_apply=%region_8.0 | all-reduce | flops 256 | bytes 2048 | tf_op jit(solution)/shard_map/psum | solution.py:38
  468.0 16.1 %all-reduce.2 = (f32[384]{0:T(512)}, f32[384]{0:T(512)}) all-reduce(f32[384]{0:T(512)S(1)} %get-tuple-element.4, f32[384]{0:T(512)S(1)} %get-tuple-element.7), channel_id=1, replica_groups=mesh['dp'=8,'tensor'=32] {'dp'}, use_global_device_ids=true, to_apply=%region_11.0 | all-reduce | flops 768 | bytes 6144 | tf_op jit(solution)/shard_map/psum | solution.py:34
  484.1 0.8 fusion.8
  484.9 279.8 %reduce-scatter.5.cloned.1.call-done = f32[1536,384]{1,0:T(8,128)} async-done(((f32[12288,384]{1,0:T(8,128)}), f32[1536,384]{1,0:T(8,128)}) %reduce-scatter.5.cloned.1.call-update) | async-done | bytes 2359312 | tf_op jit(solution)/shard_map/reduce_scatter | solution.py:19
  (8 shorter events, 0.0 us)
Async XLA Ops:
  7.2 197.1 %copy-start = (bf16[128,384]{1,0:T(8,128)(2,1)S(1)}, bf16[128,384]{1,0:T(8,128)(2,1)}, u32[]{:S(2)}) copy-start(bf16[128,384]{1,0:T(8,128)(2,1)} %param.9) | copy-start | bytes 294916
  7.2 197.1 %all-gather.3.cloned.1.call-start = ((), (), s32[]{:S(2)}) async-start(), calls=%async_computation.2 | async-start | bytes 10616832 | tf_op jit(solution)/shard_map/all_gather | solution.py:29
  7.9 315.7 %reduce-scatter.3.cloned.1.call-start = ((), (), s32[]{:S(2)}) async-start(), calls=%async_computation.3 | async-start | bytes 6488064 | tf_op jit(solution)/shard_map/reduce_scatter | solution.py:33
  213.7 0.9 copy-start.1
  213.7 110.0 %copy-start.3 = (f32[384]{0:T(512)S(1)}, f32[384]{0:T(512)}, u32[]{:S(2)}) copy-start(f32[384]{0:T(512)} %param.6) | copy-start | bytes 4612
  213.7 110.0 %copy-start.4 = (f32[384]{0:T(512)S(1)}, f32[384]{0:T(512)}, u32[]{:S(2)}) copy-start(f32[384]{0:T(512)} %param.7) | copy-start | bytes 4612
  213.7 172.0 %all-gather.5.cloned.1.call-start = ((), (), s32[]{:S(2)}) async-start(), calls=%async_computation.4 | async-start | bytes 3244032 | tf_op jit(solution)/shard_map/all_gather | solution.py:18
  325.4 439.4 %reduce-scatter.5.cloned.1.call-start = ((), (), s32[]{:S(2)}) async-start(), calls=%async_computation.5 | async-start | bytes 21233664 | tf_op jit(solution)/shard_map/reduce_scatter | solution.py:19
  396.7 87.4 %copy-start.2 = (f32[128,384]{1,0:T(8,128)S(1)}, f32[128,384]{1,0:T(8,128)}, u32[]{:S(2)}) copy-start(f32[128,384]{1,0:T(8,128)} %reduce-scatter.3.cloned.1.call-done) | copy-start | bytes 589828
Sparse Core Ops, SparseCore 0:
  9.8 194.4 all-gather.2
  213.8 109.7 reduce-scatter.2
  327.0 58.6 all-gather.4
  396.8 367.8 reduce-scatter.4
where the time goes:
time: 772 us; the launch traced here: 771 us
  waiting for transfers between devices  574 us (74%)
  blocking collectives  160 us (21%)
  matrix products  20.4 us (3%)
  between operations  13.8 us (2%)
    reduce_scatter x1, waiting for transfers between devices, body(): lax.psum_scatter(lax.dot_general(normed, grad_query, (((0,), (0,)), ((),...  280 us
    all_gather x1, waiting for transfers between devices, body(): lax.all_gather(q_weight, 'dp', axis=0, tiled=True)  196 us
    psum x1, blocking collectives, body(): lax.psum((jnp.sum(values, axis=1), jnp.sum(values * values, axis=1)), 'te...  72.3 us
    psum x1, blocking collectives, body(): lax.psum((jnp.sum(scaled, axis=1), jnp.sum(scaled * standard, axis=1)), '...  71.3 us
    all_gather x1, waiting for transfers between devices, body(): normed = lax.all_gather(normed_local, 'tensor', axis=1, tiled=True)  60.3 us
    reduce_scatter x1, waiting for transfers between devices, body(): lax.psum_scatter(partial_input, 'tensor', scatter_dimension=1, tiled=True)  36.6 us
    psum x1, blocking collectives, body(): lax.psum((jnp.sum(grad_normed * standard, axis=0), jnp.sum(grad_normed, a...  16.1 us
  transfers between devices with their start and end apart: 4, of which 4 were waited for; matrix products, arithmetic and copies ran while one was open for 0% of the time, Pallas kernels for 0%

commit v1 on v0

v1 whole, which is shorter than its diff:
```python
import jax
import jax.numpy as jnp
from jax import lax
from jax.sharding import PartitionSpec as P

AXES = ("dp", "tensor")
DATA, TENSOR = 8, 32
CAP = 32768.0


def flat(x, zl, y, zh, c):
    return ((x * 2 + zl) * 4 + y) * 8 + zh * 2 + c


def table(move):
    pairs = []
    for d in range(DATA):
        for t in range(TENSOR):
            place = (d // 2, d % 2, t // 8, (t // 2) % 4, t % 2)
            pairs.append((flat(*place), flat(*move(*place))))
    return pairs


def to_owner(k):
    def move(x, zl, y, zh, c):
        s = (zh + k) % 4
        return (y, s % 2, x, 2 * zl + s // 2, c)

    return table(move)


CORE = table(lambda x, zl, y, zh, c: (x, zl, y, zh, 1 - c))
ALONG_Y = [table(lambda x, zl, y, zh, c, k=k: (x, zl, (y + k) % 4, zh, c)) for k in range(4)]
OWNER = [to_owner(k) for k in range(4)]
HOLDER = [[(b, a) for a, b in pairs] for pairs in OWNER]


def send(array, pairs):
    return lax.ppermute(array, AXES, pairs)


def after(array, *others):
    return lax.optimization_barrier((array,) + others)[0]


def total(array, axis, size):
    copies = jnp.broadcast_to(array[None], (size,) + array.shape)
    copies = lax.all_to_all(copies, axis, split_axis=0, concat_axis=0, tiled=True)
    return jnp.sum(copies, axis=0)


def pack(values, power):
    body = (values * jnp.exp2(power)).astype(jnp.float16)
    tail = jnp.full((16, values.shape[1]), power, jnp.float32).astype(jnp.float16)
    return jnp.concatenate([body, tail], axis=0)


def unpack(message):
    power = message[-16, 0].astype(jnp.float32)
    return message[:-16].astype(jnp.float32) * jnp.exp2(-power), power


def power_for(bound):
    return jnp.clip(jnp.floor(jnp.log2(CAP / bound)), -100.0, 100.0)


def body(hidden_in, ln_gain, ln_bias, q_weight, grad_query):
    tokens, width = hidden_in.shape
    d, t = lax.axis_index("dp"), lax.axis_index("tensor")
    y, zh, c = t // 8, (t // 2) % 4, t % 2
    features = width * TENSOR

    quarters = q_weight.reshape(2, 2, width, width)
    mine = lax.dynamic_index_in_dim(quarters, c, axis=1, keepdims=False).reshape(2 * width, width)
    theirs = lax.dynamic_index_in_dim(quarters, 1 - c, axis=1, keepdims=False).reshape(2 * width, width)
    theirs = send(theirs, CORE)

    query = jnp.broadcast_to(grad_query[None], (DATA,) + grad_query.shape)
    query = lax.all_to_all(query, "dp", split_axis=0, concat_axis=0, tiled=True).reshape(4, 2 * tokens, width)
    query_other = send(query, CORE)

    highest = lambda a: jnp.max(jnp.abs(a)).astype(jnp.float32)
    bound = width * (highest(query) * highest(mine) + highest(query_other) * highest(theirs))
    power = power_for(bound)

    at = [(y + k) % 4 for k in range(4)]
    own_tokens = [lax.dynamic_index_in_dim(query, at[k], axis=0, keepdims=False) for k in range(4)]
    other_tokens = [lax.dynamic_index_in_dim(query_other, at[k], axis=0, keepdims=False) for k in range(4)]
    rows_by_rows = (((1,), (1,)), ((), ()))

    def part(k):
        return lax.dot_general(
            own_tokens[k], mine, rows_by_rows, preferred_element_type=jnp.float32
        ) + lax.dot_general(other_tokens[k], theirs, rows_by_rows, preferred_element_type=jnp.float32)

    sent = [pack(part(k), power) for k in (2, 1, 3)]
    parts = [unpack(send(m, ALONG_Y[k])) for m, k in zip(sent, (2, 1, 3))]

    values = hidden_in.astype(jnp.float32)
    sums = jnp.stack([jnp.sum(values, axis=1), jnp.sum(values * values, axis=1)])
    row_sum, row_square = total(after(sums, *sent), "tensor", TENSOR)
    row_mean = row_sum / features
    row_var = row_square / features - row_mean * row_mean
    inv_std = lax.rsqrt(row_var + 1e-05)
    standard = (values - row_mean[:, None]) * inv_std[:, None]
    normed = (standard * ln_gain + ln_bias).astype(jnp.bfloat16)

    summed = part(0) + parts[0][0] + parts[1][0] + parts[2][0]
    bound = bound + CAP * (jnp.exp2(-parts[0][1]) + jnp.exp2(-parts[1][1]) + jnp.exp2(-parts[2][1]))
    power = power_for(bound)
    summed = summed.reshape(2, tokens, 2, width)

    grad_normed = None
    for k in range(4):
        s = (zh + k) % 4
        tile = lax.dynamic_slice(summed, (s % 2, 0, s // 2, 0), (1, tokens, 1, width)).reshape(tokens, width)
        piece = unpack(send(pack(tile, power), OWNER[k]))[0]
        grad_normed = piece if grad_normed is None else grad_normed + piece

    tiles = [send(normed, HOLDER[k]) for k in range(4)]
    tiles = lax.dynamic_slice_in_dim(jnp.stack(tiles + tiles[:3]), (4 - zh) % 4, 4, axis=0)
    block = tiles.reshape(2, 2, tokens, width).transpose(1, 2, 0, 3).reshape(2 * tokens, 2 * width)
    blocks = [block] + [send(block, ALONG_Y[k]) for k in (1, 2, 3)]

    def weight_part(columns):
        out = 0.0
        for k in range(4):
            out = out + lax.dot_general(
                blocks[k], columns[(4 - k) % 4], (((0,), (0,)), ((), ())), preferred_element_type=jnp.float32
            )
        return out

    received = send(weight_part(other_tokens), CORE).reshape(2, width, width)
    kept = weight_part(own_tokens).reshape(2, width, width)
    grad_weight = jnp.where(
        c == 0, jnp.stack([kept, received], axis=1), jnp.stack([received, kept], axis=1)
    ).reshape(4 * width, width)

    scaled = grad_normed * ln_gain
    first, second = total(
        jnp.stack([jnp.sum(scaled, axis=1), jnp.sum(scaled * standard, axis=1)]), "tensor", TENSOR
    )
    first, second = first / features, second / features
    grad_input = inv_std[:, None] * (scaled - first[:, None] - standard * second[:, None])
    grad_gain, grad_bias = total(
        jnp.stack([jnp.sum(grad_normed * standard, axis=0), jnp.sum(grad_normed, axis=0)]), "dp", DATA
    )
    return (grad_input, grad_weight, grad_gain, grad_bias)


def solution(mesh):
    placed = (P("dp", "tensor"), P("tensor"), P("tensor"), P("dp", "tensor"), P("dp", "tensor"))
    return jax.shard_map(
        body,
        mesh=mesh,
        in_specs=placed,
        out_specs=(P("dp", "tensor"), P("dp", "tensor"), P("tensor"), P("tensor")),
        check_vma=False,
    )
```

time: 772 us -> 182 us (0.24)
  waiting for transfers between devices: 574 us -> 47.9 us
  blocking collectives: 160 us -> 0 us
  starting transfers between devices: 0.16 us -> 89.8 us
  local copies, waits for them, and re-layouts: 0.83 us -> 17.1 us
  matrix products: 20.4 us -> 11.4 us
    reduce_scatter x2 -> x0, waiting for transfers between devices: 316 us -> none  [the longest x1 280 us: body(): lax.psum_scatter(lax.dot_general(normed, grad_query, (((0,), (0,)), ((),...]
    all_gather x2 -> x0, waiting for transfers between devices: 257 us -> none  [the longest x1 196 us: body(): lax.all_gather(q_weight, 'dp', axis=0, tiled=True)]
    psum x3 -> x0, blocking collectives: 160 us -> none  [the longest x1 72.3 us: body(): lax.psum((jnp.sum(values, axis=1), jnp.sum(values * values, axis=1)), 'te...]
    all_to_all x0 -> x4, starting transfers between devices: none -> 52.3 us  [the longest x3 46.1 us: total(): lax.all_to_all(copies, axis, split_axis=0, concat_axis=0, tiled=True)]
    ppermute x0 -> x17, starting transfers between devices: none -> 37.5 us  [send(): return lax.ppermute(array, AXES, pairs)]
    all_to_all x0 -> x4, waiting for transfers between devices: none -> 27.7 us  [the longest x3 21 us: total(): lax.all_to_all(copies, axis, split_axis=0, concat_axis=0, tiled=True)]
    ppermute x0 -> x17, waiting for transfers between devices: none -> 20.3 us  [send(): return lax.ppermute(array, AXES, pairs)]
    dot_general x2 -> x16, matrix products: 20.4 us -> 11.4 us  [the longest x4 4.94 us: part(): lax.dot_general(other_tokens[k], theirs, rows_by_rows, preferred_element_...]
  transfers between devices with their start and end apart: 4 -> 21, of which waited for: 4 -> 9; matrix products, arithmetic and copies ran while one was open for 0% -> 11% of each run, Pallas kernels for 0% -> 0%
where the time goes in v1:
time: 182 us; the launch traced here: 181 us
  starting transfers between devices  89.8 us (49%)
  waiting for transfers between devices  47.9 us (26%)
  local copies, waits for them, and re-layouts  17.1 us (9%)
  matrix products  11.4 us (6%)
  between operations  8.91 us (5%)
  other arithmetic  6.02 us (3%)
    all_to_all x3, starting transfers between devices, total(): lax.all_to_all(copies, axis, split_axis=0, concat_axis=0, tiled=True)  46.1 us
    ppermute x17, starting transfers between devices, send(): return lax.ppermute(array, AXES, pairs)  37.5 us
    all_to_all x3, waiting for transfers between devices, total(): lax.all_to_all(copies, axis, split_axis=0, concat_axis=0, tiled=True)  21 us
    ppermute x17, waiting for transfers between devices, send(): return lax.ppermute(array, AXES, pairs)  20.3 us
    all_to_all x1, waiting for transfers between devices, body(): lax.all_to_all(query, 'dp', split_axis=0, concat_axis=0, tiled=True)  6.63 us
    all_to_all x1, starting transfers between devices, body(): lax.all_to_all(query, 'dp', split_axis=0, concat_axis=0, tiled=True)  6.2 us
    slice x7, local copies, waits for them, and re-layouts, unpack(): power = message[-16, 0].astype(jnp.float32)  5.64 us
    dot_general x4, matrix products, part(): lax.dot_general(other_tokens[k], theirs, rows_by_rows, preferred_element_...  4.94 us
  transfers between devices with their start and end apart: 21, of which 9 were waited for; matrix products, arithmetic and copies ran while one was open for 11% of the time, Pallas kernels for 0%

profile of v1, /device:TPU:1, one launch (start us, length us, event | category | flops | bytes accessed | tf_op | source)
XLA Modules:
  0.0 181.1 jit_solution(17945298348927334050)
XLA Ops:
  0.6 1.9 %broadcast_in_dim.8 = bf16[8,128,384]{2,1,0:T(8,128)(2,1)} broadcast(bf16[128,384]{1,0:T(8,128)(2,1)} %param.9), dimensions={1,2} | broadcast | bytes 884736 | tf_op jit(solution)/shard_map/broadcast_in_dim | solution.py:78
  2.6 6.2 %all-to-all-start = ((bf16[8,128,384]{2,1,0:T(8,128)(2,1)}), bf16[8,128,384]{2,1,0:T(8,128)(2,1)S(1)}, u32[]{:S(2)}, u32[]{:S(2)}) async-start(bf16[8,128,384]{2,1,0:T(8,128)(2,1)} %broadcast_in_dim.8), calls=%async_computation | async-start | bytes 1572864 | tf_op jit(solution)/shard_map/all_to_all | solution.py:79
  11.4 1.7 collective-permute-done.1
  13.8 6.6 %all-to-all-done = bf16[8,128,384]{2,1,0:T(8,128)(2,1)S(1)} async-done(((bf16[8,128,384]{2,1,0:T(8,128)(2,1)}), bf16[8,128,384]{2,1,0:T(8,128)(2,1)S(1)}, u32[]{:S(2)}, u32[]{:S(2)}) %all-to-all-start) | async-done | bytes 786464 | tf_op jit(solution)/shard_map/all_to_all | solution.py:79
  20.5 2.2 %collective-permute-start = (bf16[4,256,384]{2,1,0:T(8,128)(2,1)S(1)}, bf16[4,256,384]{2,1,0:T(8,128)(2,1)S(1)}, u32[]{:S(2)}, u32[]{:S(2)}) collective-permute-start(bf16[4,256,384]{2,1,0:T(8,128)(2,1)S(1)} %bitcast.117), channel_id=1, source_target_pairs={{0,1},{1,0},{2,3},{3,2},{4,5},{5,4},{6,7},{7,6},{8,9},{9,8},{10,11... | collective-permute-start | bytes 2359304 | tf_op jit(solution)/shard_map/ppermute | solution.py:39
  29.7 1.6 fusion.10
  34.7 2.6 %collective-permute-start.2 = (f16[272,768]{1,0:T(8,128)(2,1)}, f16[272,768]{1,0:T(8,128)(2,1)}, u32[]{:S(2)}, u32[]{:S(2)}) collective-permute-start(f16[272,768]{1,0:T(8,128)(2,1)} %concatenate.21), channel_id=1, source_target_pairs={{0,16},{1,17},{2,18},{3,19},{4,20},{5,21},{6,22},{7,23},{8,24},{9,... | collective-permute-start | bytes 1253384 | tf_op jit(solution)/shard_map/ppermute | solution.py:39
  40.2 8.7 %all-to-all-start.1 = ((f32[32,2,128]{2,1,0:T(2,128)}), f32[32,2,128]{2,1,0:T(2,128)}, u32[]{:S(2)}, u32[]{:S(2)}) async-start(f32[32,2,128]{2,1,0:T(2,128)} %broadcast_in_dim.9), calls=%async_computation.1 | async-start | bytes 65536 | tf_op jit(solution)/shard_map/all_to_all | solution.py:48
  49.4 9.3 %all-to-all-done.1 = f32[32,2,128]{2,1,0:T(2,128)} async-done(((f32[32,2,128]{2,1,0:T(2,128)}), f32[32,2,128]{2,1,0:T(2,128)}, u32[]{:S(2)}, u32[]{:S(2)}) %all-to-all-start.1) | async-done | bytes 32800 | tf_op jit(solution)/shard_map/all_to_all | solution.py:48
  65.4 2.6 %fusion.8 = f32[256,768]{1,0:T(8,128)} fusion(f32[256,768]{1,0:T(8,128)S(1)} %fusion.32, bf16[768,384]{1,0:T(8,128)(2,1)S(1)} %collective-permute-done.1, f16[272,768]{1,0:T(8,128)(2,1)} %collective-permute-done.4, f16[272,768]{1,0:T(8,128)(2,1)} %collective-permute-done.3, f16[272,768]{1,0:T(8,128)(2,1)} %collective-permute-done.2, f32[]{:T(128)} %bitcast.18, ...), kind=kOutput, calls=%fused_computation.16 | convolution fusion | flops 152961024 | bytes 3538960 | tf_op jit(solution)/shard_map/dot_general | solution.py:94
  71.0 7.3 %collective-permute-start.6 = (f16[144,384]{1,0:T(8,128)(2,1)S(1)}, f16[144,384]{1,0:T(8,128)(2,1)S(1)}, u32[]{:S(2)}, u32[]{:S(2)}) collective-permute-start(f16[144,384]{1,0:T(8,128)(2,1)S(1)} %concatenate.25), channel_id=1, source_target_pairs={{0,32},{1,33},{2,2},{3,3},{4,34},{5,35},{6,0},{7,1},{8,96},{9,97},... | collective-permute-start | bytes 331784 | tf_op jit(solution)/shard_map/ppermute | solution.py:39
  78.5 5.1 %collective-permute-start.8 = (f16[144,384]{1,0:T(8,128)(2,1)S(1)}, f16[144,384]{1,0:T(8,128)(2,1)S(1)}, u32[]{:S(2)}, u32[]{:S(2)}) collective-permute-start(f16[144,384]{1,0:T(8,128)(2,1)S(1)} %concatenate.27), channel_id=1, source_target_pairs={{0,34},{1,35},{2,0},{3,1},{4,32},{5,33},{6,2},{7,3},{8,98},{9,99},... | collective-permute-start | bytes 331784 | tf_op jit(solution)/shard_map/ppermute | solution.py:39
  86.1 3.2 %collective-permute-done.7 = f16[144,384]{1,0:T(8,128)(2,1)S(1)} collective-permute-done((f16[144,384]{1,0:T(8,128)(2,1)S(1)}, f16[144,384]{1,0:T(8,128)(2,1)S(1)}, u32[]{:S(2)}, u32[]{:S(2)}) %collective-permute-start.7) | collective-permute-done | bytes 110624 | tf_op jit(solution)/shard_map/ppermute | solution.py:39
  92.7 5.3 %collective-permute-start.10 = (bf16[128,384]{1,0:T(8,128)(2,1)S(1)}, bf16[128,384]{1,0:T(8,128)(2,1)S(1)}, u32[]{:S(2)}, u32[]{:S(2)}) collective-permute-start(bf16[128,384]{1,0:T(8,128)(2,1)S(1)} %get-tuple-element.22), channel_id=1, source_target_pairs={{32,0},{33,1},{2,2},{3,3},{34,4},{35,5},{0,6},{1,7},{96,8},{97,9},... | collective-permute-start | bytes 294920 | tf_op jit(solution)/shard_map/ppermute | solution.py:39
  98.0 2.6 %collective-permute-start.11 = (bf16[128,384]{1,0:T(8,128)(2,1)S(1)}, bf16[128,384]{1,0:T(8,128)(2,1)S(1)}, u32[]{:S(2)}, u32[]{:S(2)}) collective-permute-start(bf16[128,384]{1,0:T(8,128)(2,1)S(1)} %get-tuple-element.22), channel_id=1, source_target_pairs={{2,0},{3,1},{34,2},{35,3},{0,4},{1,5},{32,6},{33,7},{66,8},{67,9},... | collective-permute-start | bytes 294920 | tf_op jit(solution)/shard_map/ppermute | solution.py:39
  100.6 1.9 %collective-permute-start.12 = (bf16[128,384]{1,0:T(8,128)(2,1)S(1)}, bf16[128,384]{1,0:T(8,128)(2,1)S(1)}, u32[]{:S(2)}, u32[]{:S(2)}) collective-permute-start(bf16[128,384]{1,0:T(8,128)(2,1)S(1)} %get-tuple-element.22), channel_id=1, source_target_pairs={{34,0},{35,1},{0,2},{1,3},{32,4},{33,5},{2,6},{3,7},{98,8},{99,9},... | collective-permute-start | bytes 294920 | tf_op jit(solution)/shard_map/ppermute | solution.py:39
  103.2 25.9 %all-to-all-start.3 = ((f32[8,2,384]{2,1,0:T(2,128)}), f32[8,2,384]{2,1,0:T(2,128)S(1)}, u32[]{:S(2)}, u32[]{:S(2)}) async-start(f32[8,2,384]{2,1,0:T(2,128)} %broadcast_in_dim.11), calls=%async_computation.3 | async-start | bytes 49152 | tf_op jit(solution)/shard_map/all_to_all | solution.py:48
  129.8 1.6 collective-permute-start.13
  131.5 2.7 %all-to-all-done.3 = f32[8,2,384]{2,1,0:T(2,128)S(1)} async-done(((f32[8,2,384]{2,1,0:T(2,128)}), f32[8,2,384]{2,1,0:T(2,128)S(1)}, u32[]{:S(2)}, u32[]{:S(2)}) %all-to-all-start.3) | async-done | bytes 24608 | tf_op jit(solution)/shard_map/all_to_all | solution.py:48
  134.8 11.4 %all-to-all-start.2 = ((f32[32,2,128]{2,1,0:T(2,128)}), f32[32,2,128]{2,1,0:T(2,128)S(1)}, u32[]{:S(2)}, u32[]{:S(2)}) async-start(f32[32,2,128]{2,1,0:T(2,128)} %broadcast_in_dim.10), calls=%async_computation.2 | async-start | bytes 65536 | tf_op jit(solution)/shard_map/all_to_all | solution.py:48
  146.9 9.0 %all-to-all-done.2 = f32[32,2,128]{2,1,0:T(2,128)S(1)} async-done(((f32[32,2,128]{2,1,0:T(2,128)}), f32[32,2,128]{2,1,0:T(2,128)S(1)}, u32[]{:S(2)}, u32[]{:S(2)}) %all-to-all-start.2) | async-done | bytes 32800 | tf_op jit(solution)/shard_map/all_to_all | solution.py:48
  157.0 1.8 collective-permute-start.15
  159.2 8.7 %collective-permute-done.14 = bf16[256,768]{1,0:T(8,128)(2,1)S(1)} collective-permute-done((bf16[256,768]{1,0:T(8,128)(2,1)S(1)}, bf16[256,768]{1,0:T(8,128)(2,1)S(1)}, u32[]{:S(2)}, u32[]{:S(2)}) %collective-permute-start.14) | collective-permute-done | bytes 393248 | tf_op jit(solution)/shard_map/ppermute | solution.py:39
  168.2 6.6 %collective-permute-done.15 = bf16[256,768]{1,0:T(8,128)(2,1)S(1)} collective-permute-done((bf16[256,768]{1,0:T(8,128)(2,1)S(1)}, bf16[256,768]{1,0:T(8,128)(2,1)S(1)}, u32[]{:S(2)}, u32[]{:S(2)}) %collective-permute-start.15) | collective-permute-done | bytes 393248 | tf_op jit(solution)/shard_map/ppermute | solution.py:39
  (101 shorter events, 35.6 us)
Async XLA Ops:
  2.6 17.9 %all-to-all-start = ((bf16[8,128,384]{2,1,0:T(8,128)(2,1)}), bf16[8,128,384]{2,1,0:T(8,128)(2,1)S(1)}, u32[]{:S(2)}, u32[]{:S(2)}) async-start(bf16[8,128,384]{2,1,0:T(8,128)(2,1)} %broadcast_in_dim.8), calls=%async_computation | async-start | bytes 1572864 | tf_op jit(solution)/shard_map/all_to_all | solution.py:79
  10.4 2.8 %collective-permute-start.1 = (bf16[768,384]{1,0:T(8,128)(2,1)}, bf16[768,384]{1,0:T(8,128)(2,1)S(1)}, u32[]{:S(2)}, u32[]{:S(2)}) collective-permute-start(bf16[768,384]{1,0:T(8,128)(2,1)} %bitcast.7), channel_id=1, source_target_pairs={{0,1},{1,0},{2,3},{3,2},{4,5},{5,4},{6,7},{7,6},{8,9},{9,8},{10,11... | collective-permute-start | bytes 1769480 | tf_op jit(solution)/shard_map/ppermute | solution.py:39
  20.5 7.1 %collective-permute-start = (bf16[4,256,384]{2,1,0:T(8,128)(2,1)S(1)}, bf16[4,256,384]{2,1,0:T(8,128)(2,1)S(1)}, u32[]{:S(2)}, u32[]{:S(2)}) collective-permute-start(bf16[4,256,384]{2,1,0:T(8,128)(2,1)S(1)} %bitcast.117), channel_id=1, source_target_pairs={{0,1},{1,0},{2,3},{3,2},{4,5},{5,4},{6,7},{7,6},{8,9},{9,8},{10,11... | collective-permute-start | bytes 2359304 | tf_op jit(solution)/shard_map/ppermute | solution.py:39
  32.2 27.3 %collective-permute-start.3 = (f16[272,768]{1,0:T(8,128)(2,1)}, f16[272,768]{1,0:T(8,128)(2,1)}, u32[]{:S(2)}, u32[]{:S(2)}) collective-permute-start(f16[272,768]{1,0:T(8,128)(2,1)} %concatenate.22), channel_id=1, source_target_pairs={{0,8},{1,9},{2,10},{3,11},{4,12},{5,13},{6,14},{7,15},{8,16},{9,17... | collective-permute-start | bytes 1253384 | tf_op jit(solution)/shard_map/ppermute | solution.py:39
  34.7 26.7 %collective-permute-start.2 = (f16[272,768]{1,0:T(8,128)(2,1)}, f16[272,768]{1,0:T(8,128)(2,1)}, u32[]{:S(2)}, u32[]{:S(2)}) collective-permute-start(f16[272,768]{1,0:T(8,128)(2,1)} %concatenate.21), channel_id=1, source_target_pairs={{0,16},{1,17},{2,18},{3,19},{4,20},{5,21},{6,22},{7,23},{8,24},{9,... | collective-permute-start | bytes 1253384 | tf_op jit(solution)/shard_map/ppermute | solution.py:39
  38.6 24.8 %collective-permute-start.4 = (f16[272,768]{1,0:T(8,128)(2,1)}, f16[272,768]{1,0:T(8,128)(2,1)}, u32[]{:S(2)}, u32[]{:S(2)}) collective-permute-start(f16[272,768]{1,0:T(8,128)(2,1)} %concatenate.23), channel_id=1, source_target_pairs={{0,24},{1,25},{2,26},{3,27},{4,28},{5,29},{6,30},{7,31},{8,0},{9,1... | collective-permute-start | bytes 1253384 | tf_op jit(solution)/shard_map/ppermute | solution.py:39
  40.2 18.5 %all-to-all-start.1 = ((f32[32,2,128]{2,1,0:T(2,128)}), f32[32,2,128]{2,1,0:T(2,128)}, u32[]{:S(2)}, u32[]{:S(2)}) async-start(f32[32,2,128]{2,1,0:T(2,128)} %broadcast_in_dim.9), calls=%async_computation.1 | async-start | bytes 65536 | tf_op jit(solution)/shard_map/all_to_all | solution.py:48
  70.2 21.6 %copy-start.3 = (bf16[128,384]{1,0:T(8,128)(2,1)S(1)}, bf16[128,384]{1,0:T(8,128)(2,1)}, u32[]{:S(2)}) copy-start(bf16[128,384]{1,0:T(8,128)(2,1)} %param.5) | copy-start | bytes 294916
  70.2 21.6 %copy-start.4 = (f32[384]{0:T(512)S(1)}, f32[384]{0:T(512)}, u32[]{:S(2)}) copy-start(f32[384]{0:T(512)} %param.6) | copy-start | bytes 4612
  70.2 21.6 %copy-start.5 = (f32[384]{0:T(512)S(1)}, f32[384]{0:T(512)}, u32[]{:S(2)}) copy-start(f32[384]{0:T(512)} %param.7) | copy-start | bytes 4612
  70.3 13.4 %collective-permute-start.5 = (f16[144,384]{1,0:T(8,128)(2,1)S(1)}, f16[144,384]{1,0:T(8,128)(2,1)S(1)}, u32[]{:S(2)}, u32[]{:S(2)}) collective-permute-start(f16[144,384]{1,0:T(8,128)(2,1)S(1)} %concatenate.24), channel_id=1, source_target_pairs={{0,0},{1,1},{2,32},{3,33},{4,2},{5,3},{6,34},{7,35},{8,64},{9,65},... | collective-permute-start | bytes 331784 | tf_op jit(solution)/shard_map/ppermute | solution.py:39
  71.0 13.9 %collective-permute-start.6 = (f16[144,384]{1,0:T(8,128)(2,1)S(1)}, f16[144,384]{1,0:T(8,128)(2,1)S(1)}, u32[]{:S(2)}, u32[]{:S(2)}) collective-permute-start(f16[144,384]{1,0:T(8,128)(2,1)S(1)} %concatenate.25), channel_id=1, source_target_pairs={{0,32},{1,33},{2,2},{3,3},{4,34},{5,35},{6,0},{7,1},{8,96},{9,97},... | collective-permute-start | bytes 331784 | tf_op jit(solution)/shard_map/ppermute | solution.py:39
  78.4 11.0 %collective-permute-start.7 = (f16[144,384]{1,0:T(8,128)(2,1)S(1)}, f16[144,384]{1,0:T(8,128)(2,1)S(1)}, u32[]{:S(2)}, u32[]{:S(2)}) collective-permute-start(f16[144,384]{1,0:T(8,128)(2,1)S(1)} %concatenate.26), channel_id=1, source_target_pairs={{0,2},{1,3},{2,34},{3,35},{4,0},{5,1},{6,32},{7,33},{8,66},{9,67},... | collective-permute-start | bytes 331784 | tf_op jit(solution)/shard_map/ppermute | solution.py:39
  78.5 12.0 %collective-permute-start.8 = (f16[144,384]{1,0:T(8,128)(2,1)S(1)}, f16[144,384]{1,0:T(8,128)(2,1)S(1)}, u32[]{:S(2)}, u32[]{:S(2)}) collective-permute-start(f16[144,384]{1,0:T(8,128)(2,1)S(1)} %concatenate.27), channel_id=1, source_target_pairs={{0,34},{1,35},{2,0},{3,1},{4,32},{5,33},{6,2},{7,3},{8,98},{9,99},... | collective-permute-start | bytes 331784 | tf_op jit(solution)/shard_map/ppermute | solution.py:39
  92.0 37.1 %collective-permute-start.9 = (bf16[128,384]{1,0:T(8,128)(2,1)S(1)}, bf16[128,384]{1,0:T(8,128)(2,1)S(1)}, u32[]{:S(2)}, u32[]{:S(2)}) collective-permute-start(bf16[128,384]{1,0:T(8,128)(2,1)S(1)} %get-tuple-element.22), channel_id=1, source_target_pairs={{0,0},{1,1},{32,2},{33,3},{2,4},{3,5},{34,6},{35,7},{64,8},{65,9},... | collective-permute-start | bytes 294920 | tf_op jit(solution)/shard_map/ppermute | solution.py:39
  92.7 36.4 %collective-permute-start.10 = (bf16[128,384]{1,0:T(8,128)(2,1)S(1)}, bf16[128,384]{1,0:T(8,128)(2,1)S(1)}, u32[]{:S(2)}, u32[]{:S(2)}) collective-permute-start(bf16[128,384]{1,0:T(8,128)(2,1)S(1)} %get-tuple-element.22), channel_id=1, source_target_pairs={{32,0},{33,1},{2,2},{3,3},{34,4},{35,5},{0,6},{1,7},{96,8},{97,9},... | collective-permute-start | bytes 294920 | tf_op jit(solution)/shard_map/ppermute | solution.py:39
  98.0 31.2 %collective-permute-start.11 = (bf16[128,384]{1,0:T(8,128)(2,1)S(1)}, bf16[128,384]{1,0:T(8,128)(2,1)S(1)}, u32[]{:S(2)}, u32[]{:S(2)}) collective-permute-start(bf16[128,384]{1,0:T(8,128)(2,1)S(1)} %get-tuple-element.22), channel_id=1, source_target_pairs={{2,0},{3,1},{34,2},{35,3},{0,4},{1,5},{32,6},{33,7},{66,8},{67,9},... | collective-permute-start | bytes 294920 | tf_op jit(solution)/shard_map/ppermute | solution.py:39
  100.6 28.6 %collective-permute-start.12 = (bf16[128,384]{1,0:T(8,128)(2,1)S(1)}, bf16[128,384]{1,0:T(8,128)(2,1)S(1)}, u32[]{:S(2)}, u32[]{:S(2)}) collective-permute-start(bf16[128,384]{1,0:T(8,128)(2,1)S(1)} %get-tuple-element.22), channel_id=1, source_target_pairs={{34,0},{35,1},{0,2},{1,3},{32,4},{33,5},{2,6},{3,7},{98,8},{99,9},... | collective-permute-start | bytes 294920 | tf_op jit(solution)/shard_map/ppermute | solution.py:39
  103.2 31.0 %all-to-all-start.3 = ((f32[8,2,384]{2,1,0:T(2,128)}), f32[8,2,384]{2,1,0:T(2,128)S(1)}, u32[]{:S(2)}, u32[]{:S(2)}) async-start(f32[8,2,384]{2,1,0:T(2,128)} %broadcast_in_dim.11), calls=%async_computation.3 | async-start | bytes 49152 | tf_op jit(solution)/shard_map/all_to_all | solution.py:48
  129.8 28.9 %collective-permute-start.13 = (bf16[256,768]{1,0:T(8,128)(2,1)S(1)}, bf16[256,768]{1,0:T(8,128)(2,1)S(1)}, u32[]{:S(2)}, u32[]{:S(2)}) collective-permute-start(bf16[256,768]{1,0:T(8,128)(2,1)S(1)} %bitcast.127), channel_id=1, source_target_pairs={{0,8},{1,9},{2,10},{3,11},{4,12},{5,13},{6,14},{7,15},{8,16},{9,17... | collective-permute-start | bytes 1179656 | tf_op jit(solution)/shard_map/ppermute | solution.py:39
  134.8 21.1 %all-to-all-start.2 = ((f32[32,2,128]{2,1,0:T(2,128)}), f32[32,2,128]{2,1,0:T(2,128)S(1)}, u32[]{:S(2)}, u32[]{:S(2)}) async-start(f32[32,2,128]{2,1,0:T(2,128)} %broadcast_in_dim.10), calls=%async_computation.2 | async-start | bytes 65536 | tf_op jit(solution)/shard_map/all_to_all | solution.py:48
  156.0 11.9 %collective-permute-start.14 = (bf16[256,768]{1,0:T(8,128)(2,1)S(1)}, bf16[256,768]{1,0:T(8,128)(2,1)S(1)}, u32[]{:S(2)}, u32[]{:S(2)}) collective-permute-start(bf16[256,768]{1,0:T(8,128)(2,1)S(1)} %bitcast.128), channel_id=1, source_target_pairs={{0,16},{1,17},{2,18},{3,19},{4,20},{5,21},{6,22},{7,23},{8,24},{9,... | collective-permute-start | bytes 1179656 | tf_op jit(solution)/shard_map/ppermute | solution.py:39
  157.0 17.8 %collective-permute-start.15 = (bf16[256,768]{1,0:T(8,128)(2,1)S(1)}, bf16[256,768]{1,0:T(8,128)(2,1)S(1)}, u32[]{:S(2)}, u32[]{:S(2)}) collective-permute-start(bf16[256,768]{1,0:T(8,128)(2,1)S(1)} %bitcast.129), channel_id=1, source_target_pairs={{0,24},{1,25},{2,26},{3,27},{4,28},{5,29},{6,30},{7,31},{8,0},{9,1... | collective-permute-start | bytes 1179656 | tf_op jit(solution)/shard_map/ppermute | solution.py:39
  175.6 3.8 %collective-permute-start.16 = (f32[768,384]{1,0:T(8,128)S(1)}, f32[768,384]{1,0:T(8,128)S(1)}, u32[]{:S(2)}, u32[]{:S(2)}) collective-permute-start(f32[768,384]{1,0:T(8,128)S(1)} %fusion.1), channel_id=1, source_target_pairs={{0,1},{1,0},{2,3},{3,2},{4,5},{5,4},{6,7},{7,6},{8,9},{9,8},{10,11... | collective-permute-start | bytes 3538952 | tf_op jit(solution)/shard_map/ppermute | solution.py:39
  (3 other events, 14.4 us)

commit v2 on v0

v2 whole, which is shorter than its diff:
```python
import jax
import jax.numpy as jnp
from jax import lax
from jax.experimental import pallas as pl
from jax.experimental.pallas import tpu as pltpu
from jax.sharding import PartitionSpec as P

AXES = ("dp", "tensor")
DATA, TENSOR = 8, 32
CAP = 32768.0
ROWS_BY_ROWS = (((1,), (1,)), ((), ()))
COLUMNS_BY_COLUMNS = (((0,), (0,)), ((), ()))


def flat(x, zl, y, zh, c):
    return ((x * 2 + zl) * 4 + y) * 8 + zh * 2 + c


def table(move):
    pairs = []
    for d in range(DATA):
        for t in range(TENSOR):
            place = (d // 2, d % 2, t // 8, (t // 2) % 4, t % 2)
            pairs.append((flat(*place), flat(*move(*place))))
    return pairs


def to_owner(k):
    def move(x, zl, y, zh, c):
        s = (zh + k) % 4
        return (y, s % 2, x, 2 * zl + s // 2, c)

    return table(move)


CORE = table(lambda x, zl, y, zh, c: (x, zl, y, zh, 1 - c))
ALONG_X = [
    [table(lambda x, zl, y, zh, c, i=i, j=j: ((x + i) % 4, zl ^ j, y, zh, c)) for j in range(2)] for i in range(4)
]
ALONG_Y = [table(lambda x, zl, y, zh, c, k=k: (x, zl, (y + k) % 4, zh, c)) for k in range(4)]
OWNER = [to_owner(k) for k in range(4)]
HOLDER = table(lambda x, zl, y, zh, c: (y, zh // 2, x, 2 * (zh % 2) + zl, c))
Z_GROUPS = [[8 * y + 2 * z + c for z in range(4)] for y in range(4) for c in range(2)]


def send(array, pairs):
    return lax.ppermute(array, AXES, pairs)


def after(array, *others):
    return lax.optimization_barrier((array,) + others)[0]


def exchange(array, axis, groups=None):
    return lax.all_to_all(array, axis, split_axis=0, concat_axis=0, tiled=True, axis_index_groups=groups)


def copies(array, size):
    return jnp.broadcast_to(array[None], (size,) + array.shape)


def highest(array):
    return jnp.max(jnp.abs(array), keepdims=True).reshape(1, 1).astype(jnp.float32)


def weight_kernel(at_ref, first_ref, second_ref, third_ref, fourth_ref, columns_ref, out_ref):
    total = None
    for k, block_ref in enumerate((first_ref, second_ref, third_ref, fourth_ref)):
        term = lax.dot_general(
            block_ref[0], columns_ref[at_ref[k]], COLUMNS_BY_COLUMNS, preferred_element_type=jnp.float32
        )
        total = term if total is None else total + term
    out_ref[...] = total.reshape(out_ref.shape)


def fill_kernel(core_ref, values_ref, whole_ref, out_ref):
    out_ref[...] = values_ref[...].reshape(out_ref.shape)


def weight_part(at, blocks, columns, place=None):
    halves, rows, width = blocks[0].shape
    block = pl.BlockSpec((1, rows, width), lambda i, at: (i, 0, 0))
    if place is None:
        out_shape = jax.ShapeDtypeStruct((halves, width, width), jnp.float32)
        out_spec = pl.BlockSpec((1, width, width), lambda i, at: (i, 0, 0))
    else:
        out_shape = jax.ShapeDtypeStruct((halves, 2, width, width), jnp.float32)
        out_spec = pl.BlockSpec((1, 1, width, width), lambda i, at: (i, at[4], 0, 0))
    return pl.pallas_call(
        weight_kernel,
        out_shape=out_shape,
        grid_spec=pltpu.PrefetchScalarGridSpec(
            num_scalar_prefetch=1,
            grid=(halves,),
            in_specs=[block] * 4 + [pl.BlockSpec(columns.shape, lambda i, at: (0, 0, 0))],
            out_specs=out_spec,
        ),
        compiler_params=pltpu.CompilerParams(vmem_limit_bytes=32 * 1024 * 1024),
        cost_estimate=pl.CostEstimate(
            flops=8 * halves * rows * width * width, bytes_accessed=8 * halves * rows * width, transcendentals=0
        ),
    )(at, *blocks, columns)


def fill(core, values, whole):
    halves, width, _ = values.shape
    return pl.pallas_call(
        fill_kernel,
        out_shape=jax.ShapeDtypeStruct(whole.shape, whole.dtype),
        grid_spec=pltpu.PrefetchScalarGridSpec(
            num_scalar_prefetch=1,
            grid=(halves,),
            in_specs=[
                pl.BlockSpec((1, width, width), lambda i, core: (i, 0, 0)),
                pl.BlockSpec(memory_space=pl.ANY),
            ],
            out_specs=pl.BlockSpec((1, 1, width, width), lambda i, core: (i, core[0], 0, 0)),
        ),
        input_output_aliases={2: 0},
        compiler_params=pltpu.CompilerParams(vmem_limit_bytes=32 * 1024 * 1024),
    )(core, values, whole)


def body(hidden_in, ln_gain, ln_bias, q_weight, grad_query):
    tokens, width = hidden_in.shape
    d, t = lax.axis_index("dp"), lax.axis_index("tensor")
    x, zl, y, zh, c = d // 2, d % 2, t // 8, (t // 2) % 4, t % 2
    features = width * TENSOR

    there = send(grad_query, ALONG_X[0][1])
    pair = jnp.where(zl == 0, jnp.concatenate([grad_query, there]), jnp.concatenate([there, grad_query]))
    query = jnp.stack([pair] + [send(pair, ALONG_X[i][0]) for i in (1, 2, 3)])

    values = hidden_in.astype(jnp.float32)
    told = jnp.concatenate([jnp.sum(values, axis=1), jnp.sum(values * values, axis=1)])
    told = exchange(copies(after(told, there), TENSOR), "tensor")
    query, told = lax.optimization_barrier((query, told))
    sums = jnp.sum(told, axis=0) / features
    row_mean = sums[:tokens, None]
    inv_std = lax.rsqrt(sums[tokens:, None] - row_mean * row_mean + 1e-05)
    standard = (values - row_mean) * inv_std
    normed = (standard * ln_gain + ln_bias).astype(jnp.bfloat16)

    quarters = q_weight.reshape(2, 2, width, width)
    mine = lax.dynamic_index_in_dim(quarters, c, axis=1, keepdims=False).reshape(2 * width, width)
    theirs = lax.dynamic_index_in_dim(quarters, 1 - c, axis=1, keepdims=False).reshape(2 * width, width)
    theirs = send(theirs, CORE)
    query_other = send(query, CORE)
    bound = width * highest(query) * highest(q_weight)
    bound = bound + send(bound, CORE)
    power = jnp.clip(jnp.floor(jnp.log2(CAP / bound)), -100.0, 100.0)

    at = [(x - y - k) % 4 for k in range(4)]
    own_tokens = [lax.dynamic_index_in_dim(query, at[k], axis=0, keepdims=False) for k in range(4)]
    other_tokens = [lax.dynamic_index_in_dim(query_other, at[k], axis=0, keepdims=False) for k in range(4)]

    extended = 2 * tokens + 16
    last = lax.broadcasted_iota(jnp.int32, (extended, 2 * width), 0) >= 2 * tokens
    longer = lambda array: jnp.pad(array, ((0, 16), (0, 0)))
    sent, received = [], []
    for k in (2, 1, 3, 0):
        part = lax.dot_general(
            longer(own_tokens[k]), mine, ROWS_BY_ROWS, preferred_element_type=jnp.float32
        ) + lax.dot_general(longer(other_tokens[k]), theirs, ROWS_BY_ROWS, preferred_element_type=jnp.float32)
        sent.append(jnp.where(last, power, part * jnp.exp2(power)).astype(jnp.float16))
        received.append(send(sent[-1], ALONG_Y[k]) if k else sent[-1])


    normed = send(after(normed, *sent), HOLDER)
    *received, normed = lax.optimization_barrier((*received, normed))

    powers = [lax.dynamic_slice(message, (2 * tokens, 0), (1, 1)).astype(jnp.float32) for message in received]
    power = jnp.minimum(jnp.minimum(powers[0], powers[1]), jnp.minimum(powers[2], powers[3])) - 2.0
    scales = [jnp.exp2(power - other) for other in powers]
    last = lax.broadcasted_iota(jnp.int32, (tokens + 16, width), 0) >= tokens
    pieces = []
    for k in range(4):
        s = (zh + k) % 4
        cut = ((s % 2) * tokens, (s // 2) * width)
        piece = sum(
            lax.dynamic_slice(message, cut, (tokens + 16, width)).astype(jnp.float32) * scale
            for message, scale in zip(received, scales)
        )
        pieces.append(jnp.where(last, power, piece).astype(jnp.float16))
    pieces = [send(piece, OWNER[k]) for k, piece in enumerate(pieces)]

    block = exchange(copies(normed, 4), "tensor", Z_GROUPS).reshape(2, 2 * tokens, width)
    pieces, block = lax.optimization_barrier((pieces, block))
    blocks = [block] + [send(block, ALONG_Y[k]) for k in (1, 2, 3)]

    grad_normed = sum(
        piece[:tokens].astype(jnp.float32) * jnp.exp2(-piece[tokens : tokens + 1].astype(jnp.float32)) for piece in pieces
    )

    scaled = grad_normed * ln_gain
    told = jnp.concatenate([jnp.sum(scaled, axis=1), jnp.sum(scaled * standard, axis=1)])
    told = exchange(copies(told, TENSOR), "tensor")
    sums = jnp.stack([jnp.sum(grad_normed * standard, axis=0), jnp.sum(grad_normed, axis=0)])
    other = send(sums, ALONG_X[0][1])
    told, other, blocks = lax.optimization_barrier((told, other, blocks))
    sums = sums + other
    sums = sums + send(sums, ALONG_X[1][0]) + send(sums, ALONG_X[2][0]) + send(sums, ALONG_X[3][0])
    told = jnp.sum(told, axis=0) / features
    grad_input = inv_std * (scaled - told[:tokens, None] - standard * told[tokens:, None])

    at = jnp.stack([(x - y + k) % 4 for k in range(4)] + [c]).astype(jnp.int32)
    grad_other = send(weight_part(at, blocks, query_other), CORE)
    grad_mine = weight_part(at, blocks, query, c)
    grad_weight = fill((1 - c).astype(jnp.int32).reshape(1), grad_other, grad_mine).reshape(4 * width, width)
    return (grad_input, grad_weight, sums[0], sums[1])


def solution(mesh):
    placed = (P("dp", "tensor"), P("tensor"), P("tensor"), P("dp", "tensor"), P("dp", "tensor"))
    return jax.shard_map(
        body,
        mesh=mesh,
        in_specs=placed,
        out_specs=(P("dp", "tensor"), P("dp", "tensor"), P("tensor"), P("tensor")),
        check_vma=False,
    )
```

time: 772 us -> 149 us (0.19)
  waiting for transfers between devices: 574 us -> 46.2 us
  blocking collectives: 160 us -> 0 us
  starting transfers between devices: 0.16 us -> 68.6 us
  matrix products: 20.4 us -> 3.21 us
  local copies, waits for them, and re-layouts: 0.83 us -> 9.32 us
    reduce_scatter x2 -> x0, waiting for transfers between devices: 316 us -> none  [the longest x1 280 us: body(): lax.psum_scatter(lax.dot_general(normed, grad_query, (((0,), (0,)), ((),...]
    all_gather x2 -> x0, waiting for transfers between devices: 257 us -> none  [the longest x1 196 us: body(): lax.all_gather(q_weight, 'dp', axis=0, tiled=True)]
    psum x3 -> x0, blocking collectives: 160 us -> none  [the longest x1 72.3 us: body(): lax.psum((jnp.sum(values, axis=1), jnp.sum(values * values, axis=1)), 'te...]
    ppermute x0 -> x23, starting transfers between devices: none -> 44.4 us  [send(): return lax.ppermute(array, AXES, pairs)]
    ppermute x0 -> x23, waiting for transfers between devices: none -> 27.8 us  [send(): return lax.ppermute(array, AXES, pairs)]
    all_to_all x0 -> x3, starting transfers between devices: none -> 24.2 us  [exchange(): lax.all_to_all(array, axis, split_axis=0, concat_axis=0, tiled=True, axis...]
    all_to_all x0 -> x3, waiting for transfers between devices: none -> 18.4 us  [exchange(): lax.all_to_all(array, axis, split_axis=0, concat_axis=0, tiled=True, axis...]
    dot_general x2 -> x8, matrix products: 20.4 us -> 3.21 us  [the longest x4 1.62 us: body(): lax.dot_general(longer(other_tokens[k]), theirs, ROWS_BY_ROWS, preferred_...]
  transfers between devices with their start and end apart: 4 -> 26, of which waited for: 4 -> 7; matrix products, arithmetic and copies ran while one was open for 0% -> 13% of each run, Pallas kernels for 0% -> 2%
where the time goes in v2:
time: 149 us; the launch traced here: 148 us
  starting transfers between devices  68.6 us (46%)
  waiting for transfers between devices  46.2 us (31%)
  local copies, waits for them, and re-layouts  9.32 us (6%)
  other arithmetic  7.33 us (5%)
  Pallas kernels  7.33 us (5%)
  between operations  6.14 us (4%)
  matrix products  3.21 us (2%)
    ppermute x23, starting transfers between devices, send(): return lax.ppermute(array, AXES, pairs)  44.4 us
    ppermute x23, waiting for transfers between devices, send(): return lax.ppermute(array, AXES, pairs)  27.8 us
    all_to_all x3, starting transfers between devices, exchange(): lax.all_to_all(array, axis, split_axis=0, concat_axis=0, tiled=True, axis...  24.2 us
    all_to_all x3, waiting for transfers between devices, exchange(): lax.all_to_all(array, axis, split_axis=0, concat_axis=0, tiled=True, axis...  18.4 us
    pallas_call x2, Pallas kernels, weight_part(): pl.pallas_call(weight_kernel, out_shape=out_shape, grid_spec=pltpu.Prefet...  5.22 us
    dynamic_slice x4, local copies, waits for them, and re-layouts, body(): lax.dynamic_slice(message, (2 * tokens, 0), (1, 1)).astype(jnp.float32)  4.08 us
  transfers between devices with their start and end apart: 26, of which 7 were waited for; matrix products, arithmetic and copies ran while one was open for 13% of the time, Pallas kernels for 2%

profile of v2, /device:TPU:1, one launch (start us, length us, event | category | flops | bytes accessed | tf_op | source)
XLA Modules:
  0.0 148.2 jit_solution(3517191336949846490)
XLA Ops:
  0.6 2.6 %collective-permute-start = (bf16[128,384]{1,0:T(8,128)(2,1)}, bf16[128,384]{1,0:T(8,128)(2,1)S(1)}, u32[]{:S(2)}, u32[]{:S(2)}) collective-permute-start(bf16[128,384]{1,0:T(8,128)(2,1)} %param.9), channel_id=1, source_target_pairs={{0,32},{1,33},{2,34},{3,35},{4,36},{5,37},{6,38},{7,39},{8,40},{9,... | collective-permute-start | bytes 294920 | tf_op jit(solution)/shard_map/ppermute | solution.py:47
  3.2 2.3 %constant_dynamic-slice_fusion = (bf16[2,1,384,384]{3,2,1,0:T(8,128)(2,1)}, bf16[2,1,384,384]{3,2,1,0:T(8,128)(2,1)S(1)}) fusion(bf16[2,2,384,384]{3,2,1,0:T(8,128)(2,1)} %bitcast.64, s32[]{:T(128)S(6)} %select_n.227, s32[]{:T(128)S(6)} %select_n.226), kind=kLoop, calls=%fused_computation.66 | loop fusion | bytes 2359304 | tf_op jit(solution)/shard_map/jit(dynamic_index_in_dim)/dynamic_slice | solution.py:146
  7.4 2.6 %collective-permute-start.3 = (bf16[256,384]{1,0:T(8,128)(2,1)S(1)}, bf16[256,384]{1,0:T(8,128)(2,1)S(1)}, u32[]{:S(2)}, u32[]{:S(2)}) collective-permute-start(bf16[256,384]{1,0:T(8,128)(2,1)S(1)} %maximum_select_fusion.1), channel_id=1, source_target_pairs={{0,192},{1,193},{2,194},{3,195},{4,196},{5,197},{6,198},{7,199},{8... | collective-permute-start | bytes 589832 | tf_op jit(solution)/shard_map/ppermute | solution.py:47
  11.7 11.8 %all-to-all-start = ((f32[32,1,256]{2,1,0:T(1,128)}), f32[32,1,256]{2,1,0:T(1,128)S(1)}, u32[]{:S(2)}, u32[]{:S(2)}) async-start(f32[32,1,256]{2,1,0:T(1,128)} %broadcast_in_dim.64), calls=%async_computation | async-start | bytes 65536 | tf_op jit(solution)/shard_map/all_to_all | solution.py:55
  23.6 9.6 %all-to-all-done = f32[32,1,256]{2,1,0:T(1,128)S(1)} async-done(((f32[32,1,256]{2,1,0:T(1,128)}), f32[32,1,256]{2,1,0:T(1,128)S(1)}, u32[]{:S(2)}, u32[]{:S(2)}) %all-to-all-start) | async-done | bytes 32800 | tf_op jit(solution)/shard_map/all_to_all | solution.py:55
  41.3 1.3 collective-permute-start.7
  44.4 6.5 %collective-permute-done.9 = f16[272,768]{1,0:T(8,128)(2,1)} collective-permute-done((f16[272,768]{1,0:T(8,128)(2,1)S(1)}, f16[272,768]{1,0:T(8,128)(2,1)}, u32[]{:S(2)}, u32[]{:S(2)}) %collective-permute-start.9) | collective-permute-done | bytes 417824 | tf_op jit(solution)/shard_map/ppermute | solution.py:47
  50.9 4.3 %collective-permute-done.7 = f16[272,768]{1,0:T(8,128)(2,1)} collective-permute-done((f16[272,768]{1,0:T(8,128)(2,1)S(1)}, f16[272,768]{1,0:T(8,128)(2,1)}, u32[]{:S(2)}, u32[]{:S(2)}) %collective-permute-start.7) | collective-permute-done | bytes 417824 | tf_op jit(solution)/shard_map/ppermute | solution.py:47
  55.2 9.0 %collective-permute-done.8 = f16[272,768]{1,0:T(8,128)(2,1)} collective-permute-done((f16[272,768]{1,0:T(8,128)(2,1)S(1)}, f16[272,768]{1,0:T(8,128)(2,1)}, u32[]{:S(2)}, u32[]{:S(2)}) %collective-permute-start.8) | collective-permute-done | bytes 417824 | tf_op jit(solution)/shard_map/ppermute | solution.py:47
  65.0 3.5 %all-to-all-start.1 = ((bf16[4,128,384]{2,1,0:T(8,128)(2,1)}), bf16[4,128,384]{2,1,0:T(8,128)(2,1)S(1)}, u32[]{:S(2)}, u32[]{:S(2)}) async-start(bf16[4,128,384]{2,1,0:T(8,128)(2,1)} %broadcast_in_dim.69), calls=%async_computation.1 | async-start | bytes 786432 | tf_op jit(solution)/shard_map/all_to_all | solution.py:55
  75.5 1.8 %select_convert_fusion = (f16[144,384]{1,0:T(8,128)(2,1)S(1)}, f16[144,384]{1,0:T(8,128)(2,1)S(1)}, f16[144,384]{1,0:T(8,128)(2,1)S(1)}, f16[144,384]{1,0:T(8,128)(2,1)S(1)}) fusion(f16[272,768]{1,0:T(8,128)(2,1)S(1)} %fusion.8, s32[]{:T(128)S(6)} %select_n.260, s32[]{:T(128)S(6)} %select_n.262, f16[272,768]{1,0:T(8,128)(2,1)} %collective-permute-done.9, ...), kind=kLoop, calls=%fused_computation.22 | loop fusion | flops 2875392 | bytes 2212036 | tf_op jit(solution)/shard_map/convert_element_type | solution.py:184
  77.3 4.4 %collective-permute-start.14 = (f16[144,384]{1,0:T(8,128)(2,1)S(1)}, f16[144,384]{1,0:T(8,128)(2,1)S(1)}, u32[]{:S(2)}, u32[]{:S(2)}) collective-permute-start(f16[144,384]{1,0:T(8,128)(2,1)S(1)} %get-tuple-element.53), channel_id=1, source_target_pairs={{0,34},{1,35},{2,0},{3,1},{4,32},{5,33},{6,2},{7,3},{8,98},{9,99},... | collective-permute-start | bytes 331784 | tf_op jit(solution)/shard_map/ppermute | solution.py:47
  82.1 5.9 %collective-permute-start.12 = (f16[144,384]{1,0:T(8,128)(2,1)S(1)}, f16[144,384]{1,0:T(8,128)(2,1)}, u32[]{:S(2)}, u32[]{:S(2)}) collective-permute-start(f16[144,384]{1,0:T(8,128)(2,1)S(1)} %get-tuple-element.55), channel_id=1, source_target_pairs={{0,32},{1,33},{2,2},{3,3},{4,34},{5,35},{6,0},{7,1},{8,96},{9,97},... | collective-permute-start | bytes 331784 | tf_op jit(solution)/shard_map/ppermute | solution.py:47
  88.0 1.3 collective-permute-start.11
  89.9 7.4 %collective-permute-done.12 = f16[144,384]{1,0:T(8,128)(2,1)} collective-permute-done((f16[144,384]{1,0:T(8,128)(2,1)S(1)}, f16[144,384]{1,0:T(8,128)(2,1)}, u32[]{:S(2)}, u32[]{:S(2)}) %collective-permute-start.12) | collective-permute-done | bytes 110624 | tf_op jit(solution)/shard_map/ppermute | solution.py:47
  97.3 15.5 %collective-permute-start.18 = (bf16[2,256,384]{2,1,0:T(8,128)(2,1)S(1)}, bf16[2,256,384]{2,1,0:T(8,128)(2,1)S(1)}, u32[]{:S(2)}, u32[]{:S(2)}) collective-permute-start(bf16[2,256,384]{2,1,0:T(8,128)(2,1)S(1)} %bitcast.54), channel_id=1, source_target_pairs={{0,24},{1,25},{2,26},{3,27},{4,28},{5,29},{6,30},{7,31},{8,0},{9,1... | collective-permute-start | bytes 1179656 | tf_op jit(solution)/shard_map/ppermute | solution.py:47
  114.9 1.3 fusion.33
  116.8 8.9 %all-to-all-start.2 = ((f32[32,1,256]{2,1,0:T(1,128)}), f32[32,1,256]{2,1,0:T(1,128)S(1)}, u32[]{:S(2)}, u32[]{:S(2)}) async-start(f32[32,1,256]{2,1,0:T(1,128)} %broadcast_in_dim.70), calls=%async_computation.2 | async-start | bytes 65536 | tf_op jit(solution)/shard_map/all_to_all | solution.py:55
  126.6 8.8 %all-to-all-done.2 = f32[32,1,256]{2,1,0:T(1,128)S(1)} async-done(((f32[32,1,256]{2,1,0:T(1,128)}), f32[32,1,256]{2,1,0:T(1,128)S(1)}, u32[]{:S(2)}, u32[]{:S(2)}) %all-to-all-start.2) | async-done | bytes 32800 | tf_op jit(solution)/shard_map/all_to_all | solution.py:55
  135.5 2.6 %shard_map.84 = f32[2,384,384]{2,1,0:T(8,128)} custom-call(s32[5]{0:T(128)S(1)} %stack.52.at_ref, bf16[2,256,384]{2,1,0:T(8,128)(2,1)S(1)} %bitcast.57, bf16[2,256,384]{2,1,0:T(8,128)(2,1)S(1)} %collective-permute-done.16.second_ref, bf16[2,256,384]{2,1,0:T(8,128)(2,1)S(1)} %collective-permute-done.17.third_ref, ...), custom_call_target="tpu_custom_call" | custom-call | flops 603979776 | bytes 1572864 | tf_op jit(solution)/shard_map/pallas_call | solution.py:89
  138.5 1.5 %collective-permute-start.21 = (f32[2,384]{1,0:T(2,128)S(1)}, f32[2,384]{1,0:T(2,128)S(1)}, u32[]{:S(2)}, u32[]{:S(2)}) collective-permute-start(f32[2,384]{1,0:T(2,128)S(1)} %fusion.44), channel_id=1, source_target_pairs={{0,128},{1,129},{2,130},{3,131},{4,132},{5,133},{6,134},{7,135},{8... | collective-permute-start | bytes 9224 | tf_op jit(solution)/shard_map/ppermute | solution.py:47
  140.0 1.4 collective-permute-start.22
  142.8 2.6 %shard_map.85.whole_ref = f32[2,2,384,384]{3,2,1,0:T(8,128)} custom-call(s32[5]{0:T(128)S(1)} %stack.52.at_ref, bf16[2,256,384]{2,1,0:T(8,128)(2,1)S(1)} %bitcast.58, bf16[2,256,384]{2,1,0:T(8,128)(2,1)S(1)} %collective-permute-done.16.second_ref, bf16[2,256,384]{2,1,0:T(8,128)(2,1)S(1)} %collective-permute-done.17.third_ref, ...), custom_call_target="tpu_custom_call" | custom-call | flops 603979776 | bytes 1572864 | tf_op jit(solution)/shard_map/pallas_call | solution.py:89
  146.1 2.1 %shard_map.86 = f32[2,2,384,384]{3,2,1,0:T(8,128)} custom-call(s32[1]{0:T(128)} %bitcast.25.core_ref, f32[2,384,384]{2,1,0:T(8,128)} %collective-permute-done.19.values_ref, f32[2,2,384,384]{3,2,1,0:T(8,128)} %shard_map.85.whole_ref), custom_call_target="tpu_custom_call", output_to_operand_aliasing={{}: (2, {})} | custom-call | tf_op jit(solution)/shard_map/pallas_call | solution.py:107
  (100 shorter events, 23.0 us)
Async XLA Ops:
  0.6 6.7 %collective-permute-start = (bf16[128,384]{1,0:T(8,128)(2,1)}, bf16[128,384]{1,0:T(8,128)(2,1)S(1)}, u32[]{:S(2)}, u32[]{:S(2)}) collective-permute-start(bf16[128,384]{1,0:T(8,128)(2,1)} %param.9), channel_id=1, source_target_pairs={{0,32},{1,33},{2,34},{3,35},{4,36},{5,37},{6,38},{7,39},{8,40},{9,... | collective-permute-start | bytes 294920 | tf_op jit(solution)/shard_map/ppermute | solution.py:47
  5.5 34.0 %collective-permute-start.6 = (bf16[768,384]{1,0:T(8,128)(2,1)}, bf16[768,384]{1,0:T(8,128)(2,1)S(1)}, u32[]{:S(2)}, u32[]{:S(2)}) collective-permute-start(bf16[768,384]{1,0:T(8,128)(2,1)} %bitcast.11), channel_id=1, source_target_pairs={{0,1},{1,0},{2,3},{3,2},{4,5},{5,4},{6,7},{7,6},{8,9},{9,8},{10,11... | collective-permute-start | bytes 1769480 | tf_op jit(solution)/shard_map/ppermute | solution.py:47
  7.4 25.8 %collective-permute-start.3 = (bf16[256,384]{1,0:T(8,128)(2,1)S(1)}, bf16[256,384]{1,0:T(8,128)(2,1)S(1)}, u32[]{:S(2)}, u32[]{:S(2)}) collective-permute-start(bf16[256,384]{1,0:T(8,128)(2,1)S(1)} %maximum_select_fusion.1), channel_id=1, source_target_pairs={{0,192},{1,193},{2,194},{3,195},{4,196},{5,197},{6,198},{7,199},{8... | collective-permute-start | bytes 589832 | tf_op jit(solution)/shard_map/ppermute | solution.py:47
  10.0 23.2 %collective-permute-start.2 = (bf16[256,384]{1,0:T(8,128)(2,1)S(1)}, bf16[256,384]{1,0:T(8,128)(2,1)S(1)}, u32[]{:S(2)}, u32[]{:S(2)}) collective-permute-start(bf16[256,384]{1,0:T(8,128)(2,1)S(1)} %maximum_select_fusion.1), channel_id=1, source_target_pairs={{0,128},{1,129},{2,130},{3,131},{4,132},{5,133},{6,134},{7,135},{8... | collective-permute-start | bytes 589832 | tf_op jit(solution)/shard_map/ppermute | solution.py:47
  10.5 22.7 %collective-permute-start.1 = (bf16[256,384]{1,0:T(8,128)(2,1)S(1)}, bf16[256,384]{1,0:T(8,128)(2,1)S(1)}, u32[]{:S(2)}, u32[]{:S(2)}) collective-permute-start(bf16[256,384]{1,0:T(8,128)(2,1)S(1)} %maximum_select_fusion.1), channel_id=1, source_target_pairs={{0,64},{1,65},{2,66},{3,67},{4,68},{5,69},{6,70},{7,71},{8,72},{9,... | collective-permute-start | bytes 589832 | tf_op jit(solution)/shard_map/ppermute | solution.py:47
  11.7 21.5 %all-to-all-start = ((f32[32,1,256]{2,1,0:T(1,128)}), f32[32,1,256]{2,1,0:T(1,128)S(1)}, u32[]{:S(2)}, u32[]{:S(2)}) async-start(f32[32,1,256]{2,1,0:T(1,128)} %broadcast_in_dim.64), calls=%async_computation | async-start | bytes 65536 | tf_op jit(solution)/shard_map/all_to_all | solution.py:55
  34.0 5.3 %collective-permute-start.5 = (bf16[4,256,384]{2,1,0:T(8,128)(2,1)S(1)}, bf16[4,256,384]{2,1,0:T(8,128)(2,1)S(1)}, u32[]{:S(2)}, u32[]{:S(2)}) collective-permute-start(bf16[4,256,384]{2,1,0:T(8,128)(2,1)S(1)} %pad_maximum_fusion.columns_ref), channel_id=1, source_target_pairs={{0,1},{1,0},{2,3},{3,2},{4,5},{5,4},{6,7},{7,6},{8,9},{9,8},{10,11... | collective-permute-start | bytes 2359304 | tf_op jit(solution)/shard_map/ppermute | solution.py:47
  39.9 11.0 %collective-permute-start.9 = (f16[272,768]{1,0:T(8,128)(2,1)S(1)}, f16[272,768]{1,0:T(8,128)(2,1)}, u32[]{:S(2)}, u32[]{:S(2)}) collective-permute-start(f16[272,768]{1,0:T(8,128)(2,1)S(1)} %fusion.9), channel_id=1, source_target_pairs={{0,24},{1,25},{2,26},{3,27},{4,28},{5,29},{6,30},{7,31},{8,0},{9,1... | collective-permute-start | bytes 1253384 | tf_op jit(solution)/shard_map/ppermute | solution.py:47
  41.3 13.9 %collective-permute-start.7 = (f16[272,768]{1,0:T(8,128)(2,1)S(1)}, f16[272,768]{1,0:T(8,128)(2,1)}, u32[]{:S(2)}, u32[]{:S(2)}) collective-permute-start(f16[272,768]{1,0:T(8,128)(2,1)S(1)} %fusion.11), channel_id=1, source_target_pairs={{0,16},{1,17},{2,18},{3,19},{4,20},{5,21},{6,22},{7,23},{8,24},{9,... | collective-permute-start | bytes 1253384 | tf_op jit(solution)/shard_map/ppermute | solution.py:47
  43.0 21.1 %collective-permute-start.8 = (f16[272,768]{1,0:T(8,128)(2,1)S(1)}, f16[272,768]{1,0:T(8,128)(2,1)}, u32[]{:S(2)}, u32[]{:S(2)}) collective-permute-start(f16[272,768]{1,0:T(8,128)(2,1)S(1)} %fusion.10), channel_id=1, source_target_pairs={{0,8},{1,9},{2,10},{3,11},{4,12},{5,13},{6,14},{7,15},{8,16},{9,17... | collective-permute-start | bytes 1253384 | tf_op jit(solution)/shard_map/ppermute | solution.py:47
  65.0 32.4 %all-to-all-start.1 = ((bf16[4,128,384]{2,1,0:T(8,128)(2,1)}), bf16[4,128,384]{2,1,0:T(8,128)(2,1)S(1)}, u32[]{:S(2)}, u32[]{:S(2)}) async-start(bf16[4,128,384]{2,1,0:T(8,128)(2,1)} %broadcast_in_dim.69), calls=%async_computation.1 | async-start | bytes 786432 | tf_op jit(solution)/shard_map/all_to_all | solution.py:55
  77.3 12.0 %collective-permute-start.14 = (f16[144,384]{1,0:T(8,128)(2,1)S(1)}, f16[144,384]{1,0:T(8,128)(2,1)S(1)}, u32[]{:S(2)}, u32[]{:S(2)}) collective-permute-start(f16[144,384]{1,0:T(8,128)(2,1)S(1)} %get-tuple-element.53), channel_id=1, source_target_pairs={{0,34},{1,35},{2,0},{3,1},{4,32},{5,33},{6,2},{7,3},{8,98},{9,99},... | collective-permute-start | bytes 331784 | tf_op jit(solution)/shard_map/ppermute | solution.py:47
  81.8 8.1 %collective-permute-start.13 = (f16[144,384]{1,0:T(8,128)(2,1)S(1)}, f16[144,384]{1,0:T(8,128)(2,1)}, u32[]{:S(2)}, u32[]{:S(2)}) collective-permute-start(f16[144,384]{1,0:T(8,128)(2,1)S(1)} %get-tuple-element.54), channel_id=1, source_target_pairs={{0,2},{1,3},{2,34},{3,35},{4,0},{5,1},{6,32},{7,33},{8,66},{9,67},... | collective-permute-start | bytes 331784 | tf_op jit(solution)/shard_map/ppermute | solution.py:47
  82.1 15.2 %collective-permute-start.12 = (f16[144,384]{1,0:T(8,128)(2,1)S(1)}, f16[144,384]{1,0:T(8,128)(2,1)}, u32[]{:S(2)}, u32[]{:S(2)}) collective-permute-start(f16[144,384]{1,0:T(8,128)(2,1)S(1)} %get-tuple-element.55), channel_id=1, source_target_pairs={{0,32},{1,33},{2,2},{3,3},{4,34},{5,35},{6,0},{7,1},{8,96},{9,97},... | collective-permute-start | bytes 331784 | tf_op jit(solution)/shard_map/ppermute | solution.py:47
  88.0 9.3 %collective-permute-start.11 = (f16[144,384]{1,0:T(8,128)(2,1)S(1)}, f16[144,384]{1,0:T(8,128)(2,1)}, u32[]{:S(2)}, u32[]{:S(2)}) collective-permute-start(f16[144,384]{1,0:T(8,128)(2,1)S(1)} %get-tuple-element.56), channel_id=1, source_target_pairs={{0,0},{1,1},{2,32},{3,33},{4,2},{5,3},{6,34},{7,35},{8,64},{9,65},... | collective-permute-start | bytes 331784 | tf_op jit(solution)/shard_map/ppermute | solution.py:47
  97.3 38.1 %collective-permute-start.18 = (bf16[2,256,384]{2,1,0:T(8,128)(2,1)S(1)}, bf16[2,256,384]{2,1,0:T(8,128)(2,1)S(1)}, u32[]{:S(2)}, u32[]{:S(2)}) collective-permute-start(bf16[2,256,384]{2,1,0:T(8,128)(2,1)S(1)} %bitcast.54), channel_id=1, source_target_pairs={{0,24},{1,25},{2,26},{3,27},{4,28},{5,29},{6,30},{7,31},{8,0},{9,1... | collective-permute-start | bytes 1179656 | tf_op jit(solution)/shard_map/ppermute | solution.py:47
  112.9 22.6 %collective-permute-start.17 = (bf16[2,256,384]{2,1,0:T(8,128)(2,1)S(1)}, bf16[2,256,384]{2,1,0:T(8,128)(2,1)S(1)}, u32[]{:S(2)}, u32[]{:S(2)}) collective-permute-start(bf16[2,256,384]{2,1,0:T(8,128)(2,1)S(1)} %bitcast.55), channel_id=1, source_target_pairs={{0,16},{1,17},{2,18},{3,19},{4,20},{5,21},{6,22},{7,23},{8,24},{9,... | collective-permute-start | bytes 1179656 | tf_op jit(solution)/shard_map/ppermute | solution.py:47
  112.9 22.6 %collective-permute-start.16 = (bf16[2,256,384]{2,1,0:T(8,128)(2,1)S(1)}, bf16[2,256,384]{2,1,0:T(8,128)(2,1)S(1)}, u32[]{:S(2)}, u32[]{:S(2)}) collective-permute-start(bf16[2,256,384]{2,1,0:T(8,128)(2,1)S(1)} %bitcast.56), channel_id=1, source_target_pairs={{0,8},{1,9},{2,10},{3,11},{4,12},{5,13},{6,14},{7,15},{8,16},{9,17... | collective-permute-start | bytes 1179656 | tf_op jit(solution)/shard_map/ppermute | solution.py:47
  116.8 18.6 %all-to-all-start.2 = ((f32[32,1,256]{2,1,0:T(1,128)}), f32[32,1,256]{2,1,0:T(1,128)S(1)}, u32[]{:S(2)}, u32[]{:S(2)}) async-start(f32[32,1,256]{2,1,0:T(1,128)} %broadcast_in_dim.70), calls=%async_computation.2 | async-start | bytes 65536 | tf_op jit(solution)/shard_map/all_to_all | solution.py:55
  125.8 9.7 %collective-permute-start.15 = (f32[2,384]{1,0:T(2,128)S(1)}, f32[2,384]{1,0:T(2,128)S(1)}, u32[]{:S(2)}, u32[]{:S(2)}) collective-permute-start(f32[2,384]{1,0:T(2,128)S(1)} %pad_maximum_fusion.1), channel_id=1, source_target_pairs={{0,32},{1,33},{2,34},{3,35},{4,36},{5,37},{6,38},{7,39},{8,40},{9,... | collective-permute-start | bytes 9224 | tf_op jit(solution)/shard_map/ppermute | solution.py:47
  138.1 8.0 %collective-permute-start.19 = (f32[2,384,384]{2,1,0:T(8,128)}, f32[2,384,384]{2,1,0:T(8,128)}, u32[]{:S(2)}, u32[]{:S(2)}) collective-permute-start(f32[2,384,384]{2,1,0:T(8,128)} %shard_map.84), channel_id=1, source_target_pairs={{0,1},{1,0},{2,3},{3,2},{4,5},{5,4},{6,7},{7,6},{8,9},{9,8},{10,11... | collective-permute-start | bytes 3538952 | tf_op jit(solution)/shard_map/ppermute | solution.py:47
  138.5 6.9 %collective-permute-start.21 = (f32[2,384]{1,0:T(2,128)S(1)}, f32[2,384]{1,0:T(2,128)S(1)}, u32[]{:S(2)}, u32[]{:S(2)}) collective-permute-start(f32[2,384]{1,0:T(2,128)S(1)} %fusion.44), channel_id=1, source_target_pairs={{0,128},{1,129},{2,130},{3,131},{4,132},{5,133},{6,134},{7,135},{8... | collective-permute-start | bytes 9224 | tf_op jit(solution)/shard_map/ppermute | solution.py:47
  140.0 5.4 %collective-permute-start.22 = (f32[2,384]{1,0:T(2,128)S(1)}, f32[2,384]{1,0:T(2,128)S(1)}, u32[]{:S(2)}, u32[]{:S(2)}) collective-permute-start(f32[2,384]{1,0:T(2,128)S(1)} %fusion.44), channel_id=1, source_target_pairs={{0,192},{1,193},{2,194},{3,195},{4,196},{5,197},{6,198},{7,199},{8... | collective-permute-start | bytes 9224 | tf_op jit(solution)/shard_map/ppermute | solution.py:47
  141.4 4.0 %collective-permute-start.20 = (f32[2,384]{1,0:T(2,128)S(1)}, f32[2,384]{1,0:T(2,128)S(1)}, u32[]{:S(2)}, u32[]{:S(2)}) collective-permute-start(f32[2,384]{1,0:T(2,128)S(1)} %fusion.44), channel_id=1, source_target_pairs={{0,64},{1,65},{2,66},{3,67},{4,68},{5,69},{6,70},{7,71},{8,72},{9,... | collective-permute-start | bytes 9224 | tf_op jit(solution)/shard_map/ppermute | solution.py:47
  (12 other events, 43.5 us)

commit v3 on v2

--- a/solution.py
+++ b/solution.py
@@ -169,37 +169,35 @@
     normed = send(after(normed, *sent), HOLDER)
     *received, normed = lax.optimization_barrier((*received, normed))
 
-    powers = [lax.dynamic_slice(message, (2 * tokens, 0), (1, 1)).astype(jnp.float32) for message in received]
-    power = jnp.minimum(jnp.minimum(powers[0], powers[1]), jnp.minimum(powers[2], powers[3])) - 2.0
-    scales = [jnp.exp2(power - other) for other in powers]
-    last = lax.broadcasted_iota(jnp.int32, (tokens + 16, width), 0) >= tokens
+    powers = jnp.stack([message[2 * tokens :, :width] for message in received]).astype(jnp.float32)
+    power = jnp.min(powers, axis=0) - 2.0
+    scales = jnp.exp2(power - powers)
     pieces = []
     for k in range(4):
         s = (zh + k) % 4
         cut = ((s % 2) * tokens, (s // 2) * width)
         piece = sum(
-            lax.dynamic_slice(message, cut, (tokens + 16, width)).astype(jnp.float32) * scale
-            for message, scale in zip(received, scales)
+            lax.dynamic_slice(message, cut, (tokens, width)).astype(jnp.float32) * scales[i, :1]
+            for i, message in enumerate(received)
         )
-        pieces.append(jnp.where(last, power, piece).astype(jnp.float16))
+        pieces.append(jnp.concatenate([piece, power]).astype(jnp.float16))
     pieces = [send(piece, OWNER[k]) for k, piece in enumerate(pieces)]
 
     block = exchange(copies(normed, 4), "tensor", Z_GROUPS).reshape(2, 2 * tokens, width)
     pieces, block = lax.optimization_barrier((pieces, block))
     blocks = [block] + [send(block, ALONG_Y[k]) for k in (1, 2, 3)]
 
-    grad_normed = sum(
-        piece[:tokens].astype(jnp.float32) * jnp.exp2(-piece[tokens : tokens + 1].astype(jnp.float32)) for piece in pieces
-    )
+    scales = jnp.exp2(-jnp.stack([piece[tokens:] for piece in pieces]).astype(jnp.float32))
+    grad_normed = sum(piece[:tokens].astype(jnp.float32) * scales[i, :1] for i, piece in enumerate(pieces))
 
     scaled = grad_normed * ln_gain
     told = jnp.concatenate([jnp.sum(scaled, axis=1), jnp.sum(scaled * standard, axis=1)])
     told = exchange(copies(told, TENSOR), "tensor")
     sums = jnp.stack([jnp.sum(grad_normed * standard, axis=0), jnp.sum(grad_normed, axis=0)])
-    other = send(sums, ALONG_X[0][1])
-    told, other, blocks = lax.optimization_barrier((told, other, blocks))
-    sums = sums + other
-    sums = sums + send(sums, ALONG_X[1][0]) + send(sums, ALONG_X[2][0]) + send(sums, ALONG_X[3][0])
+    others = [send(sums, ALONG_X[i][0]) for i in (1, 2, 3)]
+    told, others, blocks = lax.optimization_barrier((told, others, blocks))
+    sums = sums + others[0] + others[1] + others[2]
+    sums = sums + send(sums, ALONG_X[0][1])
     told = jnp.sum(told, axis=0) / features
     grad_input = inv_std * (scaled - told[:tokens, None] - standard * told[tokens:, None])
 

time: 149 us -> 143 us (0.960)
  starting transfers between devices: 68.6 us -> 65.8 us
  between operations: 6.14 us -> 3.37 us
  matrix products: 3.21 us -> 5.5 us
    dynamic_slice x4 -> x0, local copies, waits for them, and re-layouts: 4.08 us -> none  [body(): lax.dynamic_slice(message, (2 * tokens, 0), (1, 1)).astype(jnp.float32)]
    ppermute x23, starting transfers between devices: 44.4 us -> 41.3 us  [send(): return lax.ppermute(array, AXES, pairs)]
    another operation x0 -> x6, local copies, waits for them, and re-layouts: none -> 2.88 us  [the longest x2 1.44 us: body(): jnp.stack([message[2 * tokens:, :width] for message in received])]
    dot_general x4, matrix products: 1.62 us -> 3.92 us  [body(): lax.dot_general(longer(other_tokens[k]), theirs, ROWS_BY_ROWS, preferred_...]
    all_to_all x3, waiting for transfers between devices: 18.4 us -> 16.2 us  [exchange(): lax.all_to_all(array, axis, split_axis=0, concat_axis=0, tiled=True, axis...]
    convert_element_type x1 -> x0, other arithmetic: 1.8 us -> none  [body(): pieces.append(jnp.where(last, power, piece).astype(jnp.float16))]
    ppermute x23, waiting for transfers between devices: 27.8 us -> 29.6 us  [send(): return lax.ppermute(array, AXES, pairs)]
    another operation x0 -> x1, other arithmetic: none -> 1.69 us
  transfers between devices with their start and end apart: 26 -> 26, of which waited for: 7 -> 8; matrix products, arithmetic and copies ran while one was open for 13% -> 11% of each run, Pallas kernels for 2% -> 2%
where the time goes in v3:
time: 143 us; the launch traced here: 142 us
  starting transfers between devices  65.8 us (46%)
  waiting for transfers between devices  45.8 us (32%)
  local copies, waits for them, and re-layouts  8.19 us (6%)
  Pallas kernels  7.32 us (5%)
  other arithmetic  5.95 us (4%)
  matrix products  5.5 us (4%)
  between operations  3.37 us (2%)
    ppermute x23, starting transfers between devices, send(): return lax.ppermute(array, AXES, pairs)  41.3 us
    ppermute x23, waiting for transfers between devices, send(): return lax.ppermute(array, AXES, pairs)  29.6 us
    all_to_all x3, starting transfers between devices, exchange(): lax.all_to_all(array, axis, split_axis=0, concat_axis=0, tiled=True, axis...  24.5 us
    all_to_all x3, waiting for transfers between devices, exchange(): lax.all_to_all(array, axis, split_axis=0, concat_axis=0, tiled=True, axis...  16.2 us
    pallas_call x2, Pallas kernels, weight_part(): pl.pallas_call(weight_kernel, out_shape=out_shape, grid_spec=pltpu.Prefet...  5.21 us
    dot_general x4, matrix products, body(): lax.dot_general(longer(other_tokens[k]), theirs, ROWS_BY_ROWS, preferred_...  3.92 us
  transfers between devices with their start and end apart: 26, of which 8 were waited for; matrix products, arithmetic and copies ran while one was open for 11% of the time, Pallas kernels for 2%

profile of v3, /device:TPU:1, one launch (start us, length us, event | category | flops | bytes accessed | tf_op | source)
XLA Modules:
  0.0 141.9 jit_solution(12725324705976393634)
XLA Ops:
  0.6 2.6 %collective-permute-start = (bf16[128,384]{1,0:T(8,128)(2,1)}, bf16[128,384]{1,0:T(8,128)(2,1)S(1)}, u32[]{:S(2)}, u32[]{:S(2)}) collective-permute-start(bf16[128,384]{1,0:T(8,128)(2,1)} %param.9), channel_id=1, source_target_pairs={{0,32},{1,33},{2,34},{3,35},{4,36},{5,37},{6,38},{7,39},{8,40},{9,... | collective-permute-start | bytes 294920 | tf_op jit(solution)/shard_map/ppermute | solution.py:47
  3.2 2.3 %constant_dynamic-slice_fusion = (bf16[2,1,384,384]{3,2,1,0:T(8,128)(2,1)}, bf16[2,1,384,384]{3,2,1,0:T(8,128)(2,1)S(1)}) fusion(bf16[2,2,384,384]{3,2,1,0:T(8,128)(2,1)} %bitcast.75, s32[]{:T(128)S(6)} %select_n.214, s32[]{:T(128)S(6)} %select_n.213), kind=kLoop, calls=%fused_computation.85 | loop fusion | bytes 2359304 | tf_op jit(solution)/shard_map/jit(dynamic_index_in_dim)/dynamic_slice | solution.py:146
  7.4 2.6 %collective-permute-start.3 = (bf16[256,384]{1,0:T(8,128)(2,1)S(1)}, bf16[256,384]{1,0:T(8,128)(2,1)S(1)}, u32[]{:S(2)}, u32[]{:S(2)}) collective-permute-start(bf16[256,384]{1,0:T(8,128)(2,1)S(1)} %maximum_select_fusion.1), channel_id=1, source_target_pairs={{0,192},{1,193},{2,194},{3,195},{4,196},{5,197},{6,198},{7,199},{8... | collective-permute-start | bytes 589832 | tf_op jit(solution)/shard_map/ppermute | solution.py:47
  11.7 11.8 %all-to-all-start = ((f32[32,1,256]{2,1,0:T(1,128)}), f32[32,1,256]{2,1,0:T(1,128)S(1)}, u32[]{:S(2)}, u32[]{:S(2)}) async-start(f32[32,1,256]{2,1,0:T(1,128)} %broadcast_in_dim.25), calls=%async_computation | async-start | bytes 65536 | tf_op jit(solution)/shard_map/all_to_all | solution.py:55
  23.6 9.6 %all-to-all-done = f32[32,1,256]{2,1,0:T(1,128)S(1)} async-done(((f32[32,1,256]{2,1,0:T(1,128)}), f32[32,1,256]{2,1,0:T(1,128)S(1)}, u32[]{:S(2)}, u32[]{:S(2)}) %all-to-all-start) | async-done | bytes 32800 | tf_op jit(solution)/shard_map/all_to_all | solution.py:55
  42.6 1.2 collective-permute-start.7
  46.5 5.2 %collective-permute-done.9 = f16[272,768]{1,0:T(8,128)(2,1)} collective-permute-done((f16[272,768]{1,0:T(8,128)(2,1)}, f16[272,768]{1,0:T(8,128)(2,1)}, u32[]{:S(2)}, u32[]{:S(2)}) %collective-permute-start.9) | collective-permute-done | bytes 417824 | tf_op jit(solution)/shard_map/ppermute | solution.py:47
  51.7 4.9 %collective-permute-done.7 = f16[272,768]{1,0:T(8,128)(2,1)} collective-permute-done((f16[272,768]{1,0:T(8,128)(2,1)}, f16[272,768]{1,0:T(8,128)(2,1)}, u32[]{:S(2)}, u32[]{:S(2)}) %collective-permute-start.7) | collective-permute-done | bytes 417824 | tf_op jit(solution)/shard_map/ppermute | solution.py:47
  56.7 9.1 %collective-permute-done.8 = f16[272,768]{1,0:T(8,128)(2,1)} collective-permute-done((f16[272,768]{1,0:T(8,128)(2,1)}, f16[272,768]{1,0:T(8,128)(2,1)}, u32[]{:S(2)}, u32[]{:S(2)}) %collective-permute-start.8) | collective-permute-done | bytes 417824 | tf_op jit(solution)/shard_map/ppermute | solution.py:47
  68.0 3.5 %all-to-all-start.1 = ((bf16[4,128,384]{2,1,0:T(8,128)(2,1)}), bf16[4,128,384]{2,1,0:T(8,128)(2,1)S(1)}, u32[]{:S(2)}, u32[]{:S(2)}) async-start(bf16[4,128,384]{2,1,0:T(8,128)(2,1)} %broadcast_in_dim.49), calls=%async_computation.1 | async-start | bytes 786432 | tf_op jit(solution)/shard_map/all_to_all | solution.py:55
  71.5 1.7 %add_convert_fusion = (f16[128,384]{1,0:T(8,128)(2,1)S(1)}, f16[128,384]{1,0:T(8,128)(2,1)S(1)}, f16[128,384]{1,0:T(8,128)(2,1)S(1)}, f16[128,384]{1,0:T(8,128)(2,1)S(1)}) fusion(f16[272,768]{1,0:T(8,128)(2,1)S(1)} %fusion.8, s32[]{:T(128)S(6)} %select_n.244, s32[]{:T(128)S(6)} %select_n.246, f16[272,768]{1,0:T(8,128)(2,1)} %collective-permute-done.9, ...), kind=kLoop, calls=%fused_computation.53 | loop fusion | flops 2359296 | bytes 1972256 | tf_op jit(solution)/shard_map/convert
  73.4 4.7 %collective-permute-start.14 = (f16[144,384]{1,0:T(8,128)(2,1)S(1)}, f16[144,384]{1,0:T(8,128)(2,1)S(1)}, u32[]{:S(2)}, u32[]{:S(2)}) collective-permute-start(f16[144,384]{1,0:T(8,128)(2,1)S(1)} %get-tuple-element.81), channel_id=1, source_target_pairs={{0,34},{1,35},{2,0},{3,1},{4,32},{5,33},{6,2},{7,3},{8,98},{9,99},... | collective-permute-start | bytes 331784 | tf_op jit(solution)/shard_map/ppermute | solution.py:47
  78.0 3.4 %collective-permute-start.12 = (f16[144,384]{1,0:T(8,128)(2,1)S(1)}, f16[144,384]{1,0:T(8,128)(2,1)S(1)}, u32[]{:S(2)}, u32[]{:S(2)}) collective-permute-start(f16[144,384]{1,0:T(8,128)(2,1)S(1)} %get-tuple-element.82), channel_id=1, source_target_pairs={{0,32},{1,33},{2,2},{3,3},{4,34},{5,35},{6,0},{7,1},{8,96},{9,97},... | collective-permute-start | bytes 331784 | tf_op jit(solution)/shard_map/ppermute | solution.py:47
  81.7 1.3 collective-permute-start.11
  83.0 2.8 %collective-permute-done.14 = f16[144,384]{1,0:T(8,128)(2,1)S(1)} collective-permute-done((f16[144,384]{1,0:T(8,128)(2,1)S(1)}, f16[144,384]{1,0:T(8,128)(2,1)S(1)}, u32[]{:S(2)}, u32[]{:S(2)}) %collective-permute-start.14) | collective-permute-done | bytes 110624 | tf_op jit(solution)/shard_map/ppermute | solution.py:47
  85.8 6.8 %collective-permute-done.12 = f16[144,384]{1,0:T(8,128)(2,1)S(1)} collective-permute-done((f16[144,384]{1,0:T(8,128)(2,1)S(1)}, f16[144,384]{1,0:T(8,128)(2,1)S(1)}, u32[]{:S(2)}, u32[]{:S(2)}) %collective-permute-start.12) | collective-permute-done | bytes 110624 | tf_op jit(solution)/shard_map/ppermute | solution.py:47
  92.6 16.6 %collective-permute-start.20 = (bf16[2,256,384]{2,1,0:T(8,128)(2,1)S(1)}, bf16[2,256,384]{2,1,0:T(8,128)(2,1)S(1)}, u32[]{:S(2)}, u32[]{:S(2)}) collective-permute-start(bf16[2,256,384]{2,1,0:T(8,128)(2,1)S(1)} %bitcast.65), channel_id=1, source_target_pairs={{0,24},{1,25},{2,26},{3,27},{4,28},{5,29},{6,30},{7,31},{8,0},{9,1... | collective-permute-start | bytes 1179656 | tf_op jit(solution)/shard_map/ppermute | solution.py:47
  111.3 1.2 fusion.33
  113.2 9.2 %all-to-all-start.2 = ((f32[32,1,256]{2,1,0:T(1,128)}), f32[32,1,256]{2,1,0:T(1,128)S(1)}, u32[]{:S(2)}, u32[]{:S(2)}) async-start(f32[32,1,256]{2,1,0:T(1,128)} %broadcast_in_dim.50), calls=%async_computation.2 | async-start | bytes 65536 | tf_op jit(solution)/shard_map/all_to_all | solution.py:55
  122.4 2.2 %collective-permute-start.17 = (f32[2,384]{1,0:T(2,128)S(1)}, f32[2,384]{1,0:T(2,128)S(1)}, u32[]{:S(2)}, u32[]{:S(2)}) collective-permute-start(f32[2,384]{1,0:T(2,128)S(1)} %pad_maximum_fusion.6), channel_id=1, source_target_pairs={{0,192},{1,193},{2,194},{3,195},{4,196},{5,197},{6,198},{7,199},{8... | collective-permute-start | bytes 9224 | tf_op jit(solution)/shard_map/ppermute | solution.py:47
  125.5 6.6 %all-to-all-done.2 = f32[32,1,256]{2,1,0:T(1,128)S(1)} async-done(((f32[32,1,256]{2,1,0:T(1,128)}), f32[32,1,256]{2,1,0:T(1,128)S(1)}, u32[]{:S(2)}, u32[]{:S(2)}) %all-to-all-start.2) | async-done | bytes 32800 | tf_op jit(solution)/shard_map/all_to_all | solution.py:55
  132.2 2.6 %shard_map.84 = f32[2,384,384]{2,1,0:T(8,128)} custom-call(s32[5]{0:T(128)S(1)} %stack.92.at_ref, bf16[2,256,384]{2,1,0:T(8,128)(2,1)S(1)} %bitcast.68, bf16[2,256,384]{2,1,0:T(8,128)(2,1)S(1)} %collective-permute-done.18.second_ref, bf16[2,256,384]{2,1,0:T(8,128)(2,1)S(1)} %collective-permute-done.19.third_ref, ...), custom_call_target="tpu_custom_call" | custom-call | flops 603979776 | bytes 1572864 | tf_op jit(solution)/shard_map/pallas_call | solution.py:89
  136.6 2.6 %shard_map.85.whole_ref = f32[2,2,384,384]{3,2,1,0:T(8,128)} custom-call(s32[5]{0:T(128)S(1)} %stack.92.at_ref, bf16[2,256,384]{2,1,0:T(8,128)(2,1)S(1)} %bitcast.69, bf16[2,256,384]{2,1,0:T(8,128)(2,1)S(1)} %collective-permute-done.18.second_ref, bf16[2,256,384]{2,1,0:T(8,128)(2,1)S(1)} %collective-permute-done.19.third_ref, ...), custom_call_target="tpu_custom_call" | custom-call | flops 603979776 | bytes 1572864 | tf_op jit(solution)/shard_map/pallas_call | solution.py:89
  139.8 2.1 %shard_map.86 = f32[2,2,384,384]{3,2,1,0:T(8,128)} custom-call(s32[1]{0:T(128)} %bitcast.28.core_ref, f32[2,384,384]{2,1,0:T(8,128)} %collective-permute-done.21.values_ref, f32[2,2,384,384]{3,2,1,0:T(8,128)} %shard_map.85.whole_ref), custom_call_target="tpu_custom_call", output_to_operand_aliasing={{}: (2, {})} | custom-call | tf_op jit(solution)/shard_map/pallas_call | solution.py:107
  (108 shorter events, 22.0 us)
Async XLA Ops:
  0.6 6.7 %collective-permute-start = (bf16[128,384]{1,0:T(8,128)(2,1)}, bf16[128,384]{1,0:T(8,128)(2,1)S(1)}, u32[]{:S(2)}, u32[]{:S(2)}) collective-permute-start(bf16[128,384]{1,0:T(8,128)(2,1)} %param.9), channel_id=1, source_target_pairs={{0,32},{1,33},{2,34},{3,35},{4,36},{5,37},{6,38},{7,39},{8,40},{9,... | collective-permute-start | bytes 294920 | tf_op jit(solution)/shard_map/ppermute | solution.py:47
  5.5 33.9 %collective-permute-start.6 = (bf16[768,384]{1,0:T(8,128)(2,1)}, bf16[768,384]{1,0:T(8,128)(2,1)S(1)}, u32[]{:S(2)}, u32[]{:S(2)}) collective-permute-start(bf16[768,384]{1,0:T(8,128)(2,1)} %bitcast.11), channel_id=1, source_target_pairs={{0,1},{1,0},{2,3},{3,2},{4,5},{5,4},{6,7},{7,6},{8,9},{9,8},{10,11... | collective-permute-start | bytes 1769480 | tf_op jit(solution)/shard_map/ppermute | solution.py:47
  7.4 25.8 %collective-permute-start.3 = (bf16[256,384]{1,0:T(8,128)(2,1)S(1)}, bf16[256,384]{1,0:T(8,128)(2,1)S(1)}, u32[]{:S(2)}, u32[]{:S(2)}) collective-permute-start(bf16[256,384]{1,0:T(8,128)(2,1)S(1)} %maximum_select_fusion.1), channel_id=1, source_target_pairs={{0,192},{1,193},{2,194},{3,195},{4,196},{5,197},{6,198},{7,199},{8... | collective-permute-start | bytes 589832 | tf_op jit(solution)/shard_map/ppermute | solution.py:47
  10.0 23.2 %collective-permute-start.2 = (bf16[256,384]{1,0:T(8,128)(2,1)S(1)}, bf16[256,384]{1,0:T(8,128)(2,1)S(1)}, u32[]{:S(2)}, u32[]{:S(2)}) collective-permute-start(bf16[256,384]{1,0:T(8,128)(2,1)S(1)} %maximum_select_fusion.1), channel_id=1, source_target_pairs={{0,128},{1,129},{2,130},{3,131},{4,132},{5,133},{6,134},{7,135},{8... | collective-permute-start | bytes 589832 | tf_op jit(solution)/shard_map/ppermute | solution.py:47
  10.5 22.7 %collective-permute-start.1 = (bf16[256,384]{1,0:T(8,128)(2,1)S(1)}, bf16[256,384]{1,0:T(8,128)(2,1)S(1)}, u32[]{:S(2)}, u32[]{:S(2)}) collective-permute-start(bf16[256,384]{1,0:T(8,128)(2,1)S(1)} %maximum_select_fusion.1), channel_id=1, source_target_pairs={{0,64},{1,65},{2,66},{3,67},{4,68},{5,69},{6,70},{7,71},{8,72},{9,... | collective-permute-start | bytes 589832 | tf_op jit(solution)/shard_map/ppermute | solution.py:47
  11.7 21.5 %all-to-all-start = ((f32[32,1,256]{2,1,0:T(1,128)}), f32[32,1,256]{2,1,0:T(1,128)S(1)}, u32[]{:S(2)}, u32[]{:S(2)}) async-start(f32[32,1,256]{2,1,0:T(1,128)} %broadcast_in_dim.25), calls=%async_computation | async-start | bytes 65536 | tf_op jit(solution)/shard_map/all_to_all | solution.py:55
  34.0 5.2 %collective-permute-start.5 = (bf16[4,256,384]{2,1,0:T(8,128)(2,1)S(1)}, bf16[4,256,384]{2,1,0:T(8,128)(2,1)S(1)}, u32[]{:S(2)}, u32[]{:S(2)}) collective-permute-start(bf16[4,256,384]{2,1,0:T(8,128)(2,1)S(1)} %pad_maximum_fusion.columns_ref), channel_id=1, source_target_pairs={{0,1},{1,0},{2,3},{3,2},{4,5},{5,4},{6,7},{7,6},{8,9},{9,8},{10,11... | collective-permute-start | bytes 2359304 | tf_op jit(solution)/shard_map/ppermute | solution.py:47
  40.6 11.1 %collective-permute-start.9 = (f16[272,768]{1,0:T(8,128)(2,1)}, f16[272,768]{1,0:T(8,128)(2,1)}, u32[]{:S(2)}, u32[]{:S(2)}) collective-permute-start(f16[272,768]{1,0:T(8,128)(2,1)} %fusion.9), channel_id=1, source_target_pairs={{0,24},{1,25},{2,26},{3,27},{4,28},{5,29},{6,30},{7,31},{8,0},{9,1... | collective-permute-start | bytes 1253384 | tf_op jit(solution)/shard_map/ppermute | solution.py:47
  42.6 14.0 %collective-permute-start.7 = (f16[272,768]{1,0:T(8,128)(2,1)}, f16[272,768]{1,0:T(8,128)(2,1)}, u32[]{:S(2)}, u32[]{:S(2)}) collective-permute-start(f16[272,768]{1,0:T(8,128)(2,1)} %fusion.11), channel_id=1, source_target_pairs={{0,16},{1,17},{2,18},{3,19},{4,20},{5,21},{6,22},{7,23},{8,24},{9,... | collective-permute-start | bytes 1253384 | tf_op jit(solution)/shard_map/ppermute | solution.py:47
  45.0 20.7 %collective-permute-start.8 = (f16[272,768]{1,0:T(8,128)(2,1)}, f16[272,768]{1,0:T(8,128)(2,1)}, u32[]{:S(2)}, u32[]{:S(2)}) collective-permute-start(f16[272,768]{1,0:T(8,128)(2,1)} %fusion.10), channel_id=1, source_target_pairs={{0,8},{1,9},{2,10},{3,11},{4,12},{5,13},{6,14},{7,15},{8,16},{9,17... | collective-permute-start | bytes 1253384 | tf_op jit(solution)/shard_map/ppermute | solution.py:47
  68.0 24.6 %all-to-all-start.1 = ((bf16[4,128,384]{2,1,0:T(8,128)(2,1)}), bf16[4,128,384]{2,1,0:T(8,128)(2,1)S(1)}, u32[]{:S(2)}, u32[]{:S(2)}) async-start(bf16[4,128,384]{2,1,0:T(8,128)(2,1)} %broadcast_in_dim.49), calls=%async_computation.1 | async-start | bytes 786432 | tf_op jit(solution)/shard_map/all_to_all | solution.py:55
  73.4 12.4 %collective-permute-start.14 = (f16[144,384]{1,0:T(8,128)(2,1)S(1)}, f16[144,384]{1,0:T(8,128)(2,1)S(1)}, u32[]{:S(2)}, u32[]{:S(2)}) collective-permute-start(f16[144,384]{1,0:T(8,128)(2,1)S(1)} %get-tuple-element.81), channel_id=1, source_target_pairs={{0,34},{1,35},{2,0},{3,1},{4,32},{5,33},{6,2},{7,3},{8,98},{9,99},... | collective-permute-start | bytes 331784 | tf_op jit(solution)/shard_map/ppermute | solution.py:47
  78.0 14.6 %collective-permute-start.12 = (f16[144,384]{1,0:T(8,128)(2,1)S(1)}, f16[144,384]{1,0:T(8,128)(2,1)S(1)}, u32[]{:S(2)}, u32[]{:S(2)}) collective-permute-start(f16[144,384]{1,0:T(8,128)(2,1)S(1)} %get-tuple-element.82), channel_id=1, source_target_pairs={{0,32},{1,33},{2,2},{3,3},{4,34},{5,35},{6,0},{7,1},{8,96},{9,97},... | collective-permute-start | bytes 331784 | tf_op jit(solution)/shard_map/ppermute | solution.py:47
  81.4 11.2 %collective-permute-start.13 = (f16[144,384]{1,0:T(8,128)(2,1)S(1)}, f16[144,384]{1,0:T(8,128)(2,1)}, u32[]{:S(2)}, u32[]{:S(2)}) collective-permute-start(f16[144,384]{1,0:T(8,128)(2,1)S(1)} %get-tuple-element.83), channel_id=1, source_target_pairs={{0,2},{1,3},{2,34},{3,35},{4,0},{5,1},{6,32},{7,33},{8,66},{9,67},... | collective-permute-start | bytes 331784 | tf_op jit(solution)/shard_map/ppermute | solution.py:47
  81.7 10.9 %collective-permute-start.11 = (f16[144,384]{1,0:T(8,128)(2,1)S(1)}, f16[144,384]{1,0:T(8,128)(2,1)}, u32[]{:S(2)}, u32[]{:S(2)}) collective-permute-start(f16[144,384]{1,0:T(8,128)(2,1)S(1)} %get-tuple-element.84), channel_id=1, source_target_pairs={{0,0},{1,1},{2,32},{3,33},{4,2},{5,3},{6,34},{7,35},{8,64},{9,65},... | collective-permute-start | bytes 331784 | tf_op jit(solution)/shard_map/ppermute | solution.py:47
  92.6 39.5 %collective-permute-start.20 = (bf16[2,256,384]{2,1,0:T(8,128)(2,1)S(1)}, bf16[2,256,384]{2,1,0:T(8,128)(2,1)S(1)}, u32[]{:S(2)}, u32[]{:S(2)}) collective-permute-start(bf16[2,256,384]{2,1,0:T(8,128)(2,1)S(1)} %bitcast.65), channel_id=1, source_target_pairs={{0,24},{1,25},{2,26},{3,27},{4,28},{5,29},{6,30},{7,31},{8,0},{9,1... | collective-permute-start | bytes 1179656 | tf_op jit(solution)/shard_map/ppermute | solution.py:47
  109.2 22.9 %collective-permute-start.19 = (bf16[2,256,384]{2,1,0:T(8,128)(2,1)S(1)}, bf16[2,256,384]{2,1,0:T(8,128)(2,1)S(1)}, u32[]{:S(2)}, u32[]{:S(2)}) collective-permute-start(bf16[2,256,384]{2,1,0:T(8,128)(2,1)S(1)} %bitcast.66), channel_id=1, source_target_pairs={{0,16},{1,17},{2,18},{3,19},{4,20},{5,21},{6,22},{7,23},{8,24},{9,... | collective-permute-start | bytes 1179656 | tf_op jit(solution)/shard_map/ppermute | solution.py:47
  109.2 22.9 %collective-permute-start.18 = (bf16[2,256,384]{2,1,0:T(8,128)(2,1)S(1)}, bf16[2,256,384]{2,1,0:T(8,128)(2,1)S(1)}, u32[]{:S(2)}, u32[]{:S(2)}) collective-permute-start(bf16[2,256,384]{2,1,0:T(8,128)(2,1)S(1)} %bitcast.67), channel_id=1, source_target_pairs={{0,8},{1,9},{2,10},{3,11},{4,12},{5,13},{6,14},{7,15},{8,16},{9,17... | collective-permute-start | bytes 1179656 | tf_op jit(solution)/shard_map/ppermute | solution.py:47
  113.2 18.9 %all-to-all-start.2 = ((f32[32,1,256]{2,1,0:T(1,128)}), f32[32,1,256]{2,1,0:T(1,128)S(1)}, u32[]{:S(2)}, u32[]{:S(2)}) async-start(f32[32,1,256]{2,1,0:T(1,128)} %broadcast_in_dim.50), calls=%async_computation.2 | async-start | bytes 65536 | tf_op jit(solution)/shard_map/all_to_all | solution.py:55
  122.4 3.0 %collective-permute-start.17 = (f32[2,384]{1,0:T(2,128)S(1)}, f32[2,384]{1,0:T(2,128)S(1)}, u32[]{:S(2)}, u32[]{:S(2)}) collective-permute-start(f32[2,384]{1,0:T(2,128)S(1)} %pad_maximum_fusion.6), channel_id=1, source_target_pairs={{0,192},{1,193},{2,194},{3,195},{4,196},{5,197},{6,198},{7,199},{8... | collective-permute-start | bytes 9224 | tf_op jit(solution)/shard_map/ppermute | solution.py:47
  124.7 7.4 %collective-permute-start.16 = (f32[2,384]{1,0:T(2,128)S(1)}, f32[2,384]{1,0:T(2,128)S(1)}, u32[]{:S(2)}, u32[]{:S(2)}) collective-permute-start(f32[2,384]{1,0:T(2,128)S(1)} %pad_maximum_fusion.6), channel_id=1, source_target_pairs={{0,128},{1,129},{2,130},{3,131},{4,132},{5,133},{6,134},{7,135},{8... | collective-permute-start | bytes 9224 | tf_op jit(solution)/shard_map/ppermute | solution.py:47
  125.4 6.7 %collective-permute-start.15 = (f32[2,384]{1,0:T(2,128)S(1)}, f32[2,384]{1,0:T(2,128)S(1)}, u32[]{:S(2)}, u32[]{:S(2)}) collective-permute-start(f32[2,384]{1,0:T(2,128)S(1)} %pad_maximum_fusion.6), channel_id=1, source_target_pairs={{0,64},{1,65},{2,66},{3,67},{4,68},{5,69},{6,70},{7,71},{8,72},{9,... | collective-permute-start | bytes 9224 | tf_op jit(solution)/shard_map/ppermute | solution.py:47
  134.8 5.0 %collective-permute-start.21 = (f32[2,384,384]{2,1,0:T(8,128)}, f32[2,384,384]{2,1,0:T(8,128)}, u32[]{:S(2)}, u32[]{:S(2)}) collective-permute-start(f32[2,384,384]{2,1,0:T(8,128)} %shard_map.84), channel_id=1, source_target_pairs={{0,1},{1,0},{2,3},{3,2},{4,5},{5,4},{6,7},{7,6},{8,9},{9,8},{10,11... | collective-permute-start | bytes 3538952 | tf_op jit(solution)/shard_map/ppermute | solution.py:47
  135.2 4.0 %collective-permute-start.22 = (f32[2,384]{1,0:T(2,128)S(1)}, f32[2,384]{1,0:T(2,128)S(1)}, u32[]{:S(2)}, u32[]{:S(2)}) collective-permute-start(f32[2,384]{1,0:T(2,128)S(1)} %add_add_fusion), channel_id=1, source_target_pairs={{0,32},{1,33},{2,34},{3,35},{4,36},{5,37},{6,38},{7,39},{8,40},{9,... | collective-permute-start | bytes 9224 | tf_op jit(solution)/shard_map/ppermute | solution.py:47
  (13 other events, 58.7 us)

commit v4 on v3

--- a/solution.py
+++ b/solution.py
@@ -25,21 +25,14 @@
     return pairs
 
 
-def to_owner(k):
-    def move(x, zl, y, zh, c):
-        s = (zh + k) % 4
-        return (y, s % 2, x, 2 * zl + s // 2, c)
-
-    return table(move)
-
-
 CORE = table(lambda x, zl, y, zh, c: (x, zl, y, zh, 1 - c))
 ALONG_X = [
     [table(lambda x, zl, y, zh, c, i=i, j=j: ((x + i) % 4, zl ^ j, y, zh, c)) for j in range(2)] for i in range(4)
 ]
 ALONG_Y = [table(lambda x, zl, y, zh, c, k=k: (x, zl, (y + k) % 4, zh, c)) for k in range(4)]
-OWNER = [to_owner(k) for k in range(4)]
+ALONG_Z = [table(lambda x, zl, y, zh, c, k=k: (x, zl, y, (zh + k) % 4, c)) for k in range(4)]
 HOLDER = table(lambda x, zl, y, zh, c: (y, zh // 2, x, 2 * (zh % 2) + zl, c))
+OWNER = [(b, a) for a, b in HOLDER]
 Z_GROUPS = [[8 * y + 2 * z + c for z in range(4)] for y in range(4) for c in range(2)]
 
 
@@ -181,29 +174,33 @@
             for i, message in enumerate(received)
         )
         pieces.append(jnp.concatenate([piece, power]).astype(jnp.float16))
-    pieces = [send(piece, OWNER[k]) for k, piece in enumerate(pieces)]
+    pieces = [send(piece, ALONG_Z[k]) if k else piece for k, piece in enumerate(pieces)]
 
     block = exchange(copies(normed, 4), "tensor", Z_GROUPS).reshape(2, 2 * tokens, width)
-    pieces, block = lax.optimization_barrier((pieces, block))
     blocks = [block] + [send(block, ALONG_Y[k]) for k in (1, 2, 3)]
 
-    scales = jnp.exp2(-jnp.stack([piece[tokens:] for piece in pieces]).astype(jnp.float32))
-    grad_normed = sum(piece[:tokens].astype(jnp.float32) * scales[i, :1] for i, piece in enumerate(pieces))
+    powers = jnp.stack([piece[tokens:] for piece in pieces]).astype(jnp.float32)
+    power = jnp.min(powers, axis=0) - 2.0
+    scales = jnp.exp2(power - powers)
+    piece = sum(piece[:tokens].astype(jnp.float32) * scales[i, :1] for i, piece in enumerate(pieces))
+    piece = send(jnp.concatenate([piece, power]).astype(jnp.float16), OWNER)
+    grad_normed = piece[:tokens].astype(jnp.float32) * jnp.exp2(-piece[tokens : tokens + 1].astype(jnp.float32))
 
     scaled = grad_normed * ln_gain
     told = jnp.concatenate([jnp.sum(scaled, axis=1), jnp.sum(scaled * standard, axis=1)])
     told = exchange(copies(told, TENSOR), "tensor")
     sums = jnp.stack([jnp.sum(grad_normed * standard, axis=0), jnp.sum(grad_normed, axis=0)])
     others = [send(sums, ALONG_X[i][0]) for i in (1, 2, 3)]
-    told, others, blocks = lax.optimization_barrier((told, others, blocks))
+    at = jnp.stack([(x - y + k) % 4 for k in range(4)] + [c]).astype(jnp.int32)
+    grad_other = weight_part(at, blocks, query_other)
+    grad_mine = weight_part(at, blocks, query, c)
+    told, others, grad_other, grad_mine = lax.optimization_barrier((told, others, grad_other, grad_mine))
+    grad_other = send(grad_other, CORE)
     sums = sums + others[0] + others[1] + others[2]
     sums = sums + send(sums, ALONG_X[0][1])
     told = jnp.sum(told, axis=0) / features
     grad_input = inv_std * (scaled - told[:tokens, None] - standard * told[tokens:, None])
 
-    at = jnp.stack([(x - y + k) % 4 for k in range(4)] + [c]).astype(jnp.int32)
-    grad_other = send(weight_part(at, blocks, query_other), CORE)
-    grad_mine = weight_part(at, blocks, query, c)
     grad_weight = fill((1 - c).astype(jnp.int32).reshape(1), grad_other, grad_mine).reshape(4 * width, width)
     return (grad_input, grad_weight, sums[0], sums[1])
 

time: 143 us -> 131 us (0.916)
  starting transfers between devices: 65.8 us -> 55 us
  waiting for transfers between devices: 45.8 us -> 47.7 us
  local copies, waits for them, and re-layouts: 8.19 us -> 6.74 us
    ppermute x23, starting transfers between devices: 41.3 us -> 23.2 us  [send(): return lax.ppermute(array, AXES, pairs)]
    all_to_all x3, starting transfers between devices: 24.5 us -> 31.8 us  [exchange(): lax.all_to_all(array, axis, split_axis=0, concat_axis=0, tiled=True, axis...]
    all_to_all x3, waiting for transfers between devices: 16.2 us -> 21.7 us  [exchange(): lax.all_to_all(array, axis, split_axis=0, concat_axis=0, tiled=True, axis...]
    ppermute x23, waiting for transfers between devices: 29.6 us -> 26 us  [send(): return lax.ppermute(array, AXES, pairs)]
  transfers between devices with their start and end apart: 26 -> 26, of which waited for: 8 -> 8; matrix products, arithmetic and copies ran while one was open for 11% -> 11% of each run, Pallas kernels for 2% -> 4%
where the time goes in v4:
time: 131 us
  starting transfers between devices  55 us (42%)
  waiting for transfers between devices  47.7 us (36%)
  local copies, waits for them, and re-layouts  6.74 us (5%)
  Pallas kernels  6.24 us (5%)
  other arithmetic  6.03 us (5%)
  matrix products  5.5 us (4%)
  between operations  3.4 us (3%)
    all_to_all x3, starting transfers between devices, exchange(): lax.all_to_all(array, axis, split_axis=0, concat_axis=0, tiled=True, axis...  31.8 us
    ppermute x23, waiting for transfers between devices, send(): return lax.ppermute(array, AXES, pairs)  26 us
    ppermute x23, starting transfers between devices, send(): return lax.ppermute(array, AXES, pairs)  23.2 us
    all_to_all x3, waiting for transfers between devices, exchange(): lax.all_to_all(array, axis, split_axis=0, concat_axis=0, tiled=True, axis...  21.7 us
    pallas_call x2, Pallas kernels, weight_part(): pl.pallas_call(weight_kernel, out_shape=out_shape, grid_spec=pltpu.Prefet...  5.19 us
    dot_general x4, matrix products, body(): lax.dot_general(longer(other_tokens[k]), theirs, ROWS_BY_ROWS, preferred_...  3.92 us
    another operation x2, other arithmetic  2.67 us
  transfers between devices with their start and end apart: 26, of which 8 were waited for; matrix products, arithmetic and copies ran while one was open for 11% of the time, Pallas kernels for 4%

profile of v4, /device:TPU:1, one launch (start us, length us, event | category | flops | bytes accessed | tf_op | source)
XLA Modules:
  0.0 130.6 jit_solution(15496070934517366791)
XLA Ops:
  0.6 2.6 %collective-permute-start = (bf16[128,384]{1,0:T(8,128)(2,1)}, bf16[128,384]{1,0:T(8,128)(2,1)S(1)}, u32[]{:S(2)}, u32[]{:S(2)}) collective-permute-start(bf16[128,384]{1,0:T(8,128)(2,1)} %param.9), channel_id=1, source_target_pairs={{0,32},{1,33},{2,34},{3,35},{4,36},{5,37},{6,38},{7,39},{8,40},{9,... | collective-permute-start | bytes 294920 | tf_op jit(solution)/shard_map/ppermute | solution.py:40
  3.2 2.3 %constant_dynamic-slice_fusion = (bf16[2,1,384,384]{3,2,1,0:T(8,128)(2,1)}, bf16[2,1,384,384]{3,2,1,0:T(8,128)(2,1)S(1)}) fusion(bf16[2,2,384,384]{3,2,1,0:T(8,128)(2,1)} %bitcast.74, s32[]{:T(128)S(6)} %select_n.214, s32[]{:T(128)S(6)} %select_n.213), kind=kLoop, calls=%fused_computation.92 | loop fusion | bytes 2359304 | tf_op jit(solution)/shard_map/jit(dynamic_index_in_dim)/dynamic_slice | solution.py:139
  7.5 2.6 %collective-permute-start.3 = (bf16[256,384]{1,0:T(8,128)(2,1)S(1)}, bf16[256,384]{1,0:T(8,128)(2,1)S(1)}, u32[]{:S(2)}, u32[]{:S(2)}) collective-permute-start(bf16[256,384]{1,0:T(8,128)(2,1)S(1)} %maximum_select_fusion.1), channel_id=1, source_target_pairs={{0,192},{1,193},{2,194},{3,195},{4,196},{5,197},{6,198},{7,199},{8... | collective-permute-start | bytes 589832 | tf_op jit(solution)/shard_map/ppermute | solution.py:40
  11.8 11.7 %all-to-all-start = ((f32[32,1,256]{2,1,0:T(1,128)}), f32[32,1,256]{2,1,0:T(1,128)S(1)}, u32[]{:S(2)}, u32[]{:S(2)}) async-start(f32[32,1,256]{2,1,0:T(1,128)} %broadcast_in_dim.25), calls=%async_computation | async-start | bytes 65536 | tf_op jit(solution)/shard_map/all_to_all | solution.py:48
  23.6 9.6 %all-to-all-done = f32[32,1,256]{2,1,0:T(1,128)S(1)} async-done(((f32[32,1,256]{2,1,0:T(1,128)}), f32[32,1,256]{2,1,0:T(1,128)S(1)}, u32[]{:S(2)}, u32[]{:S(2)}) %all-to-all-start) | async-done | bytes 32800 | tf_op jit(solution)/shard_map/all_to_all | solution.py:48
  42.7 1.2 collective-permute-start.7
  44.0 1.2 fusion.10
  46.5 5.3 %collective-permute-done.9 = f16[272,768]{1,0:T(8,128)(2,1)} collective-permute-done((f16[272,768]{1,0:T(8,128)(2,1)}, f16[272,768]{1,0:T(8,128)(2,1)}, u32[]{:S(2)}, u32[]{:S(2)}) %collective-permute-start.9) | collective-permute-done | bytes 417824 | tf_op jit(solution)/shard_map/ppermute | solution.py:40
  51.8 4.9 %collective-permute-done.7 = f16[272,768]{1,0:T(8,128)(2,1)} collective-permute-done((f16[272,768]{1,0:T(8,128)(2,1)}, f16[272,768]{1,0:T(8,128)(2,1)}, u32[]{:S(2)}, u32[]{:S(2)}) %collective-permute-start.7) | collective-permute-done | bytes 417824 | tf_op jit(solution)/shard_map/ppermute | solution.py:40
  56.7 9.1 %collective-permute-done.8 = f16[272,768]{1,0:T(8,128)(2,1)} collective-permute-done((f16[272,768]{1,0:T(8,128)(2,1)}, f16[272,768]{1,0:T(8,128)(2,1)}, u32[]{:S(2)}, u32[]{:S(2)}) %collective-permute-start.8) | collective-permute-done | bytes 417824 | tf_op jit(solution)/shard_map/ppermute | solution.py:40
  67.4 1.5 %add_convert_fusion.3 = (f16[128,384]{1,0:T(8,128)(2,1)S(1)}, f16[128,384]{1,0:T(8,128)(2,1)S(1)}, f16[128,384]{1,0:T(8,128)(2,1)S(1)}) fusion(f16[272,768]{1,0:T(8,128)(2,1)S(1)} %fusion.8, s32[]{:T(128)S(6)} %select_n.234, s32[]{:T(128)S(6)} %select_n.236, f16[272,768]{1,0:T(8,128)(2,1)} %collective-permute-done.9, ...), kind=kLoop, calls=%fused_computation.55 | loop fusion | flops 1769472 | bytes 1480728 | tf_op jit(solution)/shard_map/convert.6
  69.5 2.0 %collective-permute-start.12 = (f16[144,384]{1,0:T(8,128)(2,1)S(1)}, f16[144,384]{1,0:T(8,128)(2,1)S(1)}, u32[]{:S(2)}, u32[]{:S(2)}) collective-permute-start(f16[144,384]{1,0:T(8,128)(2,1)S(1)} %get-tuple-element.68), channel_id=1, source_target_pairs={{0,4},{1,5},{2,6},{3,7},{4,0},{5,1},{6,2},{7,3},{8,12},{9,13},{10,... | collective-permute-start | bytes 331784 | tf_op jit(solution)/shard_map/ppermute | solution.py:40
  71.6 1.6 %collective-permute-start.13 = (f16[144,384]{1,0:T(8,128)(2,1)S(1)}, f16[144,384]{1,0:T(8,128)(2,1)S(1)}, u32[]{:S(2)}, u32[]{:S(2)}) collective-permute-start(f16[144,384]{1,0:T(8,128)(2,1)S(1)} %get-tuple-element.69), channel_id=1, source_target_pairs={{0,6},{1,7},{2,0},{3,1},{4,2},{5,3},{6,4},{7,5},{8,14},{9,15},{10,... | collective-permute-start | bytes 331784 | tf_op jit(solution)/shard_map/ppermute | solution.py:40
  73.9 6.3 %all-to-all-start.2 = ((bf16[4,128,384]{2,1,0:T(8,128)(2,1)}), bf16[4,128,384]{2,1,0:T(8,128)(2,1)S(1)}, u32[]{:S(2)}, u32[]{:S(2)}) async-start(bf16[4,128,384]{2,1,0:T(8,128)(2,1)} %broadcast_in_dim.51), calls=%async_computation.2 | async-start | bytes 786432 | tf_op jit(solution)/shard_map/all_to_all | solution.py:48
  80.3 5.1 %collective-permute-done.13 = f16[144,384]{1,0:T(8,128)(2,1)S(1)} collective-permute-done((f16[144,384]{1,0:T(8,128)(2,1)S(1)}, f16[144,384]{1,0:T(8,128)(2,1)S(1)}, u32[]{:S(2)}, u32[]{:S(2)}) %collective-permute-start.13) | collective-permute-done | bytes 110624 | tf_op jit(solution)/shard_map/ppermute | solution.py:40
  87.5 3.7 %all-to-all-done.2 = bf16[4,128,384]{2,1,0:T(8,128)(2,1)S(1)} async-done(((bf16[4,128,384]{2,1,0:T(8,128)(2,1)}), bf16[4,128,384]{2,1,0:T(8,128)(2,1)S(1)}, u32[]{:S(2)}, u32[]{:S(2)}) %all-to-all-start.2) | async-done | bytes 393248 | tf_op jit(solution)/shard_map/all_to_all | solution.py:48
  91.1 3.1 %collective-permute-start.20 = (bf16[2,256,384]{2,1,0:T(8,128)(2,1)S(1)}, bf16[2,256,384]{2,1,0:T(8,128)(2,1)S(1)}, u32[]{:S(2)}, u32[]{:S(2)}) collective-permute-start(bf16[2,256,384]{2,1,0:T(8,128)(2,1)S(1)} %bitcast.64), channel_id=1, source_target_pairs={{0,24},{1,25},{2,26},{3,27},{4,28},{5,29},{6,30},{7,31},{8,0},{9,1... | collective-permute-start | bytes 1179656 | tf_op jit(solution)/shard_map/ppermute | solution.py:40
  94.3 1.2 collective-permute-start.19
  97.2 13.8 %all-to-all-start.1 = ((f32[32,1,256]{2,1,0:T(1,128)}), f32[32,1,256]{2,1,0:T(1,128)S(1)}, u32[]{:S(2)}, u32[]{:S(2)}) async-start(f32[32,1,256]{2,1,0:T(1,128)} %broadcast_in_dim.50), calls=%async_computation.1 | async-start | bytes 65536 | tf_op jit(solution)/shard_map/all_to_all | solution.py:48
  111.1 1.2 collective-permute-start.16
  112.3 8.4 %all-to-all-done.1 = f32[32,1,256]{2,1,0:T(1,128)S(1)} async-done(((f32[32,1,256]{2,1,0:T(1,128)}), f32[32,1,256]{2,1,0:T(1,128)S(1)}, u32[]{:S(2)}, u32[]{:S(2)}) %all-to-all-start.1) | async-done | bytes 32800 | tf_op jit(solution)/shard_map/all_to_all | solution.py:48
  120.7 2.6 %shard_map.84 = f32[2,384,384]{2,1,0:T(8,128)} custom-call(s32[5]{0:T(128)S(1)} %stack.92.at_ref, bf16[2,256,384]{2,1,0:T(8,128)(2,1)S(1)} %bitcast.67, bf16[2,256,384]{2,1,0:T(8,128)(2,1)S(1)} %collective-permute-done.18.second_ref, bf16[2,256,384]{2,1,0:T(8,128)(2,1)S(1)} %collective-permute-done.19.third_ref, ...), custom_call_target="tpu_custom_call" | custom-call | flops 603979776 | bytes 1572864 | tf_op jit(solution)/shard_map/pallas_call | solution.py:82
  123.3 2.6 %shard_map.85.whole_ref = f32[2,2,384,384]{3,2,1,0:T(8,128)} custom-call(s32[5]{0:T(128)S(1)} %stack.92.at_ref, bf16[2,256,384]{2,1,0:T(8,128)(2,1)S(1)} %bitcast.68, bf16[2,256,384]{2,1,0:T(8,128)(2,1)S(1)} %collective-permute-done.18.second_ref, bf16[2,256,384]{2,1,0:T(8,128)(2,1)S(1)} %collective-permute-done.19.third_ref, ...), custom_call_target="tpu_custom_call" | custom-call | flops 603979776 | bytes 1572864 | tf_op jit(solution)/shard_map/pallas_call | solution.py:82
  127.4 1.6 %collective-permute-done.22 = f32[2,384]{1,0:T(2,128)S(1)} collective-permute-done((f32[2,384]{1,0:T(2,128)S(1)}, f32[2,384]{1,0:T(2,128)S(1)}, u32[]{:S(2)}, u32[]{:S(2)}) %collective-permute-start.22) | collective-permute-done | bytes 3104 | tf_op jit(solution)/shard_map/ppermute | solution.py:40
  (100 shorter events, 22.2 us)
Async XLA Ops:
  0.6 6.8 %collective-permute-start = (bf16[128,384]{1,0:T(8,128)(2,1)}, bf16[128,384]{1,0:T(8,128)(2,1)S(1)}, u32[]{:S(2)}, u32[]{:S(2)}) collective-permute-start(bf16[128,384]{1,0:T(8,128)(2,1)} %param.9), channel_id=1, source_target_pairs={{0,32},{1,33},{2,34},{3,35},{4,36},{5,37},{6,38},{7,39},{8,40},{9,... | collective-permute-start | bytes 294920 | tf_op jit(solution)/shard_map/ppermute | solution.py:40
  5.5 34.0 %collective-permute-start.6 = (bf16[768,384]{1,0:T(8,128)(2,1)}, bf16[768,384]{1,0:T(8,128)(2,1)S(1)}, u32[]{:S(2)}, u32[]{:S(2)}) collective-permute-start(bf16[768,384]{1,0:T(8,128)(2,1)} %bitcast.11), channel_id=1, source_target_pairs={{0,1},{1,0},{2,3},{3,2},{4,5},{5,4},{6,7},{7,6},{8,9},{9,8},{10,11... | collective-permute-start | bytes 1769480 | tf_op jit(solution)/shard_map/ppermute | solution.py:40
  7.5 25.7 %collective-permute-start.3 = (bf16[256,384]{1,0:T(8,128)(2,1)S(1)}, bf16[256,384]{1,0:T(8,128)(2,1)S(1)}, u32[]{:S(2)}, u32[]{:S(2)}) collective-permute-start(bf16[256,384]{1,0:T(8,128)(2,1)S(1)} %maximum_select_fusion.1), channel_id=1, source_target_pairs={{0,192},{1,193},{2,194},{3,195},{4,196},{5,197},{6,198},{7,199},{8... | collective-permute-start | bytes 589832 | tf_op jit(solution)/shard_map/ppermute | solution.py:40
  10.0 23.2 %collective-permute-start.2 = (bf16[256,384]{1,0:T(8,128)(2,1)S(1)}, bf16[256,384]{1,0:T(8,128)(2,1)S(1)}, u32[]{:S(2)}, u32[]{:S(2)}) collective-permute-start(bf16[256,384]{1,0:T(8,128)(2,1)S(1)} %maximum_select_fusion.1), channel_id=1, source_target_pairs={{0,128},{1,129},{2,130},{3,131},{4,132},{5,133},{6,134},{7,135},{8... | collective-permute-start | bytes 589832 | tf_op jit(solution)/shard_map/ppermute | solution.py:40
  10.6 22.6 %collective-permute-start.1 = (bf16[256,384]{1,0:T(8,128)(2,1)S(1)}, bf16[256,384]{1,0:T(8,128)(2,1)S(1)}, u32[]{:S(2)}, u32[]{:S(2)}) collective-permute-start(bf16[256,384]{1,0:T(8,128)(2,1)S(1)} %maximum_select_fusion.1), channel_id=1, source_target_pairs={{0,64},{1,65},{2,66},{3,67},{4,68},{5,69},{6,70},{7,71},{8,72},{9,... | collective-permute-start | bytes 589832 | tf_op jit(solution)/shard_map/ppermute | solution.py:40
  11.8 21.4 %all-to-all-start = ((f32[32,1,256]{2,1,0:T(1,128)}), f32[32,1,256]{2,1,0:T(1,128)S(1)}, u32[]{:S(2)}, u32[]{:S(2)}) async-start(f32[32,1,256]{2,1,0:T(1,128)} %broadcast_in_dim.25), calls=%async_computation | async-start | bytes 65536 | tf_op jit(solution)/shard_map/all_to_all | solution.py:48
  34.0 5.3 %collective-permute-start.5 = (bf16[4,256,384]{2,1,0:T(8,128)(2,1)S(1)}, bf16[4,256,384]{2,1,0:T(8,128)(2,1)S(1)}, u32[]{:S(2)}, u32[]{:S(2)}) collective-permute-start(bf16[4,256,384]{2,1,0:T(8,128)(2,1)S(1)} %pad_maximum_fusion.columns_ref), channel_id=1, source_target_pairs={{0,1},{1,0},{2,3},{3,2},{4,5},{5,4},{6,7},{7,6},{8,9},{9,8},{10,11... | collective-permute-start | bytes 2359304 | tf_op jit(solution)/shard_map/ppermute | solution.py:40
  35.8 2.7 %collective-permute-start.4 = (f32[1,1]{1,0:T(1,128)}, f32[1,1]{1,0:T(1,128)}, u32[]{:S(2)}, u32[]{:S(2)}) collective-permute-start(f32[1,1]{1,0:T(1,128)} %bitcast.5), channel_id=1, source_target_pairs={{0,1},{1,0},{2,3},{3,2},{4,5},{5,4},{6,7},{7,6},{8,9},{9,8},{10,11... | collective-permute-start | bytes 20 | tf_op jit(solution)/shard_map/ppermute | solution.py:40
  40.7 11.1 %collective-permute-start.9 = (f16[272,768]{1,0:T(8,128)(2,1)}, f16[272,768]{1,0:T(8,128)(2,1)}, u32[]{:S(2)}, u32[]{:S(2)}) collective-permute-start(f16[272,768]{1,0:T(8,128)(2,1)} %fusion.9), channel_id=1, source_target_pairs={{0,24},{1,25},{2,26},{3,27},{4,28},{5,29},{6,30},{7,31},{8,0},{9,1... | collective-permute-start | bytes 1253384 | tf_op jit(solution)/shard_map/ppermute | solution.py:40
  42.7 14.0 %collective-permute-start.7 = (f16[272,768]{1,0:T(8,128)(2,1)}, f16[272,768]{1,0:T(8,128)(2,1)}, u32[]{:S(2)}, u32[]{:S(2)}) collective-permute-start(f16[272,768]{1,0:T(8,128)(2,1)} %fusion.11), channel_id=1, source_target_pairs={{0,16},{1,17},{2,18},{3,19},{4,20},{5,21},{6,22},{7,23},{8,24},{9,... | collective-permute-start | bytes 1253384 | tf_op jit(solution)/shard_map/ppermute | solution.py:40
  45.1 20.7 %collective-permute-start.8 = (f16[272,768]{1,0:T(8,128)(2,1)}, f16[272,768]{1,0:T(8,128)(2,1)}, u32[]{:S(2)}, u32[]{:S(2)}) collective-permute-start(f16[272,768]{1,0:T(8,128)(2,1)} %fusion.10), channel_id=1, source_target_pairs={{0,8},{1,9},{2,10},{3,11},{4,12},{5,13},{6,14},{7,15},{8,16},{9,17... | collective-permute-start | bytes 1253384 | tf_op jit(solution)/shard_map/ppermute | solution.py:40
  69.0 11.3 %collective-permute-start.11 = (f16[144,384]{1,0:T(8,128)(2,1)S(1)}, f16[144,384]{1,0:T(8,128)(2,1)S(1)}, u32[]{:S(2)}, u32[]{:S(2)}) collective-permute-start(f16[144,384]{1,0:T(8,128)(2,1)S(1)} %get-tuple-element.67), channel_id=1, source_target_pairs={{0,2},{1,3},{2,4},{3,5},{4,6},{5,7},{6,0},{7,1},{8,10},{9,11},{10,... | collective-permute-start | bytes 331784 | tf_op jit(solution)/shard_map/ppermute | solution.py:40
  69.5 10.7 %collective-permute-start.12 = (f16[144,384]{1,0:T(8,128)(2,1)S(1)}, f16[144,384]{1,0:T(8,128)(2,1)S(1)}, u32[]{:S(2)}, u32[]{:S(2)}) collective-permute-start(f16[144,384]{1,0:T(8,128)(2,1)S(1)} %get-tuple-element.68), channel_id=1, source_target_pairs={{0,4},{1,5},{2,6},{3,7},{4,0},{5,1},{6,2},{7,3},{8,12},{9,13},{10,... | collective-permute-start | bytes 331784 | tf_op jit(solution)/shard_map/ppermute | solution.py:40
  71.6 13.8 %collective-permute-start.13 = (f16[144,384]{1,0:T(8,128)(2,1)S(1)}, f16[144,384]{1,0:T(8,128)(2,1)S(1)}, u32[]{:S(2)}, u32[]{:S(2)}) collective-permute-start(f16[144,384]{1,0:T(8,128)(2,1)S(1)} %get-tuple-element.69), channel_id=1, source_target_pairs={{0,6},{1,7},{2,0},{3,1},{4,2},{5,3},{6,4},{7,5},{8,14},{9,15},{10,... | collective-permute-start | bytes 331784 | tf_op jit(solution)/shard_map/ppermute | solution.py:40
  73.9 17.2 %all-to-all-start.2 = ((bf16[4,128,384]{2,1,0:T(8,128)(2,1)}), bf16[4,128,384]{2,1,0:T(8,128)(2,1)S(1)}, u32[]{:S(2)}, u32[]{:S(2)}) async-start(bf16[4,128,384]{2,1,0:T(8,128)(2,1)} %broadcast_in_dim.51), calls=%async_computation.2 | async-start | bytes 786432 | tf_op jit(solution)/shard_map/all_to_all | solution.py:48
  86.7 9.6 %collective-permute-start.14 = (f16[144,384]{1,0:T(8,128)(2,1)S(1)}, f16[144,384]{1,0:T(8,128)(2,1)S(1)}, u32[]{:S(2)}, u32[]{:S(2)}) collective-permute-start(f16[144,384]{1,0:T(8,128)(2,1)S(1)} %pad_maximum_fusion.4), channel_id=1, source_target_pairs={{0,0},{1,1},{4,2},{5,3},{32,4},{33,5},{36,6},{37,7},{64,8},{65,9},... | collective-permute-start | bytes 331784 | tf_op jit(solution)/shard_map/ppermute | solution.py:40
  91.1 29.5 %collective-permute-start.20 = (bf16[2,256,384]{2,1,0:T(8,128)(2,1)S(1)}, bf16[2,256,384]{2,1,0:T(8,128)(2,1)S(1)}, u32[]{:S(2)}, u32[]{:S(2)}) collective-permute-start(bf16[2,256,384]{2,1,0:T(8,128)(2,1)S(1)} %bitcast.64), channel_id=1, source_target_pairs={{0,24},{1,25},{2,26},{3,27},{4,28},{5,29},{6,30},{7,31},{8,0},{9,1... | collective-permute-start | bytes 1179656 | tf_op jit(solution)/shard_map/ppermute | solution.py:40
  94.3 26.4 %collective-permute-start.19 = (bf16[2,256,384]{2,1,0:T(8,128)(2,1)S(1)}, bf16[2,256,384]{2,1,0:T(8,128)(2,1)S(1)}, u32[]{:S(2)}, u32[]{:S(2)}) collective-permute-start(bf16[2,256,384]{2,1,0:T(8,128)(2,1)S(1)} %bitcast.65), channel_id=1, source_target_pairs={{0,16},{1,17},{2,18},{3,19},{4,20},{5,21},{6,22},{7,23},{8,24},{9,... | collective-permute-start | bytes 1179656 | tf_op jit(solution)/shard_map/ppermute | solution.py:40
  95.4 25.2 %collective-permute-start.18 = (bf16[2,256,384]{2,1,0:T(8,128)(2,1)S(1)}, bf16[2,256,384]{2,1,0:T(8,128)(2,1)S(1)}, u32[]{:S(2)}, u32[]{:S(2)}) collective-permute-start(bf16[2,256,384]{2,1,0:T(8,128)(2,1)S(1)} %bitcast.66), channel_id=1, source_target_pairs={{0,8},{1,9},{2,10},{3,11},{4,12},{5,13},{6,14},{7,15},{8,16},{9,17... | collective-permute-start | bytes 1179656 | tf_op jit(solution)/shard_map/ppermute | solution.py:40
  97.2 23.5 %all-to-all-start.1 = ((f32[32,1,256]{2,1,0:T(1,128)}), f32[32,1,256]{2,1,0:T(1,128)S(1)}, u32[]{:S(2)}, u32[]{:S(2)}) async-start(f32[32,1,256]{2,1,0:T(1,128)} %broadcast_in_dim.50), calls=%async_computation.1 | async-start | bytes 65536 | tf_op jit(solution)/shard_map/all_to_all | solution.py:48
  111.0 14.9 %collective-permute-start.17 = (f32[2,384]{1,0:T(2,128)S(1)}, f32[2,384]{1,0:T(2,128)S(1)}, u32[]{:S(2)}, u32[]{:S(2)}) collective-permute-start(f32[2,384]{1,0:T(2,128)S(1)} %pad_maximum_fusion.7), channel_id=1, source_target_pairs={{0,192},{1,193},{2,194},{3,195},{4,196},{5,197},{6,198},{7,199},{8... | collective-permute-start | bytes 9224 | tf_op jit(solution)/shard_map/ppermute | solution.py:40
  111.1 14.8 %collective-permute-start.16 = (f32[2,384]{1,0:T(2,128)S(1)}, f32[2,384]{1,0:T(2,128)S(1)}, u32[]{:S(2)}, u32[]{:S(2)}) collective-permute-start(f32[2,384]{1,0:T(2,128)S(1)} %pad_maximum_fusion.7), channel_id=1, source_target_pairs={{0,128},{1,129},{2,130},{3,131},{4,132},{5,133},{6,134},{7,135},{8... | collective-permute-start | bytes 9224 | tf_op jit(solution)/shard_map/ppermute | solution.py:40
  120.6 5.2 %collective-permute-start.15 = (f32[2,384]{1,0:T(2,128)S(1)}, f32[2,384]{1,0:T(2,128)S(1)}, u32[]{:S(2)}, u32[]{:S(2)}) collective-permute-start(f32[2,384]{1,0:T(2,128)S(1)} %pad_maximum_fusion.7), channel_id=1, source_target_pairs={{0,64},{1,65},{2,66},{3,67},{4,68},{5,69},{6,70},{7,71},{8,72},{9,... | collective-permute-start | bytes 9224 | tf_op jit(solution)/shard_map/ppermute | solution.py:40
  125.9 3.7 %collective-permute-start.21 = (f32[2,384,384]{2,1,0:T(8,128)}, f32[2,384,384]{2,1,0:T(8,128)S(1)}, u32[]{:S(2)}, u32[]{:S(2)}) collective-permute-start(f32[2,384,384]{2,1,0:T(8,128)} %shard_map.84), channel_id=1, source_target_pairs={{0,1},{1,0},{2,3},{3,2},{4,5},{5,4},{6,7},{7,6},{8,9},{9,8},{10,11... | collective-permute-start | bytes 3538952 | tf_op jit(solution)/shard_map/ppermute | solution.py:40
  (7 other events, 15.3 us)

commit v5 on v4

--- a/solution.py
+++ b/solution.py
@@ -125,10 +125,9 @@
     query = jnp.stack([pair] + [send(pair, ALONG_X[i][0]) for i in (1, 2, 3)])
 
     values = hidden_in.astype(jnp.float32)
-    told = jnp.concatenate([jnp.sum(values, axis=1), jnp.sum(values * values, axis=1)])
+    told = jnp.concatenate([jnp.sum(values, axis=1), jnp.sum(values * values, axis=1)] * 4)
     told = exchange(copies(after(told, there), TENSOR), "tensor")
-    query, told = lax.optimization_barrier((query, told))
-    sums = jnp.sum(told, axis=0) / features
+    sums = jnp.sum(told[:, : 2 * tokens], axis=0) / features
     row_mean = sums[:tokens, None]
     inv_std = lax.rsqrt(sums[tokens:, None] - row_mean * row_mean + 1e-05)
     standard = (values - row_mean) * inv_std

time: 131 us -> 130 us (level)
  waiting for transfers between devices: 47.7 us -> 37.4 us
  starting transfers between devices: 55 us -> 60.6 us
  matrix products: 5.5 us -> 8.39 us
    all_to_all x3, waiting for transfers between devices: 21.7 us -> 13.4 us  [exchange(): lax.all_to_all(array, axis, split_axis=0, concat_axis=0, tiled=True, axis...]
    ppermute x23, starting transfers between devices: 23.2 us -> 28.7 us  [send(): return lax.ppermute(array, AXES, pairs)]
    dot_general x4, matrix products: 1.59 us -> 5.23 us  [body(): lax.dot_general(longer(own_tokens[k]), mine, ROWS_BY_ROWS, preferred_elem...]
    ppermute x23, waiting for transfers between devices: 26 us -> 24 us  [send(): return lax.ppermute(array, AXES, pairs)]
    another operation x3 -> x2, other arithmetic: 2.8 us -> 2.68 us
  transfers between devices with their start and end apart: 26 -> 26, of which waited for: 8 -> 8; matrix products, arithmetic and copies ran while one was open for 11% -> 13% of each run, Pallas kernels for 4% -> 4%
where the time goes in v5:
time: 130 us; the launch traced here: 129 us
  starting transfers between devices  60.6 us (47%)
  waiting for transfers between devices  37.4 us (29%)
  matrix products  8.39 us (6%)
  local copies, waits for them, and re-layouts  6.93 us (5%)
  Pallas kernels  6.27 us (5%)
  other arithmetic  5.9 us (5%)
  between operations  3.53 us (3%)
    all_to_all x3, starting transfers between devices, exchange(): lax.all_to_all(array, axis, split_axis=0, concat_axis=0, tiled=True, axis...  31.9 us
    ppermute x23, starting transfers between devices, send(): return lax.ppermute(array, AXES, pairs)  28.7 us
    ppermute x23, waiting for transfers between devices, send(): return lax.ppermute(array, AXES, pairs)  24 us
    all_to_all x3, waiting for transfers between devices, exchange(): lax.all_to_all(array, axis, split_axis=0, concat_axis=0, tiled=True, axis...  13.4 us
    dot_general x4, matrix products, body(): lax.dot_general(longer(own_tokens[k]), mine, ROWS_BY_ROWS, preferred_elem...  5.23 us
    pallas_call x2, Pallas kernels, weight_part(): pl.pallas_call(weight_kernel, out_shape=out_shape, grid_spec=pltpu.Prefet...  5.22 us
    dot_general x4, matrix products, body(): lax.dot_general(longer(other_tokens[k]), theirs, ROWS_BY_ROWS, preferred_...  3.16 us
    another operation x2, other arithmetic  2.68 us
  transfers between devices with their start and end apart: 26, of which 8 were waited for; matrix products, arithmetic and copies ran while one was open for 13% of the time, Pallas kernels for 4%

profile of v5, /device:TPU:1, one launch (start us, length us, event | category | flops | bytes accessed | tf_op | source)
XLA Modules:
  0.0 129.0 jit_solution(16312742675181986648)
XLA Ops:
  0.6 2.6 %collective-permute-start = (bf16[128,384]{1,0:T(8,128)(2,1)}, bf16[128,384]{1,0:T(8,128)(2,1)S(1)}, u32[]{:S(2)}, u32[]{:S(2)}) collective-permute-start(bf16[128,384]{1,0:T(8,128)(2,1)} %param.9), channel_id=1, source_target_pairs={{0,32},{1,33},{2,34},{3,35},{4,36},{5,37},{6,38},{7,39},{8,40},{9,... | collective-permute-start | bytes 294920 | tf_op jit(solution)/shard_map/ppermute | solution.py:40
  3.2 2.3 %constant_dynamic-slice_fusion = (bf16[2,1,384,384]{3,2,1,0:T(8,128)(2,1)}, bf16[2,1,384,384]{3,2,1,0:T(8,128)(2,1)S(1)}) fusion(bf16[2,2,384,384]{3,2,1,0:T(8,128)(2,1)} %bitcast.74, s32[]{:T(128)S(6)} %select_n.214, s32[]{:T(128)S(6)} %select_n.213), kind=kLoop, calls=%fused_computation.101 | loop fusion | bytes 2359304 | tf_op jit(solution)/shard_map/jit(dynamic_index_in_dim)/dynamic_slice | solution.py:138
  7.5 2.6 %collective-permute-start.3 = (bf16[256,384]{1,0:T(8,128)(2,1)S(1)}, bf16[256,384]{1,0:T(8,128)(2,1)S(1)}, u32[]{:S(2)}, u32[]{:S(2)}) collective-permute-start(bf16[256,384]{1,0:T(8,128)(2,1)S(1)} %maximum_select_fusion.1), channel_id=1, source_target_pairs={{0,192},{1,193},{2,194},{3,195},{4,196},{5,197},{6,198},{7,199},{8... | collective-permute-start | bytes 589832 | tf_op jit(solution)/shard_map/ppermute | solution.py:40
  11.9 11.7 %all-to-all-start = ((f32[32,1,1024]{2,1,0:T(1,128)}), f32[32,1,1024]{2,1,0:T(1,128)S(1)}, u32[]{:S(2)}, u32[]{:S(2)}) async-start(f32[32,1,1024]{2,1,0:T(1,128)} %broadcast_in_dim.25), calls=%async_computation | async-start | bytes 262144 | tf_op jit(solution)/shard_map/all_to_all | solution.py:48
  27.3 1.3 %fusion.13 = f32[272,768]{1,0:T(8,128)} fusion(bf16[768,384]{1,0:T(8,128)(2,1)S(1)} %bitcast.69, bf16[256,384]{1,0:T(8,128)(2,1)S(1)} %get-tuple-element.57), kind=kOutput, calls=%fused_computation.23 | convolution fusion | flops 160432128 | bytes 1622016 | tf_op jit(solution)/shard_map/dot_general | solution.py:154
  29.9 1.3 %fusion.19 = f32[272,768]{1,0:T(8,128)} fusion(bf16[768,384]{1,0:T(8,128)(2,1)S(1)} %bitcast.71, bf16[256,384]{1,0:T(8,128)(2,1)S(1)} %get-tuple-element.59), kind=kOutput, calls=%fused_computation.29 | convolution fusion | flops 160432128 | bytes 1622016 | tf_op jit(solution)/shard_map/dot_general | solution.py:154
  31.2 1.3 %fusion.22 = f32[272,768]{1,0:T(8,128)} fusion(bf16[768,384]{1,0:T(8,128)(2,1)S(1)} %bitcast.72, bf16[256,384]{1,0:T(8,128)(2,1)S(1)} %get-tuple-element.60), kind=kOutput, calls=%fused_computation.32 | convolution fusion | flops 160432128 | bytes 1622016 | tf_op jit(solution)/shard_map/dot_general | solution.py:154
  36.0 1.5 %collective-permute-start.9 = (f16[272,768]{1,0:T(8,128)(2,1)}, f16[272,768]{1,0:T(8,128)(2,1)}, u32[]{:S(2)}, u32[]{:S(2)}) collective-permute-start(f16[272,768]{1,0:T(8,128)(2,1)} %fusion.9), channel_id=1, source_target_pairs={{0,24},{1,25},{2,26},{3,27},{4,28},{5,29},{6,30},{7,31},{8,0},{9,1... | collective-permute-start | bytes 1253384 | tf_op jit(solution)/shard_map/ppermute | solution.py:40
  41.7 5.7 %collective-permute-done.9 = f16[272,768]{1,0:T(8,128)(2,1)} collective-permute-done((f16[272,768]{1,0:T(8,128)(2,1)}, f16[272,768]{1,0:T(8,128)(2,1)}, u32[]{:S(2)}, u32[]{:S(2)}) %collective-permute-start.9) | collective-permute-done | bytes 417824 | tf_op jit(solution)/shard_map/ppermute | solution.py:40
  47.4 4.0 %collective-permute-done.7 = f16[272,768]{1,0:T(8,128)(2,1)} collective-permute-done((f16[272,768]{1,0:T(8,128)(2,1)S(1)}, f16[272,768]{1,0:T(8,128)(2,1)}, u32[]{:S(2)}, u32[]{:S(2)}) %collective-permute-start.7) | collective-permute-done | bytes 417824 | tf_op jit(solution)/shard_map/ppermute | solution.py:40
  51.4 9.1 %collective-permute-done.8 = f16[272,768]{1,0:T(8,128)(2,1)} collective-permute-done((f16[272,768]{1,0:T(8,128)(2,1)}, f16[272,768]{1,0:T(8,128)(2,1)}, u32[]{:S(2)}, u32[]{:S(2)}) %collective-permute-start.8) | collective-permute-done | bytes 417824 | tf_op jit(solution)/shard_map/ppermute | solution.py:40
  62.0 1.5 %add_convert_fusion.3 = (f16[128,384]{1,0:T(8,128)(2,1)S(1)}, f16[128,384]{1,0:T(8,128)(2,1)S(1)}, f16[128,384]{1,0:T(8,128)(2,1)S(1)}) fusion(f16[272,768]{1,0:T(8,128)(2,1)S(1)} %fusion.8, s32[]{:T(128)S(6)} %select_n.234, s32[]{:T(128)S(6)} %select_n.236, f16[272,768]{1,0:T(8,128)(2,1)} %collective-permute-done.9, ...), kind=kLoop, calls=%fused_computation.55 | loop fusion | flops 1769472 | bytes 1480728 | tf_op jit(solution)/shard_map/convert.6
  63.6 2.1 %collective-permute-start.11 = (f16[144,384]{1,0:T(8,128)(2,1)S(1)}, f16[144,384]{1,0:T(8,128)(2,1)S(1)}, u32[]{:S(2)}, u32[]{:S(2)}) collective-permute-start(f16[144,384]{1,0:T(8,128)(2,1)S(1)} %get-tuple-element.65), channel_id=1, source_target_pairs={{0,2},{1,3},{2,4},{3,5},{4,6},{5,7},{6,0},{7,1},{8,10},{9,11},{10,... | collective-permute-start | bytes 331784 | tf_op jit(solution)/shard_map/ppermute | solution.py:40
  65.7 4.0 %collective-permute-start.12 = (f16[144,384]{1,0:T(8,128)(2,1)S(1)}, f16[144,384]{1,0:T(8,128)(2,1)S(1)}, u32[]{:S(2)}, u32[]{:S(2)}) collective-permute-start(f16[144,384]{1,0:T(8,128)(2,1)S(1)} %get-tuple-element.66), channel_id=1, source_target_pairs={{0,4},{1,5},{2,6},{3,7},{4,0},{5,1},{6,2},{7,3},{8,12},{9,13},{10,... | collective-permute-start | bytes 331784 | tf_op jit(solution)/shard_map/ppermute | solution.py:40
  69.8 2.5 %collective-permute-start.13 = (f16[144,384]{1,0:T(8,128)(2,1)S(1)}, f16[144,384]{1,0:T(8,128)(2,1)S(1)}, u32[]{:S(2)}, u32[]{:S(2)}) collective-permute-start(f16[144,384]{1,0:T(8,128)(2,1)S(1)} %get-tuple-element.67), channel_id=1, source_target_pairs={{0,6},{1,7},{2,0},{3,1},{4,2},{5,3},{6,4},{7,5},{8,14},{9,15},{10,... | collective-permute-start | bytes 331784 | tf_op jit(solution)/shard_map/ppermute | solution.py:40
  73.1 3.5 %all-to-all-start.2 = ((bf16[4,128,384]{2,1,0:T(8,128)(2,1)}), bf16[4,128,384]{2,1,0:T(8,128)(2,1)S(1)}, u32[]{:S(2)}, u32[]{:S(2)}) async-start(bf16[4,128,384]{2,1,0:T(8,128)(2,1)} %broadcast_in_dim.51), calls=%async_computation.2 | async-start | bytes 786432 | tf_op jit(solution)/shard_map/all_to_all | solution.py:48
  76.6 3.6 %collective-permute-done.13 = f16[144,384]{1,0:T(8,128)(2,1)S(1)} collective-permute-done((f16[144,384]{1,0:T(8,128)(2,1)S(1)}, f16[144,384]{1,0:T(8,128)(2,1)S(1)}, u32[]{:S(2)}, u32[]{:S(2)}) %collective-permute-start.13) | collective-permute-done | bytes 110624 | tf_op jit(solution)/shard_map/ppermute | solution.py:40
  82.3 4.7 %all-to-all-done.2 = bf16[4,128,384]{2,1,0:T(8,128)(2,1)S(1)} async-done(((bf16[4,128,384]{2,1,0:T(8,128)(2,1)}), bf16[4,128,384]{2,1,0:T(8,128)(2,1)S(1)}, u32[]{:S(2)}, u32[]{:S(2)}) %all-to-all-start.2) | async-done | bytes 393248 | tf_op jit(solution)/shard_map/all_to_all | solution.py:48
  87.1 3.3 %collective-permute-start.20 = (bf16[2,256,384]{2,1,0:T(8,128)(2,1)S(1)}, bf16[2,256,384]{2,1,0:T(8,128)(2,1)S(1)}, u32[]{:S(2)}, u32[]{:S(2)}) collective-permute-start(bf16[2,256,384]{2,1,0:T(8,128)(2,1)S(1)} %bitcast.64), channel_id=1, source_target_pairs={{0,24},{1,25},{2,26},{3,27},{4,28},{5,29},{6,30},{7,31},{8,0},{9,1... | collective-permute-start | bytes 1179656 | tf_op jit(solution)/shard_map/ppermute | solution.py:40
  92.0 16.7 %all-to-all-start.1 = ((f32[32,1,256]{2,1,0:T(1,128)}), f32[32,1,256]{2,1,0:T(1,128)S(1)}, u32[]{:S(2)}, u32[]{:S(2)}) async-start(f32[32,1,256]{2,1,0:T(1,128)} %broadcast_in_dim.50), calls=%async_computation.1 | async-start | bytes 65536 | tf_op jit(solution)/shard_map/all_to_all | solution.py:48
  111.0 7.5 %all-to-all-done.1 = f32[32,1,256]{2,1,0:T(1,128)S(1)} async-done(((f32[32,1,256]{2,1,0:T(1,128)}), f32[32,1,256]{2,1,0:T(1,128)S(1)}, u32[]{:S(2)}, u32[]{:S(2)}) %all-to-all-start.1) | async-done | bytes 32800 | tf_op jit(solution)/shard_map/all_to_all | solution.py:48
  118.8 2.6 %shard_map.84 = f32[2,384,384]{2,1,0:T(8,128)} custom-call(s32[5]{0:T(128)S(1)} %stack.92.at_ref, bf16[2,256,384]{2,1,0:T(8,128)(2,1)S(1)} %bitcast.67, bf16[2,256,384]{2,1,0:T(8,128)(2,1)S(1)} %collective-permute-done.18.second_ref, bf16[2,256,384]{2,1,0:T(8,128)(2,1)S(1)} %collective-permute-done.19.third_ref, ...), custom_call_target="tpu_custom_call" | custom-call | flops 603979776 | bytes 1572864 | tf_op jit(solution)/shard_map/pallas_call | solution.py:82
  121.4 2.6 %shard_map.85.whole_ref = f32[2,2,384,384]{3,2,1,0:T(8,128)} custom-call(s32[5]{0:T(128)S(1)} %stack.92.at_ref, bf16[2,256,384]{2,1,0:T(8,128)(2,1)S(1)} %bitcast.68, bf16[2,256,384]{2,1,0:T(8,128)(2,1)S(1)} %collective-permute-done.18.second_ref, bf16[2,256,384]{2,1,0:T(8,128)(2,1)S(1)} %collective-permute-done.19.third_ref, ...), custom_call_target="tpu_custom_call" | custom-call | flops 603979776 | bytes 1572864 | tf_op jit(solution)/shard_map/pallas_call | solution.py:82
  125.7 1.6 %collective-permute-done.22 = f32[2,384]{1,0:T(2,128)S(1)} collective-permute-done((f32[2,384]{1,0:T(2,128)S(1)}, f32[2,384]{1,0:T(2,128)S(1)}, u32[]{:S(2)}, u32[]{:S(2)}) %collective-permute-start.22) | collective-permute-done | bytes 3104 | tf_op jit(solution)/shard_map/ppermute | solution.py:40
  (115 shorter events, 26.0 us)
Async XLA Ops:
  0.6 6.8 %collective-permute-start = (bf16[128,384]{1,0:T(8,128)(2,1)}, bf16[128,384]{1,0:T(8,128)(2,1)S(1)}, u32[]{:S(2)}, u32[]{:S(2)}) collective-permute-start(bf16[128,384]{1,0:T(8,128)(2,1)} %param.9), channel_id=1, source_target_pairs={{0,32},{1,33},{2,34},{3,35},{4,36},{5,37},{6,38},{7,39},{8,40},{9,... | collective-permute-start | bytes 294920 | tf_op jit(solution)/shard_map/ppermute | solution.py:40
  5.5 29.3 %collective-permute-start.6 = (bf16[768,384]{1,0:T(8,128)(2,1)}, bf16[768,384]{1,0:T(8,128)(2,1)S(1)}, u32[]{:S(2)}, u32[]{:S(2)}) collective-permute-start(bf16[768,384]{1,0:T(8,128)(2,1)} %bitcast.11), channel_id=1, source_target_pairs={{0,1},{1,0},{2,3},{3,2},{4,5},{5,4},{6,7},{7,6},{8,9},{9,8},{10,11... | collective-permute-start | bytes 1769480 | tf_op jit(solution)/shard_map/ppermute | solution.py:40
  7.5 16.2 %collective-permute-start.3 = (bf16[256,384]{1,0:T(8,128)(2,1)S(1)}, bf16[256,384]{1,0:T(8,128)(2,1)S(1)}, u32[]{:S(2)}, u32[]{:S(2)}) collective-permute-start(bf16[256,384]{1,0:T(8,128)(2,1)S(1)} %maximum_select_fusion.1), channel_id=1, source_target_pairs={{0,192},{1,193},{2,194},{3,195},{4,196},{5,197},{6,198},{7,199},{8... | collective-permute-start | bytes 589832 | tf_op jit(solution)/shard_map/ppermute | solution.py:40
  10.1 13.6 %collective-permute-start.2 = (bf16[256,384]{1,0:T(8,128)(2,1)S(1)}, bf16[256,384]{1,0:T(8,128)(2,1)S(1)}, u32[]{:S(2)}, u32[]{:S(2)}) collective-permute-start(bf16[256,384]{1,0:T(8,128)(2,1)S(1)} %maximum_select_fusion.1), channel_id=1, source_target_pairs={{0,128},{1,129},{2,130},{3,131},{4,132},{5,133},{6,134},{7,135},{8... | collective-permute-start | bytes 589832 | tf_op jit(solution)/shard_map/ppermute | solution.py:40
  10.6 13.1 %collective-permute-start.1 = (bf16[256,384]{1,0:T(8,128)(2,1)S(1)}, bf16[256,384]{1,0:T(8,128)(2,1)S(1)}, u32[]{:S(2)}, u32[]{:S(2)}) collective-permute-start(bf16[256,384]{1,0:T(8,128)(2,1)S(1)} %maximum_select_fusion.1), channel_id=1, source_target_pairs={{0,64},{1,65},{2,66},{3,67},{4,68},{5,69},{6,70},{7,71},{8,72},{9,... | collective-permute-start | bytes 589832 | tf_op jit(solution)/shard_map/ppermute | solution.py:40
  11.9 22.7 %all-to-all-start = ((f32[32,1,1024]{2,1,0:T(1,128)}), f32[32,1,1024]{2,1,0:T(1,128)S(1)}, u32[]{:S(2)}, u32[]{:S(2)}) async-start(f32[32,1,1024]{2,1,0:T(1,128)} %broadcast_in_dim.25), calls=%async_computation | async-start | bytes 262144 | tf_op jit(solution)/shard_map/all_to_all | solution.py:48
  25.8 6.7 %collective-permute-start.4 = (f32[1,1]{1,0:T(1,128)}, f32[1,1]{1,0:T(1,128)}, u32[]{:S(2)}, u32[]{:S(2)}) collective-permute-start(f32[1,1]{1,0:T(1,128)} %bitcast.5), channel_id=1, source_target_pairs={{0,1},{1,0},{2,3},{3,2},{4,5},{5,4},{6,7},{7,6},{8,9},{9,8},{10,11... | collective-permute-start | bytes 20 | tf_op jit(solution)/shard_map/ppermute | solution.py:40
  26.9 7.8 %collective-permute-start.5 = (bf16[4,256,384]{2,1,0:T(8,128)(2,1)S(1)}, bf16[4,256,384]{2,1,0:T(8,128)(2,1)S(1)}, u32[]{:S(2)}, u32[]{:S(2)}) collective-permute-start(bf16[4,256,384]{2,1,0:T(8,128)(2,1)S(1)} %get-tuple-element.47.columns_ref), channel_id=1, source_target_pairs={{0,1},{1,0},{2,3},{3,2},{4,5},{5,4},{6,7},{7,6},{8,9},{9,8},{10,11... | collective-permute-start | bytes 2359304 | tf_op jit(solution)/shard_map/ppermute | solution.py:40
  36.0 11.4 %collective-permute-start.9 = (f16[272,768]{1,0:T(8,128)(2,1)}, f16[272,768]{1,0:T(8,128)(2,1)}, u32[]{:S(2)}, u32[]{:S(2)}) collective-permute-start(f16[272,768]{1,0:T(8,128)(2,1)} %fusion.9), channel_id=1, source_target_pairs={{0,24},{1,25},{2,26},{3,27},{4,28},{5,29},{6,30},{7,31},{8,0},{9,1... | collective-permute-start | bytes 1253384 | tf_op jit(solution)/shard_map/ppermute | solution.py:40
  37.9 13.5 %collective-permute-start.7 = (f16[272,768]{1,0:T(8,128)(2,1)S(1)}, f16[272,768]{1,0:T(8,128)(2,1)}, u32[]{:S(2)}, u32[]{:S(2)}) collective-permute-start(f16[272,768]{1,0:T(8,128)(2,1)S(1)} %fusion.11), channel_id=1, source_target_pairs={{0,16},{1,17},{2,18},{3,19},{4,20},{5,21},{6,22},{7,23},{8,24},{9,... | collective-permute-start | bytes 1253384 | tf_op jit(solution)/shard_map/ppermute | solution.py:40
  39.8 20.6 %collective-permute-start.8 = (f16[272,768]{1,0:T(8,128)(2,1)}, f16[272,768]{1,0:T(8,128)(2,1)}, u32[]{:S(2)}, u32[]{:S(2)}) collective-permute-start(f16[272,768]{1,0:T(8,128)(2,1)} %fusion.10), channel_id=1, source_target_pairs={{0,8},{1,9},{2,10},{3,11},{4,12},{5,13},{6,14},{7,15},{8,16},{9,17... | collective-permute-start | bytes 1253384 | tf_op jit(solution)/shard_map/ppermute | solution.py:40
  63.6 12.9 %collective-permute-start.11 = (f16[144,384]{1,0:T(8,128)(2,1)S(1)}, f16[144,384]{1,0:T(8,128)(2,1)S(1)}, u32[]{:S(2)}, u32[]{:S(2)}) collective-permute-start(f16[144,384]{1,0:T(8,128)(2,1)S(1)} %get-tuple-element.65), channel_id=1, source_target_pairs={{0,2},{1,3},{2,4},{3,5},{4,6},{5,7},{6,0},{7,1},{8,10},{9,11},{10,... | collective-permute-start | bytes 331784 | tf_op jit(solution)/shard_map/ppermute | solution.py:40
  65.7 10.8 %collective-permute-start.12 = (f16[144,384]{1,0:T(8,128)(2,1)S(1)}, f16[144,384]{1,0:T(8,128)(2,1)S(1)}, u32[]{:S(2)}, u32[]{:S(2)}) collective-permute-start(f16[144,384]{1,0:T(8,128)(2,1)S(1)} %get-tuple-element.66), channel_id=1, source_target_pairs={{0,4},{1,5},{2,6},{3,7},{4,0},{5,1},{6,2},{7,3},{8,12},{9,13},{10,... | collective-permute-start | bytes 331784 | tf_op jit(solution)/shard_map/ppermute | solution.py:40
  69.8 10.5 %collective-permute-start.13 = (f16[144,384]{1,0:T(8,128)(2,1)S(1)}, f16[144,384]{1,0:T(8,128)(2,1)S(1)}, u32[]{:S(2)}, u32[]{:S(2)}) collective-permute-start(f16[144,384]{1,0:T(8,128)(2,1)S(1)} %get-tuple-element.67), channel_id=1, source_target_pairs={{0,6},{1,7},{2,0},{3,1},{4,2},{5,3},{6,4},{7,5},{8,14},{9,15},{10,... | collective-permute-start | bytes 331784 | tf_op jit(solution)/shard_map/ppermute | solution.py:40
  73.1 14.0 %all-to-all-start.2 = ((bf16[4,128,384]{2,1,0:T(8,128)(2,1)}), bf16[4,128,384]{2,1,0:T(8,128)(2,1)S(1)}, u32[]{:S(2)}, u32[]{:S(2)}) async-start(bf16[4,128,384]{2,1,0:T(8,128)(2,1)} %broadcast_in_dim.51), calls=%async_computation.2 | async-start | bytes 786432 | tf_op jit(solution)/shard_map/all_to_all | solution.py:48
  81.5 9.6 %collective-permute-start.14 = (f16[144,384]{1,0:T(8,128)(2,1)S(1)}, f16[144,384]{1,0:T(8,128)(2,1)S(1)}, u32[]{:S(2)}, u32[]{:S(2)}) collective-permute-start(f16[144,384]{1,0:T(8,128)(2,1)S(1)} %pad_maximum_fusion.4), channel_id=1, source_target_pairs={{0,0},{1,1},{4,2},{5,3},{32,4},{33,5},{36,6},{37,7},{64,8},{65,9},... | collective-permute-start | bytes 331784 | tf_op jit(solution)/shard_map/ppermute | solution.py:40
  87.1 31.4 %collective-permute-start.20 = (bf16[2,256,384]{2,1,0:T(8,128)(2,1)S(1)}, bf16[2,256,384]{2,1,0:T(8,128)(2,1)S(1)}, u32[]{:S(2)}, u32[]{:S(2)}) collective-permute-start(bf16[2,256,384]{2,1,0:T(8,128)(2,1)S(1)} %bitcast.64), channel_id=1, source_target_pairs={{0,24},{1,25},{2,26},{3,27},{4,28},{5,29},{6,30},{7,31},{8,0},{9,1... | collective-permute-start | bytes 1179656 | tf_op jit(solution)/shard_map/ppermute | solution.py:40
  90.3 28.5 %collective-permute-start.19 = (bf16[2,256,384]{2,1,0:T(8,128)(2,1)S(1)}, bf16[2,256,384]{2,1,0:T(8,128)(2,1)S(1)}, u32[]{:S(2)}, u32[]{:S(2)}) collective-permute-start(bf16[2,256,384]{2,1,0:T(8,128)(2,1)S(1)} %bitcast.65), channel_id=1, source_target_pairs={{0,16},{1,17},{2,18},{3,19},{4,20},{5,21},{6,22},{7,23},{8,24},{9,... | collective-permute-start | bytes 1179656 | tf_op jit(solution)/shard_map/ppermute | solution.py:40
  90.7 28.1 %collective-permute-start.18 = (bf16[2,256,384]{2,1,0:T(8,128)(2,1)S(1)}, bf16[2,256,384]{2,1,0:T(8,128)(2,1)S(1)}, u32[]{:S(2)}, u32[]{:S(2)}) collective-permute-start(bf16[2,256,384]{2,1,0:T(8,128)(2,1)S(1)} %bitcast.66), channel_id=1, source_target_pairs={{0,8},{1,9},{2,10},{3,11},{4,12},{5,13},{6,14},{7,15},{8,16},{9,17... | collective-permute-start | bytes 1179656 | tf_op jit(solution)/shard_map/ppermute | solution.py:40
  92.0 26.4 %all-to-all-start.1 = ((f32[32,1,256]{2,1,0:T(1,128)}), f32[32,1,256]{2,1,0:T(1,128)S(1)}, u32[]{:S(2)}, u32[]{:S(2)}) async-start(f32[32,1,256]{2,1,0:T(1,128)} %broadcast_in_dim.50), calls=%async_computation.1 | async-start | bytes 65536 | tf_op jit(solution)/shard_map/all_to_all | solution.py:48
  108.8 15.2 %collective-permute-start.17 = (f32[2,384]{1,0:T(2,128)S(1)}, f32[2,384]{1,0:T(2,128)S(1)}, u32[]{:S(2)}, u32[]{:S(2)}) collective-permute-start(f32[2,384]{1,0:T(2,128)S(1)} %pad_maximum_fusion.7), channel_id=1, source_target_pairs={{0,192},{1,193},{2,194},{3,195},{4,196},{5,197},{6,198},{7,199},{8... | collective-permute-start | bytes 9224 | tf_op jit(solution)/shard_map/ppermute | solution.py:40
  110.0 14.0 %collective-permute-start.16 = (f32[2,384]{1,0:T(2,128)S(1)}, f32[2,384]{1,0:T(2,128)S(1)}, u32[]{:S(2)}, u32[]{:S(2)}) collective-permute-start(f32[2,384]{1,0:T(2,128)S(1)} %pad_maximum_fusion.7), channel_id=1, source_target_pairs={{0,128},{1,129},{2,130},{3,131},{4,132},{5,133},{6,134},{7,135},{8... | collective-permute-start | bytes 9224 | tf_op jit(solution)/shard_map/ppermute | solution.py:40
  118.5 5.5 %collective-permute-start.15 = (f32[2,384]{1,0:T(2,128)S(1)}, f32[2,384]{1,0:T(2,128)S(1)}, u32[]{:S(2)}, u32[]{:S(2)}) collective-permute-start(f32[2,384]{1,0:T(2,128)S(1)} %pad_maximum_fusion.7), channel_id=1, source_target_pairs={{0,64},{1,65},{2,66},{3,67},{4,68},{5,69},{6,70},{7,71},{8,72},{9,... | collective-permute-start | bytes 9224 | tf_op jit(solution)/shard_map/ppermute | solution.py:40
  124.0 3.9 %collective-permute-start.21 = (f32[2,384,384]{2,1,0:T(8,128)}, f32[2,384,384]{2,1,0:T(8,128)S(1)}, u32[]{:S(2)}, u32[]{:S(2)}) collective-permute-start(f32[2,384,384]{2,1,0:T(8,128)} %shard_map.84), channel_id=1, source_target_pairs={{0,1},{1,0},{2,3},{3,2},{4,5},{5,4},{6,7},{7,6},{8,9},{9,8},{10,11... | collective-permute-start | bytes 3538952 | tf_op jit(solution)/shard_map/ppermute | solution.py:40
  (11 other events, 25.3 us)

commit v6 on v5

--- a/solution.py
+++ b/solution.py
@@ -150,7 +150,7 @@
     last = lax.broadcasted_iota(jnp.int32, (extended, 2 * width), 0) >= 2 * tokens
     longer = lambda array: jnp.pad(array, ((0, 16), (0, 0)))
     sent, received = [], []
-    for k in (2, 1, 3, 0):
+    for k in (1, 3, 2, 0):
         part = lax.dot_general(
             longer(own_tokens[k]), mine, ROWS_BY_ROWS, preferred_element_type=jnp.float32
         ) + lax.dot_general(longer(other_tokens[k]), theirs, ROWS_BY_ROWS, preferred_element_type=jnp.float32)

time: 130 us -> 129 us (level)
  waiting for transfers between devices: 37.4 us -> 34 us
  starting transfers between devices: 60.6 us -> 63.4 us
    ppermute x23, starting transfers between devices: 28.7 us -> 32.5 us  [send(): return lax.ppermute(array, AXES, pairs)]
    ppermute x23, waiting for transfers between devices: 24 us -> 21.8 us  [send(): return lax.ppermute(array, AXES, pairs)]
  transfers between devices with their start and end apart: 26 -> 26, of which waited for: 8 -> 7; matrix products, arithmetic and copies ran while one was open for 13% -> 13% of each run, Pallas kernels for 4% -> 4%
where the time goes in v6:
time: 129 us; the launch traced here: 128 us
  starting transfers between devices  63.4 us (49%)
  waiting for transfers between devices  34 us (26%)
  matrix products  8.39 us (7%)
  local copies, waits for them, and re-layouts  6.94 us (5%)
  Pallas kernels  6.27 us (5%)
  other arithmetic  5.9 us (5%)
  between operations  3.51 us (3%)
    ppermute x23, starting transfers between devices, send(): return lax.ppermute(array, AXES, pairs)  32.5 us
    all_to_all x3, starting transfers between devices, exchange(): lax.all_to_all(array, axis, split_axis=0, concat_axis=0, tiled=True, axis...  30.9 us
    ppermute x23, waiting for transfers between devices, send(): return lax.ppermute(array, AXES, pairs)  21.8 us
    all_to_all x3, waiting for transfers between devices, exchange(): lax.all_to_all(array, axis, split_axis=0, concat_axis=0, tiled=True, axis...  12.2 us
    dot_general x4, matrix products, body(): lax.dot_general(longer(own_tokens[k]), mine, ROWS_BY_ROWS, preferred_elem...  5.23 us
    pallas_call x2, Pallas kernels, weight_part(): pl.pallas_call(weight_kernel, out_shape=out_shape, grid_spec=pltpu.Prefet...  5.22 us
    dot_general x4, matrix products, body(): lax.dot_general(longer(other_tokens[k]), theirs, ROWS_BY_ROWS, preferred_...  3.16 us
    another operation x2, other arithmetic  2.68 us
  transfers between devices with their start and end apart: 26, of which 7 were waited for; matrix products, arithmetic and copies ran while one was open for 13% of the time, Pallas kernels for 4%

profile of v6, /device:TPU:1, one launch (start us, length us, event | category | flops | bytes accessed | tf_op | source)
XLA Modules:
  0.0 128.4 jit_solution(9987436933830064417)
XLA Ops:
  0.6 2.6 %collective-permute-start = (bf16[128,384]{1,0:T(8,128)(2,1)}, bf16[128,384]{1,0:T(8,128)(2,1)S(1)}, u32[]{:S(2)}, u32[]{:S(2)}) collective-permute-start(bf16[128,384]{1,0:T(8,128)(2,1)} %param.9), channel_id=1, source_target_pairs={{0,32},{1,33},{2,34},{3,35},{4,36},{5,37},{6,38},{7,39},{8,40},{9,... | collective-permute-start | bytes 294920 | tf_op jit(solution)/shard_map/ppermute | solution.py:40
  3.2 2.3 %constant_dynamic-slice_fusion = (bf16[2,1,384,384]{3,2,1,0:T(8,128)(2,1)}, bf16[2,1,384,384]{3,2,1,0:T(8,128)(2,1)S(1)}) fusion(bf16[2,2,384,384]{3,2,1,0:T(8,128)(2,1)} %bitcast.74, s32[]{:T(128)S(6)} %select_n.214, s32[]{:T(128)S(6)} %select_n.213), kind=kLoop, calls=%fused_computation.101 | loop fusion | bytes 2359304 | tf_op jit(solution)/shard_map/jit(dynamic_index_in_dim)/dynamic_slice | solution.py:138
  7.5 2.6 %collective-permute-start.3 = (bf16[256,384]{1,0:T(8,128)(2,1)S(1)}, bf16[256,384]{1,0:T(8,128)(2,1)S(1)}, u32[]{:S(2)}, u32[]{:S(2)}) collective-permute-start(bf16[256,384]{1,0:T(8,128)(2,1)S(1)} %maximum_select_fusion.1), channel_id=1, source_target_pairs={{0,192},{1,193},{2,194},{3,195},{4,196},{5,197},{6,198},{7,199},{8... | collective-permute-start | bytes 589832 | tf_op jit(solution)/shard_map/ppermute | solution.py:40
  11.9 11.7 %all-to-all-start = ((f32[32,1,1024]{2,1,0:T(1,128)}), f32[32,1,1024]{2,1,0:T(1,128)S(1)}, u32[]{:S(2)}, u32[]{:S(2)}) async-start(f32[32,1,1024]{2,1,0:T(1,128)} %broadcast_in_dim.25), calls=%async_computation | async-start | bytes 262144 | tf_op jit(solution)/shard_map/all_to_all | solution.py:48
  29.9 1.3 %fusion.19 = f32[272,768]{1,0:T(8,128)} fusion(bf16[768,384]{1,0:T(8,128)(2,1)S(1)} %bitcast.71, bf16[256,384]{1,0:T(8,128)(2,1)S(1)} %get-tuple-element.59), kind=kOutput, calls=%fused_computation.29 | convolution fusion | flops 160432128 | bytes 1622016 | tf_op jit(solution)/shard_map/dot_general | solution.py:154
  31.2 1.3 %fusion.22 = f32[272,768]{1,0:T(8,128)} fusion(bf16[768,384]{1,0:T(8,128)(2,1)S(1)} %bitcast.72, bf16[256,384]{1,0:T(8,128)(2,1)S(1)} %get-tuple-element.60), kind=kOutput, calls=%fused_computation.32 | convolution fusion | flops 160432128 | bytes 1622016 | tf_op jit(solution)/shard_map/dot_general | solution.py:154
  36.0 1.7 %collective-permute-start.9 = (f16[272,768]{1,0:T(8,128)(2,1)}, f16[272,768]{1,0:T(8,128)(2,1)}, u32[]{:S(2)}, u32[]{:S(2)}) collective-permute-start(f16[272,768]{1,0:T(8,128)(2,1)} %fusion.9), channel_id=1, source_target_pairs={{0,16},{1,17},{2,18},{3,19},{4,20},{5,21},{6,22},{7,23},{8,24},{9,... | collective-permute-start | bytes 1253384 | tf_op jit(solution)/shard_map/ppermute | solution.py:40
  39.7 2.4 %collective-permute-start.8 = (f16[272,768]{1,0:T(8,128)(2,1)}, f16[272,768]{1,0:T(8,128)(2,1)}, u32[]{:S(2)}, u32[]{:S(2)}) collective-permute-start(f16[272,768]{1,0:T(8,128)(2,1)} %fusion.10), channel_id=1, source_target_pairs={{0,24},{1,25},{2,26},{3,27},{4,28},{5,29},{6,30},{7,31},{8,0},{9,1... | collective-permute-start | bytes 1253384 | tf_op jit(solution)/shard_map/ppermute | solution.py:40
  43.5 5.5 %collective-permute-done.9 = f16[272,768]{1,0:T(8,128)(2,1)} collective-permute-done((f16[272,768]{1,0:T(8,128)(2,1)}, f16[272,768]{1,0:T(8,128)(2,1)}, u32[]{:S(2)}, u32[]{:S(2)}) %collective-permute-start.9) | collective-permute-done | bytes 417824 | tf_op jit(solution)/shard_map/ppermute | solution.py:40
  49.0 10.8 %collective-permute-done.7 = f16[272,768]{1,0:T(8,128)(2,1)} collective-permute-done((f16[272,768]{1,0:T(8,128)(2,1)S(1)}, f16[272,768]{1,0:T(8,128)(2,1)}, u32[]{:S(2)}, u32[]{:S(2)}) %collective-permute-start.7) | collective-permute-done | bytes 417824 | tf_op jit(solution)/shard_map/ppermute | solution.py:40
  61.4 1.5 %add_convert_fusion.3 = (f16[128,384]{1,0:T(8,128)(2,1)S(1)}, f16[128,384]{1,0:T(8,128)(2,1)S(1)}, f16[128,384]{1,0:T(8,128)(2,1)S(1)}) fusion(f16[272,768]{1,0:T(8,128)(2,1)S(1)} %fusion.8, s32[]{:T(128)S(6)} %select_n.234, s32[]{:T(128)S(6)} %select_n.236, f16[272,768]{1,0:T(8,128)(2,1)} %collective-permute-done.9, ...), kind=kLoop, calls=%fused_computation.55 | loop fusion | flops 1769472 | bytes 1480728 | tf_op jit(solution)/shard_map/convert.6
  63.0 2.3 %collective-permute-start.11 = (f16[144,384]{1,0:T(8,128)(2,1)S(1)}, f16[144,384]{1,0:T(8,128)(2,1)S(1)}, u32[]{:S(2)}, u32[]{:S(2)}) collective-permute-start(f16[144,384]{1,0:T(8,128)(2,1)S(1)} %get-tuple-element.65), channel_id=1, source_target_pairs={{0,2},{1,3},{2,4},{3,5},{4,6},{5,7},{6,0},{7,1},{8,10},{9,11},{10,... | collective-permute-start | bytes 331784 | tf_op jit(solution)/shard_map/ppermute | solution.py:40
  65.3 3.9 %collective-permute-start.12 = (f16[144,384]{1,0:T(8,128)(2,1)S(1)}, f16[144,384]{1,0:T(8,128)(2,1)S(1)}, u32[]{:S(2)}, u32[]{:S(2)}) collective-permute-start(f16[144,384]{1,0:T(8,128)(2,1)S(1)} %get-tuple-element.66), channel_id=1, source_target_pairs={{0,4},{1,5},{2,6},{3,7},{4,0},{5,1},{6,2},{7,3},{8,12},{9,13},{10,... | collective-permute-start | bytes 331784 | tf_op jit(solution)/shard_map/ppermute | solution.py:40
  69.2 2.7 %collective-permute-start.13 = (f16[144,384]{1,0:T(8,128)(2,1)S(1)}, f16[144,384]{1,0:T(8,128)(2,1)S(1)}, u32[]{:S(2)}, u32[]{:S(2)}) collective-permute-start(f16[144,384]{1,0:T(8,128)(2,1)S(1)} %get-tuple-element.67), channel_id=1, source_target_pairs={{0,6},{1,7},{2,0},{3,1},{4,2},{5,3},{6,4},{7,5},{8,14},{9,15},{10,... | collective-permute-start | bytes 331784 | tf_op jit(solution)/shard_map/ppermute | solution.py:40
  72.7 3.5 %all-to-all-start.2 = ((bf16[4,128,384]{2,1,0:T(8,128)(2,1)}), bf16[4,128,384]{2,1,0:T(8,128)(2,1)S(1)}, u32[]{:S(2)}, u32[]{:S(2)}) async-start(bf16[4,128,384]{2,1,0:T(8,128)(2,1)} %broadcast_in_dim.51), calls=%async_computation.2 | async-start | bytes 786432 | tf_op jit(solution)/shard_map/all_to_all | solution.py:48
  76.2 3.9 %collective-permute-done.13 = f16[144,384]{1,0:T(8,128)(2,1)S(1)} collective-permute-done((f16[144,384]{1,0:T(8,128)(2,1)S(1)}, f16[144,384]{1,0:T(8,128)(2,1)S(1)}, u32[]{:S(2)}, u32[]{:S(2)}) %collective-permute-start.13) | collective-permute-done | bytes 110624 | tf_op jit(solution)/shard_map/ppermute | solution.py:40
  82.2 4.2 %all-to-all-done.2 = bf16[4,128,384]{2,1,0:T(8,128)(2,1)S(1)} async-done(((bf16[4,128,384]{2,1,0:T(8,128)(2,1)}), bf16[4,128,384]{2,1,0:T(8,128)(2,1)S(1)}, u32[]{:S(2)}, u32[]{:S(2)}) %all-to-all-start.2) | async-done | bytes 393248 | tf_op jit(solution)/shard_map/all_to_all | solution.py:48
  86.4 4.0 %collective-permute-start.20 = (bf16[2,256,384]{2,1,0:T(8,128)(2,1)S(1)}, bf16[2,256,384]{2,1,0:T(8,128)(2,1)S(1)}, u32[]{:S(2)}, u32[]{:S(2)}) collective-permute-start(bf16[2,256,384]{2,1,0:T(8,128)(2,1)S(1)} %bitcast.64), channel_id=1, source_target_pairs={{0,24},{1,25},{2,26},{3,27},{4,28},{5,29},{6,30},{7,31},{8,0},{9,1... | collective-permute-start | bytes 1179656 | tf_op jit(solution)/shard_map/ppermute | solution.py:40
  91.8 15.8 %all-to-all-start.1 = ((f32[32,1,256]{2,1,0:T(1,128)}), f32[32,1,256]{2,1,0:T(1,128)S(1)}, u32[]{:S(2)}, u32[]{:S(2)}) async-start(f32[32,1,256]{2,1,0:T(1,128)} %broadcast_in_dim.50), calls=%async_computation.1 | async-start | bytes 65536 | tf_op jit(solution)/shard_map/all_to_all | solution.py:48
  107.6 1.9 %collective-permute-start.17 = (f32[2,384]{1,0:T(2,128)S(1)}, f32[2,384]{1,0:T(2,128)S(1)}, u32[]{:S(2)}, u32[]{:S(2)}) collective-permute-start(f32[2,384]{1,0:T(2,128)S(1)} %pad_maximum_fusion.7), channel_id=1, source_target_pairs={{0,192},{1,193},{2,194},{3,195},{4,196},{5,197},{6,198},{7,199},{8... | collective-permute-start | bytes 9224 | tf_op jit(solution)/shard_map/ppermute | solution.py:40
  110.4 6.9 %all-to-all-done.1 = f32[32,1,256]{2,1,0:T(1,128)S(1)} async-done(((f32[32,1,256]{2,1,0:T(1,128)}), f32[32,1,256]{2,1,0:T(1,128)S(1)}, u32[]{:S(2)}, u32[]{:S(2)}) %all-to-all-start.1) | async-done | bytes 32800 | tf_op jit(solution)/shard_map/all_to_all | solution.py:48
  118.2 2.6 %shard_map.84 = f32[2,384,384]{2,1,0:T(8,128)} custom-call(s32[5]{0:T(128)S(1)} %stack.92.at_ref, bf16[2,256,384]{2,1,0:T(8,128)(2,1)S(1)} %bitcast.67, bf16[2,256,384]{2,1,0:T(8,128)(2,1)S(1)} %collective-permute-done.18.second_ref, bf16[2,256,384]{2,1,0:T(8,128)(2,1)S(1)} %collective-permute-done.19.third_ref, ...), custom_call_target="tpu_custom_call" | custom-call | flops 603979776 | bytes 1572864 | tf_op jit(solution)/shard_map/pallas_call | solution.py:82
  120.8 2.6 %shard_map.85.whole_ref = f32[2,2,384,384]{3,2,1,0:T(8,128)} custom-call(s32[5]{0:T(128)S(1)} %stack.92.at_ref, bf16[2,256,384]{2,1,0:T(8,128)(2,1)S(1)} %bitcast.68, bf16[2,256,384]{2,1,0:T(8,128)(2,1)S(1)} %collective-permute-done.18.second_ref, bf16[2,256,384]{2,1,0:T(8,128)(2,1)S(1)} %collective-permute-done.19.third_ref, ...), custom_call_target="tpu_custom_call" | custom-call | flops 603979776 | bytes 1572864 | tf_op jit(solution)/shard_map/pallas_call | solution.py:82
  125.2 1.5 %collective-permute-done.22 = f32[2,384]{1,0:T(2,128)S(1)} collective-permute-done((f32[2,384]{1,0:T(2,128)S(1)}, f32[2,384]{1,0:T(2,128)S(1)}, u32[]{:S(2)}, u32[]{:S(2)}) %collective-permute-start.22) | collective-permute-done | bytes 3104 | tf_op jit(solution)/shard_map/ppermute | solution.py:40
  (115 shorter events, 25.5 us)
Async XLA Ops:
  0.6 6.8 %collective-permute-start = (bf16[128,384]{1,0:T(8,128)(2,1)}, bf16[128,384]{1,0:T(8,128)(2,1)S(1)}, u32[]{:S(2)}, u32[]{:S(2)}) collective-permute-start(bf16[128,384]{1,0:T(8,128)(2,1)} %param.9), channel_id=1, source_target_pairs={{0,32},{1,33},{2,34},{3,35},{4,36},{5,37},{6,38},{7,39},{8,40},{9,... | collective-permute-start | bytes 294920 | tf_op jit(solution)/shard_map/ppermute | solution.py:40
  5.5 29.3 %collective-permute-start.6 = (bf16[768,384]{1,0:T(8,128)(2,1)}, bf16[768,384]{1,0:T(8,128)(2,1)S(1)}, u32[]{:S(2)}, u32[]{:S(2)}) collective-permute-start(bf16[768,384]{1,0:T(8,128)(2,1)} %bitcast.11), channel_id=1, source_target_pairs={{0,1},{1,0},{2,3},{3,2},{4,5},{5,4},{6,7},{7,6},{8,9},{9,8},{10,11... | collective-permute-start | bytes 1769480 | tf_op jit(solution)/shard_map/ppermute | solution.py:40
  7.5 16.2 %collective-permute-start.3 = (bf16[256,384]{1,0:T(8,128)(2,1)S(1)}, bf16[256,384]{1,0:T(8,128)(2,1)S(1)}, u32[]{:S(2)}, u32[]{:S(2)}) collective-permute-start(bf16[256,384]{1,0:T(8,128)(2,1)S(1)} %maximum_select_fusion.1), channel_id=1, source_target_pairs={{0,192},{1,193},{2,194},{3,195},{4,196},{5,197},{6,198},{7,199},{8... | collective-permute-start | bytes 589832 | tf_op jit(solution)/shard_map/ppermute | solution.py:40
  10.1 13.6 %collective-permute-start.2 = (bf16[256,384]{1,0:T(8,128)(2,1)S(1)}, bf16[256,384]{1,0:T(8,128)(2,1)S(1)}, u32[]{:S(2)}, u32[]{:S(2)}) collective-permute-start(bf16[256,384]{1,0:T(8,128)(2,1)S(1)} %maximum_select_fusion.1), channel_id=1, source_target_pairs={{0,128},{1,129},{2,130},{3,131},{4,132},{5,133},{6,134},{7,135},{8... | collective-permute-start | bytes 589832 | tf_op jit(solution)/shard_map/ppermute | solution.py:40
  10.6 13.1 %collective-permute-start.1 = (bf16[256,384]{1,0:T(8,128)(2,1)S(1)}, bf16[256,384]{1,0:T(8,128)(2,1)S(1)}, u32[]{:S(2)}, u32[]{:S(2)}) collective-permute-start(bf16[256,384]{1,0:T(8,128)(2,1)S(1)} %maximum_select_fusion.1), channel_id=1, source_target_pairs={{0,64},{1,65},{2,66},{3,67},{4,68},{5,69},{6,70},{7,71},{8,72},{9,... | collective-permute-start | bytes 589832 | tf_op jit(solution)/shard_map/ppermute | solution.py:40
  11.9 22.7 %all-to-all-start = ((f32[32,1,1024]{2,1,0:T(1,128)}), f32[32,1,1024]{2,1,0:T(1,128)S(1)}, u32[]{:S(2)}, u32[]{:S(2)}) async-start(f32[32,1,1024]{2,1,0:T(1,128)} %broadcast_in_dim.25), calls=%async_computation | async-start | bytes 262144 | tf_op jit(solution)/shard_map/all_to_all | solution.py:48
  25.8 6.7 %collective-permute-start.4 = (f32[1,1]{1,0:T(1,128)}, f32[1,1]{1,0:T(1,128)}, u32[]{:S(2)}, u32[]{:S(2)}) collective-permute-start(f32[1,1]{1,0:T(1,128)} %bitcast.5), channel_id=1, source_target_pairs={{0,1},{1,0},{2,3},{3,2},{4,5},{5,4},{6,7},{7,6},{8,9},{9,8},{10,11... | collective-permute-start | bytes 20 | tf_op jit(solution)/shard_map/ppermute | solution.py:40
  26.9 7.8 %collective-permute-start.5 = (bf16[4,256,384]{2,1,0:T(8,128)(2,1)S(1)}, bf16[4,256,384]{2,1,0:T(8,128)(2,1)S(1)}, u32[]{:S(2)}, u32[]{:S(2)}) collective-permute-start(bf16[4,256,384]{2,1,0:T(8,128)(2,1)S(1)} %get-tuple-element.47.columns_ref), channel_id=1, source_target_pairs={{0,1},{1,0},{2,3},{3,2},{4,5},{5,4},{6,7},{7,6},{8,9},{9,8},{10,11... | collective-permute-start | bytes 2359304 | tf_op jit(solution)/shard_map/ppermute | solution.py:40
  36.0 13.0 %collective-permute-start.9 = (f16[272,768]{1,0:T(8,128)(2,1)}, f16[272,768]{1,0:T(8,128)(2,1)}, u32[]{:S(2)}, u32[]{:S(2)}) collective-permute-start(f16[272,768]{1,0:T(8,128)(2,1)} %fusion.9), channel_id=1, source_target_pairs={{0,16},{1,17},{2,18},{3,19},{4,20},{5,21},{6,22},{7,23},{8,24},{9,... | collective-permute-start | bytes 1253384 | tf_op jit(solution)/shard_map/ppermute | solution.py:40
  38.2 21.6 %collective-permute-start.7 = (f16[272,768]{1,0:T(8,128)(2,1)S(1)}, f16[272,768]{1,0:T(8,128)(2,1)}, u32[]{:S(2)}, u32[]{:S(2)}) collective-permute-start(f16[272,768]{1,0:T(8,128)(2,1)S(1)} %fusion.11), channel_id=1, source_target_pairs={{0,8},{1,9},{2,10},{3,11},{4,12},{5,13},{6,14},{7,15},{8,16},{9,17... | collective-permute-start | bytes 1253384 | tf_op jit(solution)/shard_map/ppermute | solution.py:40
  39.7 20.1 %collective-permute-start.8 = (f16[272,768]{1,0:T(8,128)(2,1)}, f16[272,768]{1,0:T(8,128)(2,1)}, u32[]{:S(2)}, u32[]{:S(2)}) collective-permute-start(f16[272,768]{1,0:T(8,128)(2,1)} %fusion.10), channel_id=1, source_target_pairs={{0,24},{1,25},{2,26},{3,27},{4,28},{5,29},{6,30},{7,31},{8,0},{9,1... | collective-permute-start | bytes 1253384 | tf_op jit(solution)/shard_map/ppermute | solution.py:40
  63.0 13.2 %collective-permute-start.11 = (f16[144,384]{1,0:T(8,128)(2,1)S(1)}, f16[144,384]{1,0:T(8,128)(2,1)S(1)}, u32[]{:S(2)}, u32[]{:S(2)}) collective-permute-start(f16[144,384]{1,0:T(8,128)(2,1)S(1)} %get-tuple-element.65), channel_id=1, source_target_pairs={{0,2},{1,3},{2,4},{3,5},{4,6},{5,7},{6,0},{7,1},{8,10},{9,11},{10,... | collective-permute-start | bytes 331784 | tf_op jit(solution)/shard_map/ppermute | solution.py:40
  65.3 10.9 %collective-permute-start.12 = (f16[144,384]{1,0:T(8,128)(2,1)S(1)}, f16[144,384]{1,0:T(8,128)(2,1)S(1)}, u32[]{:S(2)}, u32[]{:S(2)}) collective-permute-start(f16[144,384]{1,0:T(8,128)(2,1)S(1)} %get-tuple-element.66), channel_id=1, source_target_pairs={{0,4},{1,5},{2,6},{3,7},{4,0},{5,1},{6,2},{7,3},{8,12},{9,13},{10,... | collective-permute-start | bytes 331784 | tf_op jit(solution)/shard_map/ppermute | solution.py:40
  69.2 10.8 %collective-permute-start.13 = (f16[144,384]{1,0:T(8,128)(2,1)S(1)}, f16[144,384]{1,0:T(8,128)(2,1)S(1)}, u32[]{:S(2)}, u32[]{:S(2)}) collective-permute-start(f16[144,384]{1,0:T(8,128)(2,1)S(1)} %get-tuple-element.67), channel_id=1, source_target_pairs={{0,6},{1,7},{2,0},{3,1},{4,2},{5,3},{6,4},{7,5},{8,14},{9,15},{10,... | collective-permute-start | bytes 331784 | tf_op jit(solution)/shard_map/ppermute | solution.py:40
  72.7 13.7 %all-to-all-start.2 = ((bf16[4,128,384]{2,1,0:T(8,128)(2,1)}), bf16[4,128,384]{2,1,0:T(8,128)(2,1)S(1)}, u32[]{:S(2)}, u32[]{:S(2)}) async-start(bf16[4,128,384]{2,1,0:T(8,128)(2,1)} %broadcast_in_dim.51), calls=%async_computation.2 | async-start | bytes 786432 | tf_op jit(solution)/shard_map/all_to_all | solution.py:48
  81.4 9.5 %collective-permute-start.14 = (f16[144,384]{1,0:T(8,128)(2,1)S(1)}, f16[144,384]{1,0:T(8,128)(2,1)S(1)}, u32[]{:S(2)}, u32[]{:S(2)}) collective-permute-start(f16[144,384]{1,0:T(8,128)(2,1)S(1)} %pad_maximum_fusion.4), channel_id=1, source_target_pairs={{0,0},{1,1},{4,2},{5,3},{32,4},{33,5},{36,6},{37,7},{64,8},{65,9},... | collective-permute-start | bytes 331784 | tf_op jit(solution)/shard_map/ppermute | solution.py:40
  86.4 30.9 %collective-permute-start.20 = (bf16[2,256,384]{2,1,0:T(8,128)(2,1)S(1)}, bf16[2,256,384]{2,1,0:T(8,128)(2,1)S(1)}, u32[]{:S(2)}, u32[]{:S(2)}) collective-permute-start(bf16[2,256,384]{2,1,0:T(8,128)(2,1)S(1)} %bitcast.64), channel_id=1, source_target_pairs={{0,24},{1,25},{2,26},{3,27},{4,28},{5,29},{6,30},{7,31},{8,0},{9,1... | collective-permute-start | bytes 1179656 | tf_op jit(solution)/shard_map/ppermute | solution.py:40
  90.3 27.8 %collective-permute-start.19 = (bf16[2,256,384]{2,1,0:T(8,128)(2,1)S(1)}, bf16[2,256,384]{2,1,0:T(8,128)(2,1)S(1)}, u32[]{:S(2)}, u32[]{:S(2)}) collective-permute-start(bf16[2,256,384]{2,1,0:T(8,128)(2,1)S(1)} %bitcast.65), channel_id=1, source_target_pairs={{0,16},{1,17},{2,18},{3,19},{4,20},{5,21},{6,22},{7,23},{8,24},{9,... | collective-permute-start | bytes 1179656 | tf_op jit(solution)/shard_map/ppermute | solution.py:40
  90.4 27.7 %collective-permute-start.18 = (bf16[2,256,384]{2,1,0:T(8,128)(2,1)S(1)}, bf16[2,256,384]{2,1,0:T(8,128)(2,1)S(1)}, u32[]{:S(2)}, u32[]{:S(2)}) collective-permute-start(bf16[2,256,384]{2,1,0:T(8,128)(2,1)S(1)} %bitcast.66), channel_id=1, source_target_pairs={{0,8},{1,9},{2,10},{3,11},{4,12},{5,13},{6,14},{7,15},{8,16},{9,17... | collective-permute-start | bytes 1179656 | tf_op jit(solution)/shard_map/ppermute | solution.py:40
  91.8 25.4 %all-to-all-start.1 = ((f32[32,1,256]{2,1,0:T(1,128)}), f32[32,1,256]{2,1,0:T(1,128)S(1)}, u32[]{:S(2)}, u32[]{:S(2)}) async-start(f32[32,1,256]{2,1,0:T(1,128)} %broadcast_in_dim.50), calls=%async_computation.1 | async-start | bytes 65536 | tf_op jit(solution)/shard_map/all_to_all | solution.py:48
  107.6 15.8 %collective-permute-start.17 = (f32[2,384]{1,0:T(2,128)S(1)}, f32[2,384]{1,0:T(2,128)S(1)}, u32[]{:S(2)}, u32[]{:S(2)}) collective-permute-start(f32[2,384]{1,0:T(2,128)S(1)} %pad_maximum_fusion.7), channel_id=1, source_target_pairs={{0,192},{1,193},{2,194},{3,195},{4,196},{5,197},{6,198},{7,199},{8... | collective-permute-start | bytes 9224 | tf_op jit(solution)/shard_map/ppermute | solution.py:40
  109.5 13.9 %collective-permute-start.16 = (f32[2,384]{1,0:T(2,128)S(1)}, f32[2,384]{1,0:T(2,128)S(1)}, u32[]{:S(2)}, u32[]{:S(2)}) collective-permute-start(f32[2,384]{1,0:T(2,128)S(1)} %pad_maximum_fusion.7), channel_id=1, source_target_pairs={{0,128},{1,129},{2,130},{3,131},{4,132},{5,133},{6,134},{7,135},{8... | collective-permute-start | bytes 9224 | tf_op jit(solution)/shard_map/ppermute | solution.py:40
  117.3 6.1 %collective-permute-start.15 = (f32[2,384]{1,0:T(2,128)S(1)}, f32[2,384]{1,0:T(2,128)S(1)}, u32[]{:S(2)}, u32[]{:S(2)}) collective-permute-start(f32[2,384]{1,0:T(2,128)S(1)} %pad_maximum_fusion.7), channel_id=1, source_target_pairs={{0,64},{1,65},{2,66},{3,67},{4,68},{5,69},{6,70},{7,71},{8,72},{9,... | collective-permute-start | bytes 9224 | tf_op jit(solution)/shard_map/ppermute | solution.py:40
  123.4 3.9 %collective-permute-start.21 = (f32[2,384,384]{2,1,0:T(8,128)}, f32[2,384,384]{2,1,0:T(8,128)S(1)}, u32[]{:S(2)}, u32[]{:S(2)}) collective-permute-start(f32[2,384,384]{2,1,0:T(8,128)} %shard_map.84), channel_id=1, source_target_pairs={{0,1},{1,0},{2,3},{3,2},{4,5},{5,4},{6,7},{7,6},{8,9},{9,8},{10,11... | collective-permute-start | bytes 3538952 | tf_op jit(solution)/shard_map/ppermute | solution.py:40
  (11 other events, 30.1 us)
